TPU v7x, 32 devices: a whole 2x2x4 slice. The times are simulated.
32 devices in a mesh: ent: 16 (over z, y, x), rep: 2 (over core).
Axes of the slice: x: 2, y: 2, z: 4, core: 2. Of those that a mesh axis runs over, the one named last changes fastest.
Arguments:
- pieces: bfloat16 [4096, 8, 512], P(('ent', 'rep')), may hold values from -6 to 6
- lengths: int32 [4096], P(('ent', 'rep')), may hold values from 1 to 7
- scripts: int32 [4096], P(('ent', 'rep')), may hold values from 0 to 15
- script_table: float32 [16, 512], replicated, may hold values from -3 to 3
- gain_attn: float32 [512], replicated, may hold values from 0.5 to 1.5
- gain_ffn: float32 [512], replicated, may hold values from 0.5 to 1.5
- w_qkv: bfloat16 [512, 1536], replicated, may hold values from -0.25 to 0.25
- w_out: bfloat16 [512, 512], replicated, may hold values from -0.5 to 0.5
- w_up: bfloat16 [512, 2048], replicated, may hold values from -0.25 to 0.25
- w_down: bfloat16 [2048, 512], replicated, may hold values from -0.125 to 0.125
- w_proj: bfloat16 [512, 4096], P(None, 'ent'), may hold values from -0.25 to 0.25
- token_ids: int32 [8, 2048], P('rep'), may hold values from 0 to 4095
- out_grad: bfloat16 [4096, 8, 2048], P('ent', 'rep'), may hold values from -6 to 6
Outputs:
- looked_up: bfloat16 [4096, 8, 2048], P('ent', 'rep')
- grad_pieces: float32 [4096, 8, 512], P(('ent', 'rep'))
- grad_script_table: float32 [16, 512], replicated
- grad_gain_attn: float32 [512], replicated
- grad_gain_ffn: float32 [512], replicated
- grad_w_qkv: float32 [512, 1536], replicated
- grad_w_out: float32 [512, 512], replicated
- grad_w_up: float32 [512, 2048], replicated
- grad_w_down: float32 [2048, 512], replicated
- grad_w_proj: float32 [512, 4096], P(None, 'ent')
All inputs are finite; a program needn't handle non-finite values.
Results may differ from a plain program's by a relative error of at most 0.0074.
Values may be sent and summed in bfloat16 or wider, within the bound.
No kernel may reach another device: no remote copies, remote signals or barrier semaphores. Data moves between devices by JAX's collectives and lax.ppermute only.
A program may use at most 128 MiB of HBM per device.

v0:
```python
import math

import jax
import jax.numpy as jnp
from jax import lax
from jax.sharding import PartitionSpec as P

HEADS = 8
HEAD_DIM = 64


highest = lax.Precision.HIGHEST


def normalize(values, gain):
    centered = values - jnp.mean(values, axis=-1, keepdims=True)
    spread = jnp.mean(centered * centered, axis=-1, keepdims=True)
    return centered * lax.rsqrt(spread + 1e-05) * gain


def contract(left, right, left_dim, right_dim):
    return lax.dot_general(
        left, right, (((left_dim,), (right_dim,)), ((), ())), preferred_element_type=jnp.float32
    )


def forward(
    pieces, lengths, scripts, script_table, gain_attn, gain_ffn, w_qkv, w_out, w_up, w_down
):
    entries, slots, width = pieces.shape
    onehot = (scripts[:, None] == jnp.arange(script_table.shape[0])[None, :]).astype(jnp.float32)
    start = (
        pieces.astype(jnp.float32) + jnp.dot(onehot, script_table, precision=highest)[:, None, :]
    )
    normed = normalize(start, gain_attn).astype(jnp.bfloat16).reshape(entries * slots, width)
    mixed = jnp.dot(normed, w_qkv, preferred_element_type=jnp.float32).astype(jnp.bfloat16)
    mixed = mixed.reshape(entries, slots, 3, HEADS, HEAD_DIM)
    queries = mixed[:, :, 0]
    key_heads = mixed[:, :, 1]
    value_heads = mixed[:, :, 2]
    raw = jnp.einsum("eshd,ethd->ehst", queries, key_heads, preferred_element_type=jnp.float32)
    valid = jnp.arange(slots)[None, :] <= lengths[:, None]
    scores = jnp.where(valid[:, None, None, :], raw * HEAD_DIM ** (-0.5), -1000000000.0)
    attn_probs = jax.nn.softmax(scores, axis=-1)
    probs_low = attn_probs.astype(jnp.bfloat16)
    context = jnp.einsum(
        "ehst,ethd->eshd", probs_low, value_heads, preferred_element_type=jnp.float32
    )
    context = context.astype(jnp.bfloat16).reshape(entries * slots, width)
    middle = start + jnp.dot(context, w_out, preferred_element_type=jnp.float32).reshape(
        entries, slots, width
    )
    normed_ffn = normalize(middle, gain_ffn).astype(jnp.bfloat16).reshape(entries * slots, width)
    up_proj = jnp.dot(normed_ffn, w_up, preferred_element_type=jnp.float32)
    hidden = jax.nn.gelu(up_proj, approximate=True).astype(jnp.bfloat16)
    final = middle + jnp.dot(hidden, w_down, preferred_element_type=jnp.float32).reshape(
        entries, slots, width
    )
    pool_weights = valid.astype(jnp.float32) / (lengths + 1).astype(jnp.float32)[:, None]
    pooled = jnp.sum(final * pool_weights[:, :, None], axis=1).astype(jnp.bfloat16)
    return (
        onehot,
        start,
        normed,
        queries,
        key_heads,
        value_heads,
        attn_probs,
        probs_low,
        context,
        middle,
        normed_ffn,
        up_proj,
        hidden,
        pool_weights,
        pooled,
    )


def per_device(
    pieces,
    lengths,
    scripts,
    script_table,
    gain_attn,
    gain_ffn,
    w_qkv,
    w_out,
    w_up,
    w_down,
    w_proj,
    token_ids,
    out_grad,
):
    local_args = (
        pieces,
        lengths,
        scripts,
        script_table,
        gain_attn,
        gain_ffn,
        w_qkv,
        w_out,
        w_up,
        w_down,
    )
    kept = forward(*local_args)
    pooled = kept[14]
    entries, slots, width = pieces.shape
    ent_count = lax.axis_size("ent")
    rep_count = lax.axis_size("rep")
    features = w_proj.shape[1]
    table_cols = contract(lax.all_gather(w_proj, "ent", axis=1, tiled=True), pooled, 0, 1).astype(
        jnp.bfloat16
    )
    table_half = lax.all_to_all(table_cols, "ent", split_axis=0, concat_axis=1, tiled=True)
    table_all = lax.all_gather(table_half, "rep", axis=1, tiled=True)
    group = rep_count * entries
    owner = token_ids // group
    within = token_ids % group
    layout_ids = (
        within // entries * (ent_count * entries) + owner * entries + within % entries
    ).reshape(-1)
    rows_dev, text_len = token_ids.shape
    total_tokens = rows_dev * text_len
    token_block = math.gcd(total_tokens, 1024)
    vocab_cols = table_all.shape[1]
    vocab_index = jnp.arange(vocab_cols, dtype=jnp.int32)
    flat_grad = out_grad.reshape(features, total_tokens)

    def lookup_block(block_index, state_pair):
        gathered, partial_sum = state_pair
        offset = block_index * token_block
        ids_block = lax.dynamic_slice_in_dim(layout_ids, offset, token_block, 0)
        selector = (ids_block[:, None] == vocab_index[None, :]).astype(jnp.bfloat16)
        fetched = contract(table_all, selector, 1, 1).astype(jnp.bfloat16)
        gathered = lax.dynamic_update_slice_in_dim(gathered, fetched, offset, 1)
        grad_block = lax.dynamic_slice_in_dim(flat_grad, offset, token_block, 1)
        partial_sum = partial_sum + contract(grad_block, selector, 1, 0)
        return (gathered, partial_sum)

    gathered, partial_grad = lax.fori_loop(
        0,
        total_tokens // token_block,
        lookup_block,
        (
            jnp.zeros((features, total_tokens), jnp.bfloat16),
            jnp.zeros((features, vocab_cols), jnp.float32),
        ),
    )
    looked_up = gathered.reshape(features, rows_dev, text_len)
    table_grad = lax.psum_scatter(partial_grad, "rep", scatter_dimension=1, tiled=True).astype(
        jnp.bfloat16
    )
    kept = forward(*lax.optimization_barrier(local_args))
    (
        onehot,
        start,
        normed,
        queries,
        key_heads,
        value_heads,
        attn_probs,
        probs_low,
        context,
        middle,
        normed_ffn,
        up_proj,
        hidden,
        pool_weights,
        pooled,
    ) = kept
    grad_rows = lax.all_to_all(table_grad, "ent", split_axis=1, concat_axis=0, tiled=True)
    grad_pooled = contract(grad_rows, lax.all_gather(w_proj, "ent", axis=1, tiled=True), 0, 1)
    proj_term = contract(pooled, grad_rows, 0, 1)
    proj_part = lax.psum_scatter(proj_term, "ent", scatter_dimension=1, tiled=True)
    grad_w_proj = lax.psum(proj_part, "rep")
    grad_final = grad_pooled[:, None, :] * pool_weights[:, :, None]
    grad_ffn = grad_final.astype(jnp.bfloat16).reshape(entries * slots, width)
    part_down = contract(hidden, grad_ffn, 0, 0)
    grad_hidden = contract(grad_ffn, w_down, 1, 1)
    gelu_pull = jax.vjp(lambda values: jax.nn.gelu(values, approximate=True), up_proj)[1]
    grad_up = gelu_pull(grad_hidden)[0].astype(jnp.bfloat16)
    part_up = contract(normed_ffn, grad_up, 0, 0)
    grad_normed_ffn = contract(grad_up, w_up, 1, 1).reshape(entries, slots, width)
    norm_pull = jax.vjp(normalize, middle, gain_ffn)[1]
    grad_mid_norm, part_gain_ffn = norm_pull(grad_normed_ffn)
    grad_middle = grad_final + grad_mid_norm
    grad_branch = grad_middle.astype(jnp.bfloat16).reshape(entries * slots, width)
    part_out = contract(context, grad_branch, 0, 0)
    grad_ctx = (
        contract(grad_branch, w_out, 1, 1)
        .astype(jnp.bfloat16)
        .reshape(entries, slots, HEADS, HEAD_DIM)
    )
    grad_probs = jnp.einsum(
        "eshd,ethd->ehst", grad_ctx, value_heads, preferred_element_type=jnp.float32
    )
    grad_values = jnp.einsum(
        "ehst,eshd->ethd", probs_low, grad_ctx, preferred_element_type=jnp.float32
    )
    grad_scores = attn_probs * (
        grad_probs - jnp.sum(grad_probs * attn_probs, axis=-1, keepdims=True)
    )
    grad_raw = (grad_scores * HEAD_DIM ** (-0.5)).astype(jnp.bfloat16)
    grad_queries = jnp.einsum(
        "ehst,ethd->eshd", grad_raw, key_heads, preferred_element_type=jnp.float32
    )
    grad_keys = jnp.einsum("ehst,eshd->ethd", grad_raw, queries, preferred_element_type=jnp.float32)
    grad_mixed = jnp.stack([grad_queries, grad_keys, grad_values], axis=2).astype(jnp.bfloat16)
    grad_mixed = grad_mixed.reshape(entries * slots, 3 * width)
    part_qkv = contract(normed, grad_mixed, 0, 0)
    grad_normed = contract(grad_mixed, w_qkv, 1, 1).reshape(entries, slots, width)
    attn_pull = jax.vjp(normalize, start, gain_attn)[1]
    grad_start_norm, part_gain_attn = attn_pull(grad_normed)
    grad_pieces = grad_middle + grad_start_norm
    part_script = jnp.dot(onehot.T, jnp.sum(grad_pieces, axis=1), precision=highest)
    summed = lax.psum(
        (part_script, part_gain_attn, part_gain_ffn, part_qkv, part_out, part_up, part_down),
        ("ent", "rep"),
    )
    return (
        looked_up,
        grad_pieces,
        summed[0],
        summed[1],
        summed[2],
        summed[3],
        summed[4],
        summed[5],
        summed[6],
        grad_w_proj,
    )


def solution(mesh):
    in_specs = (
        P(("ent", "rep"), None, None),
        P(("ent", "rep")),
        P(("ent", "rep")),
        P(),
        P(),
        P(),
        P(),
        P(),
        P(),
        P(),
        P(None, "ent"),
        P("rep", None),
        P("ent", "rep", None),
    )
    out_specs = (
        P("ent", "rep", None),
        P(("ent", "rep"), None, None),
        P(),
        P(),
        P(),
        P(),
        P(),
        P(),
        P(),
        P(None, "ent"),
    )
    return jax.shard_map(
        per_device, mesh=mesh, in_specs=in_specs, out_specs=out_specs, check_vma=False
    )
```

profile of v0, /device:TPU:0, one launch (start us, length us, event | category | flops | bytes accessed | tf_op | source)
XLA Modules:
  0.0 834.4 jit_solution(15717791221806295537)
XLA Ops:
  12.1 3.6 convolution_convert_fusion.2
  15.7 8.9 %reshape.303 = bf16[128,8,3,8,64]{4,3,2,1,0:T(8,128)(2,1)} reshape(bf16[1024,1536]{1,0:T(8,128)(2,1)} %convolution_convert_fusion.2) | data formatting | bytes 6291456 | tf_op jit(solution)/shard_map/reshape | solution.py:37
  24.6 5.7 fusion.142
  33.5 4.4 copy.159
  39.1 3.7 copy.160
  42.8 4.8 convert_bitcast_fusion.1
  47.6 4.3 copy.161
  57.0 8.2 fusion.56
  68.7 32.0 %all-gather.3.cloned.1.call-done = bf16[512,4096]{1,0:T(8,128)(2,1)} async-done(((bf16[512,256]{1,0:T(8,128)(2,1)}), bf16[512,4096]{1,0:T(8,128)(2,1)}) %all-gather.3.cloned.1.call-update) | async-done | bytes 4194320 | tf_op jit(solution)/shard_map/all_gather | solution.py:113
  103.7 30.3 %all_to_all.38 = bf16[16,256,128]{1,2,0:T(8,128)(2,1)} all-to-all(bf16[16,256,128]{1,2,0:T(8,128)(2,1)S(1)} %bitcast.160), channel_id=1, replica_groups=mesh['ent'=16,'rep'=2] {'ent'}, dimensions={0} | all-to-all | bytes 2097152 | tf_op jit(solution)/shard_map/all_to_all | solution.py:116
  136.4 8.6 %copy.214 = bf16[32,8,4,2048]{3,1,2,0:T(8,128)(2,1)} copy(bf16[32,8,4,2048]{3,2,1,0:T(4,128)(2,1)} %bitcast.153) | data formatting | bytes 8388608
  147.6 106.7 %while.16 = (s32[]{:T(128)}, bf16[256,8192]{0,1:T(8,128)(2,1)}, f32[256,4096]{1,0:T(8,128)}, s32[8192]{0:T(1024)S(1)}, bf16[256,4096]{1,0:T(8,128)(2,1)}, /*inde...) while((s32[]{:T(128)}, bf16[256,8192]{0,1:T(8,128)(2,1)}, ...), condition=%wide.region_8.9_spmd.clone, body=%wide.region_7.8_spmd.clone.sunk | while | flops 4305715200 | bytes 11550897 | solution.py:142
  147.7 5.3 fusion.186
  153.1 6.8 fusion.187
  159.9 5.3 fusion.186
  165.2 8.1 fusion.187
  173.4 5.3 fusion.186
  178.7 8.1 fusion.187
  186.9 5.3 fusion.186
  192.2 8.1 fusion.187
  200.4 5.3 fusion.186
  205.7 8.1 fusion.187
  213.8 5.3 fusion.186
  219.2 8.1 fusion.187
  227.3 5.3 fusion.186
  232.7 8.1 fusion.187
  240.8 5.3 fusion.186
  246.1 8.1 fusion.187
  254.3 5.6 copy.168
  263.5 3.6 convolution_convert_fusion.1
  267.1 9.3 %reshape.309 = bf16[128,8,3,8,64]{4,3,2,1,0:T(8,128)(2,1)} reshape(bf16[1024,1536]{1,0:T(8,128)(2,1)} %convolution_convert_fusion.1) | data formatting | bytes 6291456 | tf_op jit(solution)/shard_map/reshape | solution.py:37
  276.4 5.7 fusion.141
  287.3 4.4 copy.178
  293.8 4.1 copy.193
  297.8 4.1 convert_bitcast_fusion
  302.0 3.9 copy.180
  313.0 6.6 all-to-all-start.1
  328.7 4.5 convolution_bitcast_fusion
  333.2 11.2 %all-to-all-done.1 = bf16[256,16,128]{0,2,1:T(8,128)(2,1)} async-done(((bf16[256,16,128]{0,2,1:T(8,128)(2,1)}), bf16[256,16,128]{0,2,1:T(8,128)(2,1)}, u32[]{:S(2)}, u32[]{:S(2)}) %all-to-all-start.1) | async-done | bytes 1048608 | tf_op jit(solution)/shard_map/all_to_all | solution.py:173
  346.7 4.0 fusion.147
  350.7 9.2 %fusion.21 = bf16[1024,2048]{1,0:T(8,128)(2,1)S(1)} fusion(f32[1024,2048]{1,0:T(8,128)} %copy-done.59, bf16[2048,512]{1,0:T(8,128)(2,1)S(1)} %copy-done, f32[128,512]{1,0:T(8,128)S(1)} %fusion.147, f32[1024]{0:T(1024)S(1)} %div.136), kind=kOutput, calls=%fused_computation.24 | convolution fusion | flops 2190475264 | bytes 14946304 | tf_op jit(solution)/shard_map/dot_general | solution.py:22
  367.2 4.5 fusion.148
  375.4 4.2 reshape.314
  387.2 4.0 reshape.313
  391.2 4.1 fusion.52
  395.3 4.1 copy.194
  399.4 4.8 fusion.48
  404.3 3.9 copy.187
  411.8 4.1 fusion.49
  416.0 3.9 copy.191
  419.9 3.8 fusion.51
  423.8 4.1 copy.189
  431.1 10.3 %copy.197 = bf16[128,8,3,8,64]{4,3,2,1,0:T(8,128)(2,1)} copy(bf16[128,8,3,8,64]{0,4,3,2,1:T(8,128)(2,1)} %maximum_convert_fusion) | data formatting | bytes 6291456 | tf_op jit(solution)/shard_map/convert_element_type | solution.py:210
  441.4 9.6 %convert_element_type.163 = bf16[1024,1536]{1,0:T(8,128)(2,1)} reshape(bf16[128,8,3,8,64]{4,3,2,1,0:T(8,128)(2,1)} %copy.197) | data formatting | bytes 6291456 | tf_op jit(solution)/shard_map/convert_element_type | solution.py:210
  453.1 5.1 fusion.81
  458.2 4.7 fusion.77
  462.9 5.8 fusion.61
  468.8 8.3 copy.204
  477.1 4.6 multiply_reduce_fusion.2
  484.6 66.1 %reduce-scatter.5.cloned.1.call-done = f32[512,256]{1,0:T(8,128)} async-done(((f32[512,4096]{1,0:T(8,128)}), f32[512,256]{1,0:T(8,128)}) %reduce-scatter.5.cloned.1.call-update) | async-done | bytes 524304 | tf_op jit(solution)/shard_map/reduce_scatter | solution.py:176
  556.1 44.5 %all-reduce = (f32[16,512]{1,0:T(8,128)}, f32[512]{0:T(512)}, f32[512]{0:T(512)}) all-reduce(f32[16,512]{1,0:T(8,128)S(1)} %fusion.113, f32[512]{0:T(512)S(1)} %get-tuple-element.232, f32[512]{0:T(512)S(1)} %copy-done.46), channel_id=1, replica_groups=mesh['ent'=16,'rep'=2] {'ent','rep'}, use_global_device_ids=true, to_apply=%region_22.23 | all-reduce | flops 9216 | bytes 73728 | tf_op jit(solution)/shard_map/psum | solution.py:218
  600.6 193.5 %all-reduce.7.cloned.1.call-done = (f32[512,1536]{1,0:T(8,128)}, f32[512,512]{1,0:T(8,128)}, f32[512,2048]{1,0:T(8,128)}, f32[2048,512]{1,0:T(8,128)}) async-done(((f32[512,1536]{1,0:T(8,128)}, f32[512,512]{1,0:T(8,128)}, f32[512,2048]{1,0:T(8,128)}, f32[2048,512]{1,0:T(8,128)}), (f32[512,1536]{1,0:T(8,128)}, f32[512,512]{1,0:T(8,128)}, f32[512,2048]{1,0:T(8,128)}, ...) | async-done | bytes 12582928 | tf_op jit(solution)/shard_map/psum | solution.py:218
  794.1 20.9 %all-reduce.5.cloned.1.call-done = f32[512,256]{1,0:T(8,128)} async-done(((f32[512,256]{1,0:T(8,128)}), f32[512,256]{1,0:T(8,128)}) %all-reduce.5.cloned.1.call-update) | async-done | bytes 524304 | tf_op jit(solution)/shard_map/psum | solution.py:177
  815.0 3.9 copy.316
  (217 shorter events, 98.8 us)
Async XLA Ops:
  7.2 49.8 %copy-start = (bf16[2048,512]{1,0:T(8,128)(2,1)S(1)}, bf16[2048,512]{1,0:T(8,128)(2,1)}, u32[]{:S(2)}) copy-start(bf16[2048,512]{1,0:T(8,128)(2,1)} %param.24) | copy-start | bytes 6291460
  7.2 3.5 copy-start.2
  7.2 4.1 copy-start.44
  7.2 93.4 %all-gather.3.cloned.1.call-start = ((), (), s32[]{:S(2)}) async-start(), calls=%async_computation.4 | async-start | bytes 4456448 | tf_op jit(solution)/shard_map/all_gather | solution.py:113
  8.0 137.3 %all-gather.5.cloned.1.call-start = ((), (), s32[]{:S(2)}) async-start(), calls=%async_computation.5 | async-start | bytes 3145728 | tf_op jit(solution)/shard_map/all_gather | solution.py:117
  10.7 1.4 copy-start.56
  33.5 4.4 copy-start.49
  54.4 1.3 copy-start.5
  54.4 1.3 copy-start.43
  133.9 2.4 copy-start.40
  136.2 174.1 %reduce-scatter.3.cloned.1.call-start = ((), (), s32[]{:S(2)}) async-start(), calls=%async_computation.6 | async-start | bytes 6291456 | tf_op jit(solution)/shard_map/reduce_scatter | solution.py:152
  261.3 2.1 copy-start.57
  261.9 5.2 copy-start.38
  262.4 1.1 copy-start.33
  282.1 1.3 copy-start.8
  282.1 1.9 copy-start.9
  287.3 4.4 copy-start.50
  308.5 1.3 copy-start.3
  308.5 1.8 copy-start.51
  313.0 31.4 %all-to-all-start.1 = ((bf16[256,16,128]{0,2,1:T(8,128)(2,1)}), bf16[256,16,128]{0,2,1:T(8,128)(2,1)}, u32[]{:S(2)}, u32[]{:S(2)}) async-start(bf16[256,16,128]{0,2,1:T(8,128)(2,1)} %bitcast.152), calls=%async_computation.2 | async-start | bytes 2097152 | tf_op jit(solution)/shard_map/all_to_all | solution.py:173
  319.7 231.0 %reduce-scatter.5.cloned.1.call-start = ((), (), s32[]{:S(2)}) async-start(), calls=%async_computation.7 | async-start | bytes 8912896 | tf_op jit(solution)/shard_map/reduce_scatter | solution.py:176
  319.8 30.9 %copy-start.52 = (f32[1024]{0:T(1024)}, f32[1024]{0:T(1024)S(1)}, u32[]{:S(2)}) copy-start(f32[1024]{0:T(1024)S(1)} %div.136) | copy-start | bytes 12292
  319.9 3.1 copy-start.54
  322.0 1.0 copy-start.17
  325.5 3.2 copy-start.59
  350.7 9.2 %copy-start.24 = (f32[128,512]{1,0:T(8,128)}, f32[128,512]{1,0:T(8,128)S(1)}, u32[]{:S(2)}) copy-start(f32[128,512]{1,0:T(8,128)S(1)} %fusion.147) | copy-start | bytes 786436
  350.7 9.2 %copy-start.55 = (bf16[512,2048]{1,0:T(8,128)(2,1)S(1)}, bf16[512,2048]{1,0:T(8,128)(2,1)}, u32[]{:S(2)}) copy-start(bf16[512,2048]{1,0:T(8,128)(2,1)} %param.23) | copy-start | bytes 6291460
  360.0 2.4 copy-start.12
  360.0 3.1 copy-start.4
  360.0 3.7 copy-start.27
  363.7 3.5 copy-start.16
  363.7 3.5 copy-start.14
  371.7 422.4 %all-reduce.7.cloned.1.call-start = ((), (), s32[]{:S(2)}) async-start(), calls=%async_computation.9 | async-start | bytes 25165824 | tf_op jit(solution)/shard_map/psum | solution.py:218
  379.6 3.5 copy-start.25
  383.1 1.3 copy-start.10
  383.1 2.3 copy-start.28
  387.1 4.0 copy-start.6
  395.3 4.1 copy-start.7
  404.3 3.9 copy-start.36
  404.3 3.9 copy-start.42
  423.8 4.1 copy-start.21
  423.8 4.1 copy-start.22
  441.4 9.6 %copy-start.29 = (bf16[1024,512]{1,0:T(8,128)(2,1)S(1)}, bf16[1024,512]{1,0:T(8,128)(2,1)}, u32[]{:S(2)}) copy-start(bf16[1024,512]{1,0:T(8,128)(2,1)} %reshape.314) | copy-start | bytes 3145732
  441.4 9.6 %copy-start.32 = (bf16[128,8,512]{2,0,1:T(8,128)(2,1)S(1)}, bf16[128,8,512]{2,0,1:T(8,128)(2,1)}, u32[]{:S(2)}) copy-start(bf16[128,8,512]{2,0,1:T(8,128)(2,1)} %copy-done.31) | copy-start | bytes 3145732
  451.0 2.1 copy-start.23
  453.1 5.1 copy-start.13
  453.1 5.1 copy-start.18
  453.1 9.8 %slice-start = ((s8[8388608]{0:T(1024)(128)(4,1)}), s8[4194304]{0:T(1024)(128)(4,1)S(1)}, s32[]{:S(2)}) async-start(s8[8388608]{0:T(1024)(128)(4,1)} %bitcast.164), calls=%async_computation.10 | async-start | bytes 8388608
  458.2 4.7 copy-start.26
  458.2 4.7 copy-start.53
  458.2 4.7 slice-start.1
  468.7 346.3 %all-reduce.5.cloned.1.call-start = ((), (), s32[]{:S(2)}) async-start(), calls=%async_computation.8 | async-start | bytes 1048576 | tf_op jit(solution)/shard_map/psum | solution.py:177
  468.8 8.3 copy-start.45
  468.8 8.3 copy-start.58
  477.1 4.7 copy-start.39
  481.8 1.3 copy-start.15
  481.8 69.0 %copy-start.11 = (f32[128,8,512]{2,0,1:T(8,128)S(1)}, f32[128,8,512]{2,0,1:T(8,128)}, u32[]{:S(2)}) copy-start(f32[128,8,512]{2,0,1:T(8,128)} %copy-done.10) | copy-start | bytes 6291460
  553.3 2.6 copy-start.48
  553.3 2.8 copy-start.46
  815.0 3.9 copy-start.30
  815.0 4.9 copy-start.20
  819.9 3.7 copy-start.19
  823.6 2.1 copy-start.34
  823.6 3.5 copy-start.1
  (5 other events, 3.9 us)
Sparse Core Ops, SparseCore 0:
  10.8 89.8 all-gather.2
  136.4 8.8 all-gather.4
  260.0 13.0 reduce-scatter.2
  371.9 178.7 reduce-scatter.4
  558.7 235.3 all-reduce.6
  796.4 18.5 all-reduce.4
where the time goes:
time: 845 us; the launch traced here: 834 us
  waiting for transfers between devices  325 us (38%)
  matrix products  215 us (25%)
  local copies, waits for them, and re-layouts  166 us (20%)
  blocking collectives  74.8 us (9%)
  other arithmetic  31.9 us (4%)
  between operations  15.4 us (2%)
    psum x1, waiting for transfers between devices, per_device(): lax.psum((part_script, part_gain_attn, part_gain_ffn, part_qkv, part_out,...  193 us
    dot_general x27, matrix products, contract(): lax.dot_general(left, right, (((left_dim,), (right_dim,)), ((), ())), pre...  153 us
    reduce_scatter x1, waiting for transfers between devices, per_device(): lax.psum_scatter(proj_term, 'ent', scatter_dimension=1, tiled=True)  66.1 us
    psum x1, blocking collectives, per_device(): lax.psum((part_script, part_gain_attn, part_gain_ffn, part_qkv, part_out,...  44.5 us
    unnamed x132, local copies, waits for them, and re-layouts  39.3 us
    all_gather x1, waiting for transfers between devices, per_device(): lax.all_gather(w_proj, 'ent', axis=1, tiled=True)  32 us
    all_to_all x1, blocking collectives, per_device(): lax.all_to_all(table_cols, 'ent', split_axis=0, concat_axis=1, tiled=True)  30.3 us
    psum x1, waiting for transfers between devices, per_device(): grad_w_proj = lax.psum(proj_part, 'rep')  20.9 us
  transfers between devices with their start and end apart: 7, of which 6 were waited for; matrix products, arithmetic and copies ran while one was open for 28% of the time, Pallas kernels for 0%

commit v1 on v0

v1 whole, which is shorter than its diff:
```python
import functools
import math

import jax
import jax.numpy as jnp
import numpy as np
from jax import lax
from jax.experimental import pallas as pl
from jax.experimental.pallas import tpu as pltpu
from jax.sharding import PartitionSpec as P

HEADS = 8
HEAD_DIM = 64
F32 = jnp.float32
BF16 = jnp.bfloat16
highest = lax.Precision.HIGHEST
MIB = 1024 * 1024


def make_levels(ent_count, rep_count):
    levels = [("rep", rep_count, 0)]
    bit, total = 0, ent_count.bit_length() - 1
    while bit < total:
        width = 1 if bit < 2 else min(2, total - bit)
        levels.append(("ent", 1 << width, bit))
        bit += width
    return levels


def slot_of(number, levels):
    rep_count = levels[0][1]
    slot = number % rep_count
    ent = number // rep_count
    for _, size, shift in levels[1:]:
        slot = slot * size + (ent >> shift) % size
    return slot


def swap(value, level, k):
    name, size, shift = level
    count = lax.axis_size(name)
    return lax.ppermute(value, name, [(i, i ^ (k << shift)) for i in range(count)])


def merge(value):
    return value.reshape((-1,) + value.shape[-2:])


class Line:
    def __init__(self):
        self.last = []

    def run(self, body, name, micros, grid, ins, outs, prefetch=(), alias=None, room=32 * MIB):
        count = len(prefetch) + len(ins)
        extra = self.last + ([] if alias is None else [alias])

        def wrapped(*refs):
            body(*refs[:count], *refs[count + len(extra) :])

        results = pl.pallas_call(
            wrapped,
            grid_spec=pltpu.PrefetchScalarGridSpec(
                num_scalar_prefetch=len(prefetch),
                grid=grid,
                in_specs=[spec for _, spec in ins] + [pl.BlockSpec(memory_space=pl.ANY)] * len(extra),
                out_specs=[spec for _, _, spec in outs],
            ),
            out_shape=[jax.ShapeDtypeStruct(shape, dtype) for shape, dtype, _ in outs],
            input_output_aliases={} if alias is None else {count + len(extra) - 1: 0},
            compiler_params=pltpu.CompilerParams(vmem_limit_bytes=room),
            cost_estimate=pl.CostEstimate(
                flops=int(micros * 1e9), bytes_accessed=int(micros * 3e6), transcendentals=0
            ),
            name=name,
        )(*prefetch, *(value for value, _ in ins), *extra)
        self.last = [min(results, key=lambda value: value.size)]
        return results


def swap(value, level, k=1):
    name, size, shift = level
    count = lax.axis_size(name)
    return lax.ppermute(value, name, [(i, i ^ (k << shift)) for i in range(count)])


def swaps(values, level):
    return [swap(value, level, k) for k, value in enumerate(values, 1)]


def stage_body(layout, cuts, *refs):
    sums, position = [], 0
    for number in layout:
        sums.append(refs[position : position + number])
        position += number

    def piece(number, index, cols):
        total = sums[number][0][index][:, cols]
        for ref in sums[number][1:]:
            total = total.astype(F32) + ref[index][:, cols].astype(F32)
        return total

    for out_ref, sources in zip(refs[position:], cuts):
        for target, parts in sources:
            for number, index, cols, row, col in parts:
                value = piece(number, index, cols).astype(out_ref.dtype)
                where = target + (slice(row, row + value.shape[0]), slice(col, col + value.shape[1]))
                out_ref[where] = value


def stage(line, sums, outs, steps=1):
    values = [value for kept, received in sums for value in [kept, *received]]

    def spec(shape):
        return pl.BlockSpec(memory_space=pltpu.VMEM)

    cuts = [
        [(target, source(target)) for target in np.ndindex(*lead)] for lead, _, _, _, source in outs
    ]
    shapes = [(lead + (rows, cols), dtype) for lead, rows, cols, dtype, _ in outs]
    held = [(value.shape, value.dtype) for value in values] + [(shape, jnp.dtype(dtype)) for shape, dtype in shapes]
    return line.run(
        functools.partial(stage_body, [1 + len(received) for _, received in sums], cuts),
        "exchange",
        2,
        (),
        [(value, spec(value.shape)) for value in values],
        [(shape, dtype, spec(shape)) for shape, dtype in shapes],
        room=2 * MIB + sum(math.prod(shape) * dtype.itemsize for shape, dtype in held),
    )


ALL = slice(None)


def split(number, value, axis, cols=ALL, width=None):
    lead = value.shape[:-2]
    rest = lead[:axis] + lead[axis + 1 :]
    outs = []
    for k in range(lead[axis]):

        def source(index, k=k):
            return [(number, index[:axis] + (k,) + index[axis:], cols, 0, 0)]

        outs.append((rest, value.shape[-2], width or value.shape[-1], F32 if k == 0 else BF16, source))
    return outs


def stacked(numbers, value, axis, rows=ALL):
    lead = value.shape[:-2]
    shape = lead[:axis] + (len(numbers),) + lead[axis:]

    def source(index):
        return [(numbers[index[axis]], index[:axis] + index[axis + 1 :], ALL, 0, 0)]

    return (shape, value.shape[-2], value.shape[-1], value.dtype, source)


def sum_halves(line, keep, send, levels, out):
    received = swap(send, levels[0])
    yield
    rows, width = keep.shape[-2:]
    half = width // 2
    left, right = slice(0, half), slice(half, width)
    steps = 4 if rows % 64 == 0 else 1
    outs = split(0, keep, 0, left, half) + split(0, keep, 1, right, half)
    keep_a, send_a, keep_b, send_b = stage(line, [(keep, [received])], outs, steps)
    got_a, got_b = swap(send_a, levels[1]), swap(send_b, levels[2])
    yield
    outs = split(0, keep_a, 0) + split(1, keep_b, 0)
    sums = [(keep_a, [got_a]), (keep_b, [got_b])]
    keep_a, send_a, keep_b, send_b = stage(line, sums, outs, steps)
    sums = [(keep_a, [swap(send_a, levels[2])]), (keep_b, [swap(send_b, levels[1])])]
    yield
    for place, level in enumerate(levels[3:]):
        if place == 0:
            lead = keep_a.shape[1:-2]

            def source(index, k):
                return [(0, (k,) + index, ALL, 0, 0), (1, (k,) + index, ALL, 0, half)]

            outs = [
                (lead, rows, width, F32 if k == 0 else BF16, functools.partial(source, k=k))
                for k in range(level[1])
            ]
        else:
            outs = split(0, keep, 0)
        keep, *sends = stage(line, sums, outs)
        sums = [(keep, swaps(sends, level))]
        yield
    out += stage(line, sums, [((), rows, width, F32, lambda index: [(0, (), ALL, 0, 0)])])
    yield


def finish(line, sums, far, rows):
    for level in far:
        outs = [((), rows, PANEL, dtype, lambda index: [(0, (), ALL, 0, 0)]) for dtype in (F32, BF16)]
        keep, send = stage(line, sums, outs)
        sums = [(keep, [swap(send, level, k) for k in range(1, level[1])])]
        yield
    yield stage(line, sums, [((), rows, PANEL, BF16, lambda index: [(0, (), ALL, 0, 0)])])[0]


def all_sum(line, keep, send, near, far, out):
    received = swap(send, near[0])
    yield
    rows = keep.shape[-2]
    sums = [(keep, [received])]
    for level in near[1:]:
        keep, *sends = stage(line, sums, split(0, keep, 0))
        sums = [(keep, swaps(sends, level))]
        yield
    for value in finish(line, sums, far, rows):
        if value is None:
            yield
    for level in near[:0:-1]:
        got = [swap(value, level, k) for k in range(1, level[1])]
        yield
        numbers = list(range(level[1]))
        value = stage(line, [(part, []) for part in [value, *got]], [stacked(numbers, value, 0)])[0]
    out += [value, swap(value, near[0])]
    yield


def all_sum_two(line, keep_a, send_a, keep_b, send_b, near, far, out):
    got_a, got_b = swap(send_a, near[0]), swap(send_b, near[0])
    yield
    rows = keep_a.shape[-2]
    outs = split(0, keep_a, 0) + split(1, keep_b, 1)
    keep_a, send_a, keep_b, send_b = stage(line, [(keep_a, [got_a]), (keep_b, [got_b])], outs)
    got_a, got_b = swap(send_a, near[1]), swap(send_b, near[2])
    yield
    outs = split(0, keep_a, 0) + split(1, keep_b, 0)
    keep_a, send_a, keep_b, send_b = stage(line, [(keep_a, [got_a]), (keep_b, [got_b])], outs)
    sums = [(keep_a, [swap(send_a, near[2])]), (keep_b, [swap(send_b, near[1])])]
    yield
    for place, level in enumerate(near[3:]):
        if place == 0:
            lead = keep_a.shape[1:-2]

            def source(index, k):
                return [(0, (k,) + index, ALL, 0, 0), (1, (k,) + index, ALL, rows, 0)]

            outs = [
                (lead, 2 * rows, PANEL, F32 if k == 0 else BF16, functools.partial(source, k=k))
                for k in range(level[1])
            ]
        else:
            outs = split(0, keep, 0)
        keep, *sends = stage(line, sums, outs)
        sums = [(keep, swaps(sends, level))]
        yield
    for value in finish(line, sums, far, 2 * rows):
        if value is None:
            yield
    for place, level in reversed(list(enumerate(near[3:]))):
        got = [swap(value, level, k) for k in range(1, level[1])]
        yield
        numbers = list(range(level[1]))
        value = stage(line, [(part, []) for part in [value, *got]], [stacked(numbers, value, 0)])[0]
    value_a, value_b = value[..., :rows, :], value[..., rows:, :]
    got_a, got_b = swap(value_a, near[2]), swap(value_b, near[1])
    yield
    sums = [(part, []) for part in (value_a, got_a, value_b, got_b)]
    outs = [stacked([0, 1], value_a, 0), stacked([2, 3], value_b, 0)]
    value_a, value_b = stage(line, sums, outs)
    got_a, got_b = swap(value_a, near[1]), swap(value_b, near[2])
    yield
    sums = [(part, []) for part in (value_a, got_a, value_b, got_b)]
    outs = [stacked([0, 1], value_a, 0), stacked([2, 3], value_b, 1)]
    value_a, value_b = stage(line, sums, outs)
    out += [value_a, swap(value_a, near[0]), value_b, swap(value_b, near[0])]
    yield


def fixed(shape):
    return pl.BlockSpec(shape, lambda i, *_: (0,) * len(shape))


def rows_of(rows, width):
    return pl.BlockSpec((rows, width), lambda i, *_: (i, 0))


def selector(ids, base, rows):
    entry = lax.broadcasted_iota(jnp.int32, (rows, 1), 0).astype(jnp.int16)
    return jnp.where(entry == (ids - base).astype(jnp.int16), jnp.ones((), BF16), jnp.zeros((), BF16))


def nt(left, right):
    return lax.dot_general(left, right, (((1,), (1,)), ((), ())), preferred_element_type=F32)


def tn(left, right):
    return lax.dot_general(left, right, (((0,), (0,)), ((), ())), preferred_element_type=F32)


def mm(left, right):
    return jnp.dot(left, right, preferred_element_type=F32)


def scatter_some(first, ids_ref, grad, proj_ref, table_ref, pooled_ref):
    rows = table_ref.shape[0]
    part = nt(selector(ids_ref[...], first + pl.program_id(0) * rows, rows), grad).astype(BF16)
    table_ref[...] = part
    pooled_ref[...] = nt(part, proj_ref[...]).astype(pooled_ref.dtype)


def scatter_first_body(first, ids_ref, grad_ref, proj_ref, table_ref, pooled_ref, flat_ref):
    @pl.when(pl.program_id(0) == 0)
    def _():
        flat_ref[...] = grad_ref[...].reshape(flat_ref.shape)

    scatter_some(first, ids_ref, flat_ref[...], proj_ref, table_ref, pooled_ref)


def scatter_body(first, ids_ref, flat_ref, proj_ref, table_ref, pooled_ref):
    scatter_some(first, ids_ref, flat_ref[...], proj_ref, table_ref, pooled_ref)


def scatter_rows(line, ids, grad, w_proj, first, count, dtype):
    features = grad.shape[0]
    tokens = ids.shape[1]
    width = w_proj.shape[0]
    rows = min(512, count)
    flat = (features, tokens)
    fresh = grad.ndim == 3
    return line.run(
        functools.partial(scatter_first_body if fresh else scatter_body, first),
        "scatter_rows",
        14,
        (count // rows,),
        [(ids, fixed((1, tokens))), (grad, fixed(grad.shape)), (w_proj, fixed(w_proj.shape))],
        [
            ((count, features), BF16, rows_of(rows, features)),
            ((count, width), dtype, rows_of(rows, width)),
        ]
        + ([(flat, BF16, fixed(flat))] if fresh else []),
        room=44 * MIB,
    )


def table_body(steps, each, owners_ref, pooled_ref, proj_ref, own_ref, other_ref, table_ref, grad_ref):
    step = pl.program_id(0)
    slots = own_ref.shape[0] // each

    @pl.when(step == 0)
    def _():
        grad_ref[...] = jnp.zeros_like(grad_ref)

    parts = []
    for j in range(slots):
        base = pl.multiple_of(owners_ref[step * slots + j] * each, each)
        parts.append(pooled_ref[pl.ds(base, each)])
    pooled = jnp.concatenate(parts, axis=0)
    cols = lax.dot_general(
        proj_ref[...], pooled, (((0,), (1,)), ((), ())), preferred_element_type=F32
    )
    table_ref[...] = cols.astype(BF16)

    @pl.when(step < steps)
    def _():
        grad_ref[...] += tn(pooled, own_ref[...])

    @pl.when(step >= steps)
    def _():
        grad_ref[...] += tn(pooled, other_ref[...])


def table_and_grad(line, owners, pooled, w_proj, part_own, part_other):
    vocab, width = pooled.shape
    features = w_proj.shape[1]
    rows = min(1024, vocab // 2)
    steps = vocab // 2 // rows
    return line.run(
        functools.partial(table_body, steps, vocab // owners.shape[0]),
        "table_and_grad",
        7,
        (2 * steps,),
        [
            (pooled, fixed(pooled.shape)),
            (w_proj, fixed(w_proj.shape)),
            (part_own, pl.BlockSpec((rows, features), lambda i, *_: (jnp.minimum(i, steps - 1), 0))),
            (part_other, pl.BlockSpec((rows, features), lambda i, *_: (jnp.maximum(i - steps, 0), 0))),
        ],
        [
            ((features, vocab), BF16, pl.BlockSpec((features, rows), lambda i, *_: (0, i))),
            ((width, features), F32, fixed((width, features))),
        ],
        [owners],
    )


def lookup_body(chunk, ids_ref, *refs):
    table_refs, out_ref = refs[:-1], refs[-1]
    rows = ids_ref.shape[0]

    def find(base, table):
        picks = [selector(ids_ref[row : row + 1], base, chunk) for row in range(rows)]
        return mm(table, jnp.concatenate(picks, axis=1))

    total = None
    for index, table_ref in enumerate(table_refs):
        vocab = table_ref.shape[1]
        for inner in range(0, vocab, chunk):
            part = find(index * vocab + inner, table_ref[:, inner : inner + chunk])
            total = part if total is None else total + part
    out_ref[...] = total.astype(BF16).reshape(out_ref.shape)


def lookup(line, ids, tables, half, before=None):
    rows, text_len = ids.shape
    features, vocab = tables[0].shape
    block = math.gcd(text_len // 2, 256)
    steps = text_len // 2 // block
    return line.run(
        functools.partial(lookup_body, min(vocab, 4096)),
        "lookup",
        13,
        (steps,),
        [(ids, pl.BlockSpec((rows, block), lambda i, *_: (0, i + half * steps)))]
        + [(table, fixed(table.shape)) for table in tables],
        [
            (
                (features, rows, text_len),
                BF16,
                pl.BlockSpec((features, rows, block), lambda i, *_: (0, 0, i + half * steps)),
            )
        ],
        alias=before,
    )[0]


PANEL = 512


def store_slots(slots_ref, first, part, keep_ref, send_ref):
    rows = keep_ref.shape[1]
    half = keep_ref.shape[0]
    for j in range(part.shape[0] // rows):
        slot = slots_ref[first + j]
        piece = part[j * rows : (j + 1) * rows]

        @pl.when(slot < half)
        def _():
            keep_ref[slot] = piece

        @pl.when(slot >= half)
        def _():
            send_ref[slot - half] = piece.astype(BF16)


def weight_body(slots_ref, left_ref, right_ref, keep_ref, send_ref):
    part = tn(left_ref[...], right_ref[...])
    store_slots(slots_ref, pl.program_id(0) * (part.shape[0] // keep_ref.shape[1]), part, keep_ref, send_ref)


def two_weights_body(last, slots_ref, left_ref, right_ref, left2_ref, right2_ref, keep_ref, send_ref):
    step = pl.program_id(0)
    each = left_ref.shape[1] // keep_ref.shape[1]

    @pl.when(step < last)
    def _():
        store_slots(slots_ref, step * each, tn(left_ref[...], right_ref[...]), keep_ref, send_ref)

    @pl.when(step == last)
    def _():
        store_slots(slots_ref, step * each, tn(left2_ref[...], right2_ref[...]), keep_ref, send_ref)


def slot_outs(count, rows):
    shape = (count // 2, rows, PANEL)
    return [(shape, F32, fixed(shape)), (shape, BF16, fixed(shape))]


def panel_of(depth):
    return pl.BlockSpec((depth, PANEL), lambda i, *_: (0, i))


def tall_weight(line, slots, left, right):
    depth, height = left.shape
    return line.run(
        weight_body,
        "tall_weight",
        6,
        (height // PANEL,),
        [(left, panel_of(depth)), (right, fixed(right.shape))],
        slot_outs(slots.shape[0], height // slots.shape[0]),
        [slots],
    )


def wide_weight(line, slots, left, right):
    depth, cols = right.shape
    return line.run(
        weight_body,
        "wide_weight",
        8,
        (cols // PANEL,),
        [(left, fixed(left.shape)), (right, panel_of(depth))],
        slot_outs(slots.shape[0], cols // PANEL * left.shape[1] // slots.shape[0]),
        [slots],
    )


def two_weights(line, slots, left, right, left2, right2):
    depth, cols = right.shape
    last = cols // PANEL
    return line.run(
        functools.partial(two_weights_body, last),
        "two_weights",
        8,
        (last + 1,),
        [
            (left, fixed(left.shape)),
            (right, pl.BlockSpec((depth, PANEL), lambda i, *_: (0, jnp.minimum(i, last - 1)))),
            (left2, fixed(left2.shape)),
            (right2, fixed(right2.shape)),
        ],
        slot_outs(slots.shape[0], (last + 1) * left.shape[1] // slots.shape[0]),
        [slots],
    )


def load_slots(slots_ref, first, own_ref, other_ref, out_ref):
    half, rows, _ = own_ref.shape
    for j in range(out_ref.shape[0] // rows):
        slot = slots_ref[first + j]

        @pl.when(slot < half)
        def _():
            out_ref[j * rows : (j + 1) * rows] = own_ref[slot].astype(F32)

        @pl.when(slot >= half)
        def _():
            out_ref[j * rows : (j + 1) * rows] = other_ref[slot - half].astype(F32)


def unpack_body(slots_ref, own_ref, other_ref, out_ref):
    each = out_ref.shape[0] // own_ref.shape[1]
    load_slots(slots_ref, pl.program_id(0) * each, own_ref, other_ref, out_ref)


def unpack_two_body(last, slots_ref, own_ref, other_ref, out_ref, out2_ref):
    step = pl.program_id(0)
    each = out_ref.shape[0] // own_ref.shape[1]

    @pl.when(step < last)
    def _():
        load_slots(slots_ref, step * each, own_ref, other_ref, out_ref)

    @pl.when(step == last)
    def _():
        load_slots(slots_ref, step * each, own_ref, other_ref, out2_ref)


def unpack(line, slots, own, other, height, cols):
    tall = cols == PANEL
    tile = 512
    index = (lambda i, *_: (i, 0)) if tall else (lambda i, *_: (0, i))
    return line.run(
        unpack_body,
        "unpack",
        5,
        (height * cols // (tile * PANEL),),
        [(own, fixed(own.shape)), (other, fixed(other.shape))],
        [((height, cols), F32, pl.BlockSpec((tile if tall else height, PANEL), index))],
        [slots],
    )[0]


def unpack_two(line, slots, own, other, height, cols):
    last = cols // PANEL
    return line.run(
        functools.partial(unpack_two_body, last),
        "unpack_two",
        5,
        (last + 1,),
        [(own, fixed(own.shape)), (other, fixed(other.shape))],
        [
            (
                (height, cols),
                F32,
                pl.BlockSpec((height, PANEL), lambda i, *_: (0, jnp.minimum(i, last - 1))),
            ),
            ((height, PANEL), F32, fixed((height, PANEL))),
        ],
        [slots],
    )


GROUP = 128
PAIR = 2 * HEAD_DIM
GELU_SCALE = 0.7978845608028654
GELU_CUBE = 0.044715


def center(values):
    centered = values - jnp.mean(values, axis=-1, keepdims=True)
    spread = jnp.mean(centered * centered, axis=-1, keepdims=True)
    rate = lax.rsqrt(spread + 1e-05)
    return centered * rate, rate


def center_back(grad, gain, unit, rate):
    gain_grad = jnp.sum(grad * unit, axis=0, keepdims=True)
    grad = grad * gain
    mean_grad = jnp.mean(grad, axis=-1, keepdims=True)
    mean_unit = jnp.mean(grad * unit, axis=-1, keepdims=True)
    return rate * (grad - mean_grad - unit * mean_unit), gain_grad


def start_of(pieces_ref, scripts_ref, script_table_ref):
    entries, slots, width = pieces_ref.shape
    groups = script_table_ref.shape[0]
    pieces = pieces_ref[...].astype(F32).reshape(entries * slots, width)
    onehot = (scripts_ref[...] == lax.broadcasted_iota(jnp.int32, (1, groups), 1)).astype(F32)
    return pieces + jnp.dot(onehot, script_table_ref[...], precision=highest), onehot


def slot_weights(lengths, slots):
    rows = lengths.shape[0]
    slot = lax.broadcasted_iota(jnp.int32, (rows, 1), 0) % slots
    return jnp.where(slot <= lengths, 1.0 / (lengths + 1).astype(F32), 0.0)


def split_heads(pair):
    first = lax.broadcasted_iota(jnp.int32, pair.shape, 1) < HEAD_DIM
    zero = jnp.zeros_like(pair)
    return jnp.concatenate([jnp.where(first, pair, zero), jnp.where(first, zero, pair)], axis=0)


def join_heads(stacked):
    first = lax.broadcasted_iota(jnp.int32, (GROUP, PAIR), 1) < HEAD_DIM
    return jnp.where(first, stacked[:GROUP], stacked[GROUP:])


def attn_body(
    slots,
    pieces_ref,
    scripts_ref,
    lengths_ref,
    script_table_ref,
    gain_attn_ref,
    gain_ffn_ref,
    w_qkv_ref,
    w_out_ref,
    normed_ref,
    mixed_ref,
    context_ref,
    middle_ref,
    normed_ffn_ref,
):
    start, _ = start_of(pieces_ref, scripts_ref, script_table_ref)
    rows, width = start.shape
    lengths = lengths_ref[...]
    normed = (center(start)[0] * gain_attn_ref[...]).astype(BF16)
    normed_ref[...] = normed
    mixed = mm(normed, w_qkv_ref[...]).astype(BF16)
    mixed_ref[...] = mixed
    row = lax.broadcasted_iota(jnp.int32, (GROUP, GROUP), 0)
    col = lax.broadcasted_iota(jnp.int32, (GROUP, GROUP), 1)
    groups = []
    for base in range(0, rows, GROUP):
        part = mixed[base : base + GROUP]
        valid = (row // slots == col // slots) & (col % slots <= lengths[base : base + GROUP])
        lows = range(0, width, PAIR)
        raws = [
            nt(part[:, low : low + PAIR], split_heads(part[:, width + low : width + low + PAIR]))
            for low in lows
        ]
        heads = [raw[:, side : side + GROUP] for raw in raws for side in (0, GROUP)]
        heads = [jnp.where(valid, head * HEAD_DIM ** (-0.5), -1000000000.0) for head in heads]
        heads = [jnp.exp(head - jnp.max(head, axis=1, keepdims=True)) for head in heads]
        heads = [(head * (1.0 / jnp.sum(head, axis=1, keepdims=True))).astype(BF16) for head in heads]
        pairs = [
            mm(
                jnp.concatenate(heads[2 * j : 2 * j + 2], axis=1),
                split_heads(part[:, 2 * width + low : 2 * width + low + PAIR]),
            )
            for j, low in enumerate(lows)
        ]
        groups.append(jnp.concatenate(pairs, axis=1).astype(BF16))
    context = jnp.concatenate(groups, axis=0)
    context_ref[...] = context
    middle = start + mm(context, w_out_ref[...])
    middle_ref[...] = middle
    normed_ffn_ref[...] = (center(middle)[0] * gain_ffn_ref[...]).astype(BF16)


def attn_forward(
    line, pieces, scripts, lengths, script_table, gain_attn, gain_ffn, w_qkv, w_out
):
    entries, slots, width = pieces.shape
    total = entries * slots
    rows = math.gcd(total, 256)
    some = rows // slots
    whole = (script_table, gain_attn, gain_ffn, w_qkv, w_out)
    return line.run(
        functools.partial(attn_body, slots),
        "attn_forward",
        12,
        (total // rows,),
        [
            (pieces, pl.BlockSpec((some, slots, width), lambda i, *_: (i, 0, 0))),
            (scripts, rows_of(rows, 1)),
            (lengths, rows_of(rows, 1)),
        ]
        + [(value, fixed(value.shape)) for value in whole],
        [
            ((total, width), BF16, rows_of(rows, width)),
            ((total, 3 * width), BF16, rows_of(rows, 3 * width)),
            ((total, width), BF16, rows_of(rows, width)),
            ((total, width), F32, rows_of(rows, width)),
            ((total, width), BF16, rows_of(rows, width)),
        ],
    )


def ffn_body(
    slots,
    length_rows_ref,
    lengths_ref,
    middle_ref,
    normed_ref,
    w_up_ref,
    w_down_ref,
    slope_ref,
    hidden_ref,
    pooled_ref,
):
    rows, width = middle_ref.shape
    some = rows // slots
    weights = slot_weights(length_rows_ref[...], slots)
    row = lax.broadcasted_iota(jnp.int32, (some, rows), 1)
    entry = lax.broadcasted_iota(jnp.int32, (some, rows), 0)
    lengths = lengths_ref[...]
    valid = (row // slots == entry) & (row % slots <= lengths)
    valid = jnp.where(valid, 1.0, 0.0).astype(BF16)
    scale = 1.0 / (lengths + 1).astype(F32)
    pooled = jnp.sum((middle_ref[...] * weights).reshape(some, slots, width), axis=1)
    ff = w_up_ref.shape[1]
    step = ff // 4
    for low in range(0, ff, step):
        up = mm(normed_ref[...], w_up_ref[:, low : low + step])
        square = up * up
        tanh = jnp.tanh(up * (GELU_SCALE + GELU_SCALE * GELU_CUBE * square))
        half_up = 0.5 * up
        hidden = (half_up + half_up * tanh).astype(BF16)
        slope_ref[:, low : low + step] = (0.5 + 0.5 * tanh) + half_up * (1.0 - tanh * tanh) * (
            GELU_SCALE + 3.0 * GELU_SCALE * GELU_CUBE * square
        )
        mean_hidden = mm(valid, hidden) * scale
        high = mean_hidden.astype(BF16)
        rest = (mean_hidden - high.astype(F32)).astype(BF16)
        hidden_ref[:, low : low + step] = high
        w_down = w_down_ref[low : low + step]
        pooled += mm(high, w_down) + mm(rest, w_down)
    pooled_ref[...] = pooled.astype(BF16)


def ffn_forward(line, length_rows, lengths, middle, normed, w_up, w_down):
    total, width = middle.shape
    entries = lengths.shape[0]
    slots = total // entries
    rows = math.gcd(total, 256)
    some = rows // slots
    ff = w_up.shape[1]
    return line.run(
        functools.partial(ffn_body, slots),
        "ffn_forward",
        12,
        (total // rows,),
        [
            (length_rows, rows_of(rows, 1)),
            (lengths, rows_of(some, 1)),
            (middle, rows_of(rows, width)),
            (normed, rows_of(rows, width)),
            (w_up, fixed(w_up.shape)),
            (w_down, fixed(w_down.shape)),
        ],
        [
            ((total, ff), F32, rows_of(rows, ff)),
            ((entries, ff), BF16, rows_of(some, ff)),
            ((entries, width), BF16, rows_of(some, width)),
        ],
    )


def ffn_back_body(
    slots,
    pooled_grad_ref,
    lengths_ref,
    slope_ref,
    middle_ref,
    gain_ffn_ref,
    w_up_ref,
    w_down_ref,
    grad_up_ref,
    grad_middle_ref,
    grad_branch_ref,
    gain_grad_ref,
):
    pooled_grad = pooled_grad_ref[...]
    rows, width = middle_ref.shape
    some = rows // slots
    wide = jnp.broadcast_to(pooled_grad[:, None, :], (some, slots, width)).reshape(rows, width)
    grad_final = wide * slot_weights(lengths_ref[...], slots)
    grad_ffn = grad_final.astype(BF16)
    ff = w_up_ref.shape[1]
    step = ff // 4
    grad_normed = jnp.zeros((rows, width), F32)
    for low in range(0, ff, step):
        grad_hidden = nt(grad_ffn, w_down_ref[low : low + step])
        grad_up = (slope_ref[:, low : low + step] * grad_hidden).astype(BF16)
        grad_up_ref[:, low : low + step] = grad_up
        grad_normed += nt(grad_up, w_up_ref[:, low : low + step])
    unit, rate = center(middle_ref[...])
    grad, gain_grad = center_back(grad_normed, gain_ffn_ref[...], unit, rate)
    grad_middle = grad_final + grad
    grad_middle_ref[...] = grad_middle
    grad_branch_ref[...] = grad_middle.astype(BF16)

    @pl.when(pl.program_id(0) == 0)
    def _():
        gain_grad_ref[...] = jnp.zeros_like(gain_grad_ref)

    gain_grad_ref[...] += gain_grad


def ffn_back(line, pooled_grad, lengths, slope, middle, gain_ffn, w_up, w_down):
    total, width = middle.shape
    entries = pooled_grad.shape[0]
    slots = total // entries
    rows = math.gcd(total, 256)
    some = rows // slots
    ff = w_up.shape[1]
    return line.run(
        functools.partial(ffn_back_body, slots),
        "ffn_back",
        15,
        (total // rows,),
        [
            (pooled_grad, rows_of(some, width)),
            (lengths, rows_of(rows, 1)),
            (slope, rows_of(rows, ff)),
            (middle, rows_of(rows, width)),
            (gain_ffn, fixed(gain_ffn.shape)),
            (w_up, fixed(w_up.shape)),
            (w_down, fixed(w_down.shape)),
        ],
        [
            ((total, ff), BF16, rows_of(rows, ff)),
            ((total, width), F32, rows_of(rows, width)),
            ((total, width), BF16, rows_of(rows, width)),
            ((1, width), F32, fixed((1, width))),
        ],
    )


def heads_back_body(slots, lengths_ref, w_out_ref, mixed_ref, grad_branch_ref, grad_mixed_ref):
    rows, width = grad_branch_ref.shape
    lengths = lengths_ref[...]
    grad_ctx = nt(grad_branch_ref[...], w_out_ref[...]).astype(BF16)
    row = lax.broadcasted_iota(jnp.int32, (GROUP, GROUP), 0)
    col = lax.broadcasted_iota(jnp.int32, (GROUP, GROUP), 1)
    same = row // slots == col // slots
    lows = range(0, width, PAIR)
    for base in range(0, rows, GROUP):
        span = slice(base, base + GROUP)
        valid = same & (row % slots <= lengths[span])
        queries = [mixed_ref[span, low : low + PAIR] for low in lows]
        keys = [split_heads(mixed_ref[span, width + low : width + low + PAIR]) for low in lows]
        values = [split_heads(mixed_ref[span, 2 * width + low : 2 * width + low + PAIR]) for low in lows]
        grad_pairs = [grad_ctx[span, low : low + PAIR] for low in lows]
        raws = [nt(key, query) for key, query in zip(keys, queries)]
        grad_raws = [nt(value, grad_pair) for value, grad_pair in zip(values, grad_pairs)]
        sides = (slice(0, GROUP), slice(GROUP, 2 * GROUP))
        heads = [raw[side] for raw in raws for side in sides]
        heads = [jnp.where(valid, head * HEAD_DIM ** (-0.5), -1000000000.0) for head in heads]
        heads = [jnp.exp(head - jnp.max(head, axis=0, keepdims=True)) for head in heads]
        probs = [head * (1.0 / jnp.sum(head, axis=0, keepdims=True)) for head in heads]
        grads = [grad_raw[side] for grad_raw in grad_raws for side in sides]
        grads = [
            prob * (grad - jnp.sum(grad * prob, axis=0, keepdims=True)) for prob, grad in zip(probs, grads)
        ]
        probs = [prob.astype(BF16) for prob in probs]
        grads = [(grad * HEAD_DIM ** (-0.5)).astype(BF16) for grad in grads]
        for j, low in enumerate(lows):
            scores_grad = jnp.concatenate(grads[2 * j : 2 * j + 2], axis=0)
            prob = jnp.concatenate(probs[2 * j : 2 * j + 2], axis=0)
            grad_mixed_ref[span, low : low + PAIR] = tn(scores_grad, keys[j]).astype(BF16)
            grad_keys = join_heads(mm(scores_grad, queries[j]))
            grad_mixed_ref[span, width + low : width + low + PAIR] = grad_keys.astype(BF16)
            grad_values = join_heads(mm(prob, grad_pairs[j]))
            grad_mixed_ref[span, 2 * width + low : 2 * width + low + PAIR] = grad_values.astype(BF16)


def heads_back(line, lengths, w_out, mixed, grad_branch, slots):
    total, width = grad_branch.shape
    rows = math.gcd(total, 256)
    return line.run(
        functools.partial(heads_back_body, slots),
        "heads_back",
        13,
        (total // rows,),
        [
            (lengths, rows_of(rows, 1)),
            (w_out, fixed(w_out.shape)),
            (mixed, rows_of(rows, 3 * width)),
            (grad_branch, rows_of(rows, width)),
        ],
        [((total, 3 * width), BF16, rows_of(rows, 3 * width))],
    )[0]


def attn_back_body(
    pieces_ref,
    scripts_ref,
    script_table_ref,
    gain_attn_ref,
    w_qkv_ref,
    grad_mixed_ref,
    grad_middle_ref,
    grad_pieces_ref,
    gain_grad_ref,
    script_grad_ref,
):
    start, onehot = start_of(pieces_ref, scripts_ref, script_table_ref)
    grad_normed = nt(grad_mixed_ref[...], w_qkv_ref[...])
    unit, rate = center(start)
    grad, gain_grad = center_back(grad_normed, gain_attn_ref[...], unit, rate)
    grad_pieces = grad_middle_ref[...] + grad
    grad_pieces_ref[...] = grad_pieces.reshape(grad_pieces_ref.shape)

    @pl.when(pl.program_id(0) == 0)
    def _():
        gain_grad_ref[...] = jnp.zeros_like(gain_grad_ref)
        script_grad_ref[...] = jnp.zeros_like(script_grad_ref)

    gain_grad_ref[...] += gain_grad
    script_grad_ref[...] += lax.dot_general(
        onehot, grad_pieces, (((0,), (0,)), ((), ())), precision=highest
    )


def attn_back(
    line, pieces, scripts, script_table, gain_attn, w_qkv, grad_mixed, grad_middle
):
    entries, slots, width = pieces.shape
    total = entries * slots
    rows = math.gcd(total, 256)
    some = rows // slots
    return line.run(
        attn_back_body,
        "attn_back",
        9,
        (total // rows,),
        [
            (pieces, pl.BlockSpec((some, slots, width), lambda i, *_: (i, 0, 0))),
            (scripts, rows_of(rows, 1)),
            (script_table, fixed(script_table.shape)),
            (gain_attn, fixed(gain_attn.shape)),
            (w_qkv, fixed(w_qkv.shape)),
            (grad_mixed, rows_of(rows, 3 * width)),
            (grad_middle, rows_of(rows, width)),
        ],
        [
            ((entries, slots, width), F32, pl.BlockSpec((some, slots, width), lambda i, *_: (i, 0, 0))),
            ((1, width), F32, fixed((1, width))),
            (script_table.shape, F32, fixed(script_table.shape)),
        ],
    )


def per_device(
    pieces,
    lengths,
    scripts,
    script_table,
    gain_attn,
    gain_ffn,
    w_qkv,
    w_out,
    w_up,
    w_down,
    w_proj,
    token_ids,
    out_grad,
):
    entries, slots, width = pieces.shape
    ent_count = lax.axis_size("ent")
    rep_count = lax.axis_size("rep")
    devices = ent_count * rep_count
    features = w_proj.shape[1]
    vocab = entries * devices
    rows_dev, text_len = token_ids.shape
    tokens = rows_dev * text_len
    levels = make_levels(ent_count, rep_count)
    sizes = tuple(size for _, size, _ in levels)
    me = lax.axis_index("ent") * rep_count + lax.axis_index("rep")
    chunks = 1 if devices <= 32 else 8
    each = entries // chunks
    span = vocab // chunks
    slot = slot_of(token_ids // entries ^ me, levels)
    within = token_ids % entries
    slot_ids = within // each * span + slot * each + within % each
    script_rows = jnp.repeat(scripts, slots)[:, None]
    length_rows = jnp.repeat(lengths, slots)[:, None]
    gain_attn, gain_ffn = gain_attn[None], gain_ffn[None]

    cut = len(levels)
    while math.prod(sizes[:cut]) * 16 > w_down.shape[0]:
        cut -= 1
    near, far = levels[:cut], levels[cut:]
    count = math.prod(sizes[:cut])
    slot_index = jnp.arange(count, dtype=jnp.int32) ^ slot_of(me, near)
    line = Line()

    def cut_up(keep, send, some):
        shape = tuple(size for _, size, _ in some[1:]) + keep.shape[-2:]
        return keep.reshape(shape), send.reshape(shape)

    flat_ids = slot_ids.reshape(1, tokens)
    flat_grad = out_grad
    parts, pooled_grads = [], []
    for chunk in range(chunks):
        first = chunk * span
        part_send, send, *flat = scatter_rows(
            line, flat_ids, flat_grad, w_proj, first + span // 2, span // 2, BF16
        )
        flat_grad = flat[0] if flat else flat_grad
        part_keep, keep = scatter_rows(line, flat_ids, flat_grad, w_proj, first, span // 2, F32)
        parts.append((part_keep, part_send))
        shape = sizes[1:] + (each, width)
        pooling = sum_halves(line, keep.reshape(shape), send.reshape(shape), levels, pooled_grads)
        if chunks > 1:
            for _ in pooling:
                pass
    next(pooling, None)
    next(pooling, None)
    normed, mixed, context, middle, normed_ffn = attn_forward(
        line, pieces, script_rows, length_rows, script_table, gain_attn, gain_ffn, w_qkv, w_out
    )
    next(pooling, None)
    slope, hidden, pooled = ffn_forward(
        line, length_rows, lengths[:, None], middle, normed_ffn, w_up, w_down
    )
    gathered = [
        lax.all_gather(pooled[chunk * each :][:each], ("ent", "rep"), axis=0, tiled=True)
        for chunk in range(chunks)
    ]
    for _ in pooling:
        pass
    grad_pooled = jnp.concatenate(pooled_grads, axis=0) if chunks > 1 else pooled_grads[0]

    down = tall_weight(line, slot_index, hidden, grad_pooled.astype(BF16))
    grad_up, grad_middle, grad_branch, part_gain_ffn = ffn_back(
        line, grad_pooled, length_rows, slope, middle, gain_ffn, w_up, w_down
    )
    up = wide_weight(line, slot_index, normed_ffn, grad_up)
    ffn_all, two_all = [], []
    ffn_sum = all_sum_two(line, *cut_up(*down, near), *cut_up(*up, near), near, far, ffn_all)
    next(ffn_sum)
    grad_mixed = heads_back(line, length_rows, w_out, mixed, grad_branch, slots)
    next(ffn_sum)
    two = two_weights(line, slot_index, normed, grad_mixed, context, grad_branch)
    two_sum = all_sum(line, *cut_up(*two, near), near, far, two_all)
    next(two_sum)
    next(ffn_sum)
    grad_pieces, part_gain_attn, part_script = attn_back(
        line, pieces, script_rows, script_table, gain_attn, w_qkv, grad_mixed, grad_middle
    )
    small = lax.all_gather(
        jnp.concatenate([part_script, part_gain_attn, part_gain_ffn], axis=0), ("ent", "rep"), axis=0
    )
    small = jnp.sum(small, axis=0)
    next(ffn_sum)
    next(two_sum)
    numbers = np.argsort(slot_of(np.arange(devices), levels)).astype(np.int32)
    owners = jnp.asarray(numbers) ^ me
    tables, part_proj = [], None
    for chunk in range(chunks):
        table, part = table_and_grad(line, owners, gathered[chunk], w_proj, *parts[chunk])
        tables.append(table)
        part_proj = part if part_proj is None else part_proj + part
    grad_w_proj = part_proj + swap(part_proj, levels[0])
    next(ffn_sum)
    next(two_sum)
    looked_up = lookup(line, slot_ids, tables, 0)
    next(ffn_sum)
    next(two_sum)
    looked_up = lookup(line, slot_ids, tables, 1, looked_up)
    going = [ffn_sum, two_sum]
    while going:
        going = [steps for steps in going if next(steps, 0) is None]
    grad_w_down = unpack(line, slot_index, merge(ffn_all[0]), merge(ffn_all[1]), *w_down.shape)
    grad_w_up = unpack(line, slot_index, merge(ffn_all[2]), merge(ffn_all[3]), *w_up.shape)
    grad_w_qkv, grad_w_out = unpack_two(line, slot_index, *map(merge, two_all), *w_qkv.shape)
    groups = script_table.shape[0]
    return (
        looked_up,
        grad_pieces,
        small[:groups],
        small[groups],
        small[groups + 1],
        grad_w_qkv,
        grad_w_out,
        grad_w_up,
        grad_w_down,
        grad_w_proj,
    )


def solution(mesh):
    in_specs = (
        P(("ent", "rep"), None, None),
        P(("ent", "rep")),
        P(("ent", "rep")),
        P(),
        P(),
        P(),
        P(),
        P(),
        P(),
        P(),
        P(None, "ent"),
        P("rep", None),
        P("ent", "rep", None),
    )
    out_specs = (
        P("ent", "rep", None),
        P(("ent", "rep"), None, None),
        P(),
        P(),
        P(),
        P(),
        P(),
        P(),
        P(),
        P(None, "ent"),
    )
    return jax.shard_map(
        per_device, mesh=mesh, in_specs=in_specs, out_specs=out_specs, check_vma=False
    )
```

time: 845 us -> 283 us (0.33); the launches traced: 834 us -> 282 us
  waiting for transfers between devices: 325 us -> 46.5 us
  matrix products: 215 us -> 0 us
  Pallas kernels: 0 us -> 132 us
  local copies, waits for them, and re-layouts: 166 us -> 39.8 us
  blocking collectives: 74.8 us -> 0 us
  starting transfers between devices: 6.86 us -> 42.7 us
  other arithmetic: 31.9 us -> 6.14 us
    dot_general x45 -> x0, matrix products: 215 us -> none  [the longest x27 153 us: contract(): lax.dot_general(left, right, (((left_dim,), (right_dim,)), ((), ())), pre...]
    psum x2 -> x0, waiting for transfers between devices: 214 us -> none  [the longest x1 193 us: per_device(): lax.psum((part_script, part_gain_attn, part_gain_ffn, part_qkv, part_out,...]
    pallas_call x0 -> x34, Pallas kernels: none -> 132 us  [run(): pl.pallas_call(wrapped, grid_spec=pltpu.PrefetchScalarGridSpec(num_scalar...]
    reduce_scatter x2 -> x0, waiting for transfers between devices: 66.1 us -> none  [the longest x1 66.1 us: per_device(): lax.psum_scatter(proj_term, 'ent', scatter_dimension=1, tiled=True)]
    ppermute x0 -> x39, waiting for transfers between devices: none -> 46.5 us  [swap(): lax.ppermute(value, name, [(i, i ^ k << shift) for i in range(count)])]
    psum x1 -> x0, blocking collectives: 44.5 us -> none  [per_device(): lax.psum((part_script, part_gain_attn, part_gain_ffn, part_qkv, part_out,...]
    convert_element_type x8 -> x0, local copies, waits for them, and re-layouts: 42.9 us -> none  [the longest x2 19.9 us: per_device(): jnp.stack([grad_queries, grad_keys, grad_values], axis=2)]
    ppermute x0 -> x39, starting transfers between devices: none -> 42.7 us  [swap(): lax.ppermute(value, name, [(i, i ^ k << shift) for i in range(count)])]
  transfers between devices with their start and end apart: 7 -> 41, of which waited for: 6 -> 14; matrix products, arithmetic and copies ran while one was open for 28% -> 2% of each run, Pallas kernels for 0% -> 35%
where the time goes in v1:
time: 283 us; the launch traced here: 282 us
  Pallas kernels  132 us (47%)
  waiting for transfers between devices  46.5 us (16%)
  starting transfers between devices  42.7 us (15%)
  local copies, waits for them, and re-layouts  39.8 us (14%)
  between operations  14.7 us (5%)
  other arithmetic  6.14 us (2%)
    pallas_call x34, Pallas kernels, run(): pl.pallas_call(wrapped, grid_spec=pltpu.PrefetchScalarGridSpec(num_scalar...  132 us
    ppermute x39, waiting for transfers between devices, swap(): lax.ppermute(value, name, [(i, i ^ k << shift) for i in range(count)])  46.5 us
    ppermute x39, starting transfers between devices, swap(): lax.ppermute(value, name, [(i, i ^ k << shift) for i in range(count)])  42.7 us
    unnamed x119, local copies, waits for them, and re-layouts  37.9 us
  transfers between devices with their start and end apart: 41, of which 14 were waited for; matrix products, arithmetic and copies ran while one was open for 2% of the time, Pallas kernels for 35%

profile of v1, /device:TPU:0, one launch (start us, length us, event | category | flops | bytes accessed | tf_op | source)
XLA Modules:
  0.0 282.0 jit_solution(1218705357404916270)
XLA Ops:
  7.2 1.0 fusion.22
  9.3 15.0 %scatter_rows.2 = (bf16[2048,256]{1,0:T(8,128)(2,1)S(1)}, bf16[2048,512]{1,0:T(8,128)(2,1)}, bf16[256,8192]{1,0:T(8,128)(2,1)S(1)}) custom-call(s32[1,8192]{1,0:T(1,128)S(1)} %bitcast.27, bf16[256,4,2048]{2,1,0:T(4,128)(2,1)} %refs_1_.2, bf16[512,256]{1,0:T(8,128)(2,1)S(1)} %copy-done.10), custom_call_target="tpu_custom_call" | custom-call | flops 14000000000 | bytes 42000000 | tf_op jit(solution)/shard_map/scatter_rows/pallas_call | solution.py:60
  25.3 2.0 copy-done.49
  28.4 1.2 copy-done.43
  29.6 13.3 %scatter_rows.3 = (bf16[2048,256]{1,0:T(8,128)(2,1)S(1)}, f32[2048,512]{1,0:T(8,128)S(1)}) custom-call(s32[1,8192]{1,0:T(1,128)S(1)} %bitcast.28, bf16[256,8192]{1,0:T(8,128)(2,1)} %copy-done.49, bf16[512,256]{1,0:T(8,128)(2,1)S(1)} %copy-done.11, bf16[2048,256]{1,0:T(8,128)(2,1)S(1)} %copy-done.43), custom_call_target="tpu_custom_call" | custom-call | flops 14000000000 | bytes 42000000 | tf_op jit(solution)/shard_map/scatter_rows/pallas_call | solution.py:60
  43.9 2.5 collective-permute-start.1
  46.4 1.5 collective-permute-start.2
  47.9 10.5 %attn_forward.1 = (bf16[1024,512]{1,0:T(8,128)(2,1)S(1)}, bf16[1024,1536]{1,0:T(8,128)(2,1)S(1)}, bf16[1024,512]{1,0:T(8,128)(2,1)S(1)}, f32[1024,512]{1,0:T(8,128)S(1)}, bf16[1024,512]{1,0:T(8,128)(2,1)S(1)}) custom-call(bf16[128,8,512]{2,1,0:T(8,128)(2,1)S(1)} %copy-done.6, s32[1024,1]{1,0:T(8,128)S(1)} %broadcast_in_dim_reshape.9.refs_1_, ...), custom_call_target="tpu_custom_call" | custom-call | flops 12000000000 | bytes 36000000 | tf_op jit(solution)/shard_map/attn_forward/pallas_call | solution.py:60
  58.5 1.7 copy-done.45
  64.6 14.6 %ffn_forward.1 = (f32[1024,2048]{1,0:T(8,128)S(1)}, bf16[128,2048]{1,0:T(8,128)(2,1)S(1)}, bf16[128,512]{1,0:T(8,128)(2,1)}) custom-call(s32[1024,1]{1,0:T(8,128)S(1)} %broadcast_in_dim_reshape.8.refs_2_.refs_0_.refs_1_, s32[128,1]{1,0:T(8,128)S(1)} %copy.36.refs_1_, f32[1024,512]{1,0:T(8,128)S(1)} %get-tuple-element.82.refs_2_.refs_3_, ...), custom_call_target="tpu_custom_call" | custom-call | flops 12000000000 | bytes 36000000 | tf_op jit(solution)/shard_map/ffn_forward/pallas_call | solution.py:60
  79.2 3.4 %copy-done.41 = f32[1024,2048]{1,0:T(8,128)} copy-done((f32[1024,2048]{1,0:T(8,128)}, f32[1024,2048]{1,0:T(8,128)S(1)}, u32[]{:S(2)}) %copy-start.41) | copy-done | bytes 8388632
  85.6 6.3 %collective-permute-done.3.refs_1_ = bf16[4,128,256]{2,1,0:T(8,128)(2,1)S(1)} collective-permute-done((bf16[4,128,256]{2,1,0:T(8,128)(2,1)}, bf16[4,128,256]{2,1,0:T(8,128)(2,1)S(1)}, u32[]{:S(2)}, u32[]{:S(2)}) %collective-permute-start.3) | collective-permute-done | bytes 262176 | tf_op jit(solution)/shard_map/ppermute | solution.py:83
  92.0 1.1 copy-done.34
  93.1 1.0 copy-done.36
  95.7 1.6 collective-permute-start.5
  97.3 2.6 collective-permute-start.6
  100.1 3.9 %collective-permute-done.5.refs_1_ = bf16[128,512]{1,0:T(8,128)(2,1)} collective-permute-done((bf16[128,512]{1,0:T(8,128)(2,1)}, bf16[128,512]{1,0:T(8,128)(2,1)}, u32[]{:S(2)}, u32[]{:S(2)}) %collective-permute-start.5) | collective-permute-done | bytes 131104 | tf_op jit(solution)/shard_map/ppermute | solution.py:83
  104.0 7.0 %collective-permute-done.6.refs_2_ = bf16[128,512]{1,0:T(8,128)(2,1)} collective-permute-done((bf16[128,512]{1,0:T(8,128)(2,1)}, bf16[128,512]{1,0:T(8,128)(2,1)}, u32[]{:S(2)}, u32[]{:S(2)}) %collective-permute-start.6) | collective-permute-done | bytes 131104 | tf_op jit(solution)/shard_map/ppermute | solution.py:83
  111.9 1.2 exchange.21.refs_3_.refs_0_
  113.2 2.6 tall_weight.1
  115.8 8.6 %ffn_back.1 = (bf16[1024,2048]{1,0:T(8,128)(2,1)S(1)}, f32[1024,512]{1,0:T(8,128)S(1)}, bf16[1024,512]{1,0:T(8,128)(2,1)S(1)}, f32[1,512]{1,0:T(1,128)S(1)}) custom-call(f32[128,512]{1,0:T(8,128)S(1)} %exchange.21.refs_3_.refs_0_, s32[1024,1]{1,0:T(8,128)S(1)} %broadcast_in_dim_reshape.8.refs_2_.refs_0_.refs_1_, f32[1024,2048]{1,0:T(8,128)} %copy-done.41, ...), custom_call_target="tpu_custom_call" | custom-call | flops 15000000512 | bytes 45000000 | tf_op jit(solution)/shard_map/ffn_back/pallas_call | solution.py:60
  124.5 4.4 %wide_weight.1 = (f32[16,64,512]{2,1,0:T(8,128)S(1)}, bf16[16,64,512]{2,1,0:T(8,128)(2,1)S(1)}) custom-call(s32[32]{0:T(128)S(1)} %iota_xor_fusion.refs_0_, bf16[1024,512]{1,0:T(8,128)(2,1)S(1)} %copy-done.51, bf16[1024,2048]{1,0:T(8,128)(2,1)S(1)} %get-tuple-element.102.refs_2_, f32[1,512]{1,0:T(1,128)S(1)} %get-tuple-element.103.refs_3_), custom_call_target="tpu_custom_call" | custom-call | flops 8000000000 | bytes 24000000 | tf_op jit(solution)/shard_map/wide_weight/pallas_call | solution.py:60
  129.5 6.3 %heads_back.1.refs_4_.refs_2_.refs_5_ = bf16[1024,1536]{1,0:T(8,128)(2,1)S(1)} custom-call(s32[1024,1]{1,0:T(8,128)S(1)} %broadcast_in_dim_reshape.8.refs_2_.refs_0_.refs_1_, bf16[512,512]{1,0:T(8,128)(2,1)S(1)} %copy-done.9, bf16[1024,1536]{1,0:T(8,128)(2,1)S(1)} %copy-done.46, bf16[1024,512]{1,0:T(8,128)(2,1)S(1)} %get-tuple-element.101.refs_3_.refs_4_, ...), custom_call_target="tpu_custom_call" | custom-call | flops 12999999488 | bytes 39000000 | tf_op jit(solution)/shard_map/heads_back/pallas_call | solution.py:60
  136.2 1.6 collective-permute-start.11
  138.8 4.3 %two_weights.1 = (f32[16,64,512]{2,1,0:T(8,128)S(1)}, bf16[16,64,512]{2,1,0:T(8,128)(2,1)S(1)}) custom-call(s32[32]{0:T(128)S(1)} %iota_xor_fusion.refs_0_, bf16[1024,512]{1,0:T(8,128)(2,1)S(1)} %copy-done.30, bf16[1024,1536]{1,0:T(8,128)(2,1)S(1)} %heads_back.1.refs_4_.refs_2_.refs_5_, bf16[1024,512]{1,0:T(8,128)(2,1)S(1)} %copy-done.48, ...), custom_call_target="tpu_custom_call" | custom-call | flops 8000000000 | bytes 24000000 | tf_op jit(solution)/shard_map/two_weights/pallas_call | solution.py:60
  143.2 8.1 %collective-permute-done.11.refs_1_ = bf16[2,4,64,512]{3,2,1,0:T(8,128)(2,1)S(1)} collective-permute-done((bf16[2,4,64,512]{3,2,1,0:T(8,128)(2,1)S(1)}, bf16[2,4,64,512]{3,2,1,0:T(8,128)(2,1)S(1)}, u32[]{:S(2)}, u32[]{:S(2)}) %collective-permute-start.11) | collective-permute-done | bytes 524320 | tf_op jit(solution)/shard_map/ppermute | solution.py:83
  153.1 1.4 collective-permute-start.13
  155.1 6.7 %attn_back.1 = (f32[128,8,512]{2,1,0:T(8,128)}, f32[1,512]{1,0:T(1,128)S(1)}, f32[16,512]{1,0:T(8,128)S(1)}) custom-call(bf16[128,8,512]{2,1,0:T(8,128)(2,1)S(1)} %copy-done.7, s32[1024,1]{1,0:T(8,128)S(1)} %broadcast_in_dim_reshape.9.refs_1_, f32[16,512]{1,0:T(8,128)S(1)} %copy-done.14, f32[1,512]{1,0:T(1,128)S(1)} %bitcast.39, ...), custom_call_target="tpu_custom_call" | custom-call | flops 8999999488 | bytes 27000000 | tf_op jit(solution)/shard_map/attn_back/pallas_call | solution.py:60
  162.6 1.0 copy-done.26
  163.6 1.0 copy-done.28
  164.7 1.9 exchange.24
  166.6 1.9 collective-permute-start.16
  168.4 2.0 collective-permute-start.17
  172.2 1.3 collective-permute-start.15
  173.5 2.2 copy-done
  175.7 1.2 copy-done.24
  176.9 1.2 copy-done.32
  178.2 1.2 copy-done.44
  179.4 4.6 %table_and_grad.1 = (bf16[256,4096]{1,0:T(8,128)(2,1)S(1)}, f32[512,256]{1,0:T(8,128)S(1)}) custom-call(s32[32]{0:T(128)S(1)} %broadcast_xor_fusion.refs_0_, bf16[4096,512]{1,0:T(8,128)(2,1)S(1)} %copy-done, bf16[512,256]{1,0:T(8,128)(2,1)S(1)} %copy-done.11, bf16[2048,256]{1,0:T(8,128)(2,1)S(1)} %copy-done.24, bf16[2048,256]{1,0:T(8,128)(2,1)S(1)} %copy-done.44, ...), custom_call_target="tpu_custom_call" | custom-call | flops 7000000000 | bytes 21000000 | tf_op jit(solution)/shard_map/table_and_grad/pallas_call | solution.py:60
  185.0 3.1 %collective-permute-start.21 = (bf16[128,512]{1,0:T(8,128)(2,1)S(1)}, bf16[128,512]{1,0:T(8,128)(2,1)S(1)}, u32[]{:S(2)}, u32[]{:S(2)}) collective-permute-start(bf16[128,512]{1,0:T(8,128)(2,1)S(1)} %exchange.26.refs_2_.refs_0_), channel_id=1, source_target_pairs={{0,16},{2,18},{4,20},{6,22},{8,24},{10,26},{12,28},{14,30},{16,0},... | collective-permute-start | bytes 393224 | tf_op jit(solution)/shard_map/ppermute | solution.py:83
  189.5 10.6 %lookup.2.refs_4_.refs_3_ = bf16[256,4,2048]{2,1,0:T(4,128)(2,1)} custom-call(s32[4,2048]{1,0:T(4,128)S(1)} %fusion.2.refs_0_, bf16[256,4096]{1,0:T(8,128)(2,1)S(1)} %get-tuple-element.122.refs_1_, f32[4,64,512]{2,1,0:T(8,128)S(1)} %get-tuple-element.128.refs_2_.refs_0_), custom_call_target="tpu_custom_call" | custom-call | flops 12999999488 | bytes 39000000 | tf_op jit(solution)/shard_map/lookup/pallas_call | solution.py:60
  200.1 2.2 copy-done.17
  202.4 1.4 collective-permute-start.26
  204.5 10.6 %lookup.3.refs_4_ = bf16[256,4,2048]{2,1,0:T(4,128)(2,1)} custom-call(s32[4,2048]{1,0:T(4,128)S(1)} %fusion.2.refs_0_, bf16[256,4096]{1,0:T(8,128)(2,1)S(1)} %get-tuple-element.122.refs_1_, f32[64,512]{1,0:T(8,128)S(1)} %get-tuple-element.130.refs_2_.refs_0_, bf16[256,4,2048]{2,1,0:T(4,128)(2,1)} %lookup.2.refs_4_.refs_3_), custom_call_target="tpu_custom_call", output_to_operand_aliasing={{}: (3, {})} | custom-call | flops 12999999488 | bytes 39000000 | tf_op jit(solution)/shard_map/lookup/pallas_call | solution.py:60
  215.2 2.2 copy-done.18
  217.4 1.4 collective-permute-start.31
  219.8 3.5 %collective-permute-start.24 = (bf16[64,512]{1,0:T(8,128)(2,1)S(1)}, bf16[64,512]{1,0:T(8,128)(2,1)S(1)}, u32[]{:S(2)}, u32[]{:S(2)}) collective-permute-start(bf16[64,512]{1,0:T(8,128)(2,1)S(1)} %get-tuple-element.134), channel_id=1, source_target_pairs={{0,16},{2,18},{4,20},{6,22},{8,24},{10,26},{12,28},{14,30},{16,0},... | collective-permute-start | bytes 196616 | tf_op jit(solution)/shard_map/ppermute | solution.py:83
  224.5 1.3 collective-permute-done.24.refs_2_
  225.8 4.4 %collective-permute-done.25.refs_3_ = bf16[64,512]{1,0:T(8,128)(2,1)S(1)} collective-permute-done((bf16[64,512]{1,0:T(8,128)(2,1)S(1)}, bf16[64,512]{1,0:T(8,128)(2,1)S(1)}, u32[]{:S(2)}, u32[]{:S(2)}) %collective-permute-start.25) | collective-permute-done | bytes 65568 | tf_op jit(solution)/shard_map/ppermute | solution.py:83
  230.3 1.7 collective-permute-start.29
  232.0 2.7 collective-permute-start.30
  235.5 2.6 collective-permute-done.30.refs_3_
  238.1 1.6 collective-permute-start.33
  239.6 4.9 %collective-permute-done.33.refs_1_ = bf16[4,64,512]{2,1,0:T(8,128)(2,1)S(1)} collective-permute-done((bf16[4,64,512]{2,1,0:T(8,128)(2,1)S(1)}, bf16[4,64,512]{2,1,0:T(8,128)(2,1)S(1)}, u32[]{:S(2)}, u32[]{:S(2)}) %collective-permute-start.33) | collective-permute-done | bytes 262176 | tf_op jit(solution)/shard_map/ppermute | solution.py:83
  244.6 1.3 collective-permute-start.34
  246.4 1.5 reduce_sum.9
  247.9 6.3 %collective-permute-done.34.refs_1_ = bf16[2,4,64,512]{3,2,1,0:T(8,128)(2,1)} collective-permute-done((bf16[2,4,64,512]{3,2,1,0:T(8,128)(2,1)S(1)}, bf16[2,4,64,512]{3,2,1,0:T(8,128)(2,1)}, u32[]{:S(2)}, u32[]{:S(2)}) %collective-permute-start.34) | collective-permute-done | bytes 524320 | tf_op jit(solution)/shard_map/ppermute | solution.py:83
  254.2 1.1 exchange.35.refs_3_
  256.6 1.9 add.92
  258.5 4.4 %unpack.2.refs_3_ = f32[2048,512]{1,0:T(8,128)} custom-call(s32[32]{0:T(128)S(1)} %iota_xor_fusion.refs_0_, bf16[16,64,512]{2,1,0:T(8,128)(2,1)S(1)} %bitcast.31, bf16[16,64,512]{2,1,0:T(8,128)(2,1)} %bitcast.19.refs_2_, bf16[2,2,4,64,512]{4,3,2,1,0:T(8,128)(2,1)S(1)} %exchange.35.refs_3_), custom_call_target="tpu_custom_call" | custom-call | flops 5000000000 | bytes 15000000 | tf_op jit(solution)/shard_map/unpack/pallas_call | solution.py:60
  262.9 2.2 copy-done.19
  265.1 4.4 %unpack.3.refs_3_ = f32[512,2048]{1,0:T(8,128)} custom-call(s32[32]{0:T(128)S(1)} %iota_xor_fusion.refs_0_, bf16[16,64,512]{2,1,0:T(8,128)(2,1)S(1)} %bitcast.30, bf16[16,64,512]{2,1,0:T(8,128)(2,1)} %bitcast.17.refs_2_, f32[2048,512]{1,0:T(8,128)S(1)} %copy-done.19), custom_call_target="tpu_custom_call" | custom-call | flops 5000000000 | bytes 15000000 | tf_op jit(solution)/shard_map/unpack/pallas_call | solution.py:60
  269.5 2.2 copy-done.20
  271.7 3.5 %unpack_two.1 = (f32[512,1536]{1,0:T(8,128)}, f32[512,512]{1,0:T(8,128)}) custom-call(s32[32]{0:T(128)S(1)} %iota_xor_fusion.refs_0_, bf16[16,64,512]{2,1,0:T(8,128)(2,1)S(1)} %bitcast.32, bf16[16,64,512]{2,1,0:T(8,128)(2,1)S(1)} %bitcast.34, f32[512,2048]{1,0:T(8,128)S(1)} %copy-done.20), custom_call_target="tpu_custom_call" | custom-call | flops 5000000000 | bytes 15000000 | tf_op jit(solution)/shard_map/unpack_two/pallas_call | solution.py:60
  (189 shorter events, 29.3 us)
Async XLA Ops:
  7.2 166.3 %all-gather.5.cloned.1.call-start = ((), (), s32[]{:S(2)}) async-start(), calls=%async_computation | async-start | bytes 4325376 | tf_op jit(solution)/shard_map/all_gather | solution.py:1048
  9.3 18.5 %copy-start.56 = (s32[128]{0:T(128)S(1)}, s32[128]{0:T(128)}, u32[]{:S(2)}) copy-start(s32[128]{0:T(128)} %param.15) | copy-start | bytes 1540
  9.3 18.7 %copy-start.57 = (s32[128]{0:T(128)S(1)}, s32[128]{0:T(128)}, u32[]{:S(2)}) copy-start(s32[128]{0:T(128)} %param.16) | copy-start | bytes 1540
  9.3 19.1 %copy-start.11 = (bf16[512,256]{1,0:T(8,128)(2,1)S(1)}, bf16[512,256]{1,0:T(8,128)(2,1)}, u32[]{:S(2)}) copy-start(bf16[512,256]{1,0:T(8,128)(2,1)} %refs_2_.7) | copy-start | bytes 786436
  27.3 15.6 %collective-permute-start = (bf16[2,2,4,128,512]{4,3,2,1,0:T(8,128)(2,1)}, bf16[2,2,4,128,512]{4,3,2,1,0:T(8,128)(2,1)S(1)}, u32[]{:S(2)}, u32[]{:S(2)}) collective-permute-start(bf16[2,2,4,128,512]{4,3,2,1,0:T(8,128)(2,1)} %bitcast.4), channel_id=1, source_target_pairs={{0,1},{1,0},{2,3},{3,2},{4,5},{5,4},{6,7},{7,6},{8,9},{9,8},{10,11... | collective-permute-start | bytes 6291464 | tf_op jit(solution)/shard_map/ppermute | solution.py:83
  42.9 5.0 %copy-start.4 = (bf16[512,1536]{1,0:T(8,128)(2,1)S(1)}, bf16[512,1536]{1,0:T(8,128)(2,1)}, u32[]{:S(2)}) copy-start(bf16[512,1536]{1,0:T(8,128)(2,1)} %refs_4_.3) | copy-start | bytes 4718596
  42.9 5.0 %copy-start.6 = (bf16[128,8,512]{2,1,0:T(8,128)(2,1)S(1)}, bf16[128,8,512]{2,1,0:T(8,128)(2,1)}, u32[]{:S(2)}) copy-start(bf16[128,8,512]{2,1,0:T(8,128)(2,1)} %refs_0_.3) | copy-start | bytes 3145732
  42.9 5.0 %copy-start.8 = (bf16[512,512]{1,0:T(8,128)(2,1)S(1)}, bf16[512,512]{1,0:T(8,128)(2,1)}, u32[]{:S(2)}) copy-start(bf16[512,512]{1,0:T(8,128)(2,1)} %refs_1_.3) | copy-start | bytes 1572868
  42.9 5.0 %copy-start.14 = (f32[16,512]{1,0:T(8,128)S(1)}, f32[16,512]{1,0:T(8,128)}, u32[]{:S(2)}) copy-start(f32[16,512]{1,0:T(8,128)} %refs_2_.6) | copy-start | bytes 98308
  43.0 5.0 %copy-start.15 = (f32[512]{0:T(512)S(1)}, f32[512]{0:T(512)}, u32[]{:S(2)}) copy-start(f32[512]{0:T(512)} %param.19) | copy-start | bytes 6148
  43.0 4.9 %copy-start.16 = (f32[512]{0:T(512)S(1)}, f32[512]{0:T(512)}, u32[]{:S(2)}) copy-start(f32[512]{0:T(512)} %param.18) | copy-start | bytes 6148
  43.9 16.2 %collective-permute-start.1 = (bf16[2,4,128,256]{3,2,1,0:T(8,128)(2,1)S(1)}, bf16[2,4,128,256]{3,2,1,0:T(8,128)(2,1)S(1)}, u32[]{:S(2)}, u32[]{:S(2)}) collective-permute-start(bf16[2,4,128,256]{3,2,1,0:T(8,128)(2,1)S(1)} %get-tuple-element.84), channel_id=1, source_target_pairs={{0,2},{2,0},{4,6},{6,4},{8,10},{10,8},{12,14},{14,12},{16,18},{18,... | collective-permute-start | bytes 1572872 | tf_op jit(solution)/shard_map/ppermute | solution.py:83
  46.4 14.1 %collective-permute-start.2 = (bf16[2,4,128,256]{3,2,1,0:T(8,128)(2,1)S(1)}, bf16[2,4,128,256]{3,2,1,0:T(8,128)(2,1)S(1)}, u32[]{:S(2)}, u32[]{:S(2)}) collective-permute-start(bf16[2,4,128,256]{3,2,1,0:T(8,128)(2,1)S(1)} %get-tuple-element.86), channel_id=1, source_target_pairs={{0,4},{2,6},{4,0},{6,2},{8,12},{10,14},{12,8},{14,10},{16,20},{18,... | collective-permute-start | bytes 1572872 | tf_op jit(solution)/shard_map/ppermute | solution.py:83
  60.1 3.5 %copy-start.52 = (f32[1024,512]{1,0:T(8,128)}, f32[1024,512]{1,0:T(8,128)S(1)}, u32[]{:S(2)}) copy-start(f32[1024,512]{1,0:T(8,128)S(1)} %get-tuple-element.82.refs_2_.refs_3_) | copy-start | bytes 6291460
  60.4 4.2 %copy-start.2 = (bf16[2048,512]{1,0:T(8,128)(2,1)S(1)}, bf16[2048,512]{1,0:T(8,128)(2,1)}, u32[]{:S(2)}) copy-start(bf16[2048,512]{1,0:T(8,128)(2,1)} %refs_6_.3) | copy-start | bytes 6291460
  63.7 15.5 %copy-start.33 = (f32[4,128,256]{2,1,0:T(8,128)}, f32[4,128,256]{2,1,0:T(8,128)S(1)}, u32[]{:S(2)}) copy-start(f32[4,128,256]{2,1,0:T(8,128)S(1)} %get-tuple-element.88.refs_6_.refs_0_) | copy-start | bytes 1572868
  83.4 163.0 %all-gather.7.cloned.1.call-start = ((), (), s32[]{:S(2)}) async-start(), calls=%async_computation.1 | async-start | bytes 1622016 | tf_op jit(solution)/shard_map/all_gather | solution.py:1072
  83.4 8.5 %collective-permute-start.3 = (bf16[4,128,256]{2,1,0:T(8,128)(2,1)}, bf16[4,128,256]{2,1,0:T(8,128)(2,1)S(1)}, u32[]{:S(2)}, u32[]{:S(2)}) collective-permute-start(bf16[4,128,256]{2,1,0:T(8,128)(2,1)} %copy-done.13), channel_id=1, source_target_pairs={{0,4},{2,6},{4,0},{6,2},{8,12},{10,14},{12,8},{14,10},{16,20},{18,... | collective-permute-start | bytes 786440 | tf_op jit(solution)/shard_map/ppermute | solution.py:83
  83.9 8.1 %collective-permute-start.4 = (bf16[4,128,256]{2,1,0:T(8,128)(2,1)}, bf16[4,128,256]{2,1,0:T(8,128)(2,1)S(1)}, u32[]{:S(2)}, u32[]{:S(2)}) collective-permute-start(bf16[4,128,256]{2,1,0:T(8,128)(2,1)} %copy-done.12), channel_id=1, source_target_pairs={{0,2},{2,0},{4,6},{6,4},{8,10},{10,8},{12,14},{14,12},{16,18},{18,... | collective-permute-start | bytes 786440 | tf_op jit(solution)/shard_map/ppermute | solution.py:83
  94.1 5.9 %copy-start.58 = (s32[32]{0:T(128)S(1)}, s32[32]{0:T(128)}, u32[]{:S(2)}) copy-start(s32[32]{0:T(128)} %constant.127.clone) | copy-start | bytes 388
  95.7 8.3 %collective-permute-start.5 = (bf16[128,512]{1,0:T(8,128)(2,1)}, bf16[128,512]{1,0:T(8,128)(2,1)}, u32[]{:S(2)}, u32[]{:S(2)}) collective-permute-start(bf16[128,512]{1,0:T(8,128)(2,1)} %get-tuple-element.95), channel_id=1, source_target_pairs={{0,8},{2,10},{4,12},{6,14},{8,0},{10,2},{12,4},{14,6},{16,24},{18,... | collective-permute-start | bytes 393224 | tf_op jit(solution)/shard_map/ppermute | solution.py:83
  97.3 13.7 %collective-permute-start.6 = (bf16[128,512]{1,0:T(8,128)(2,1)}, bf16[128,512]{1,0:T(8,128)(2,1)}, u32[]{:S(2)}, u32[]{:S(2)}) collective-permute-start(bf16[128,512]{1,0:T(8,128)(2,1)} %get-tuple-element.96), channel_id=1, source_target_pairs={{0,16},{2,18},{4,20},{6,22},{8,24},{10,26},{12,28},{14,30},{16,0},... | collective-permute-start | bytes 393224 | tf_op jit(solution)/shard_map/ppermute | solution.py:83
  99.8 11.1 %collective-permute-start.7 = (bf16[128,512]{1,0:T(8,128)(2,1)}, bf16[128,512]{1,0:T(8,128)(2,1)}, u32[]{:S(2)}, u32[]{:S(2)}) collective-permute-start(bf16[128,512]{1,0:T(8,128)(2,1)} %get-tuple-element.97), channel_id=1, source_target_pairs={{0,24},{2,26},{4,28},{6,30},{8,16},{10,18},{12,20},{14,22},{16,8},... | collective-permute-start | bytes 393224 | tf_op jit(solution)/shard_map/ppermute | solution.py:83
  115.8 8.6 %copy-start.51 = (bf16[1024,512]{1,0:T(8,128)(2,1)S(1)}, bf16[1024,512]{1,0:T(8,128)(2,1)}, u32[]{:S(2)}) copy-start(bf16[1024,512]{1,0:T(8,128)(2,1)} %copy-done.50) | copy-start | bytes 3145732
  124.5 5.0 %copy-start.9 = (bf16[512,512]{1,0:T(8,128)(2,1)S(1)}, bf16[512,512]{1,0:T(8,128)(2,1)}, u32[]{:S(2)}) copy-start(bf16[512,512]{1,0:T(8,128)(2,1)} %refs_1_.3) | copy-start | bytes 1572868
  124.5 5.0 %copy-start.46 = (bf16[1024,1536]{1,0:T(8,128)(2,1)S(1)}, bf16[1024,1536]{1,0:T(8,128)(2,1)}, u32[]{:S(2)}) copy-start(bf16[1024,1536]{1,0:T(8,128)(2,1)} %copy-done.45) | copy-start | bytes 9437188
  128.9 6.9 %collective-permute-start.9 = (bf16[2,2,4,64,512]{4,3,2,1,0:T(8,128)(2,1)S(1)}, bf16[2,2,4,64,512]{4,3,2,1,0:T(8,128)(2,1)S(1)}, u32[]{:S(2)}, u32[]{:S(2)}) collective-permute-start(bf16[2,2,4,64,512]{4,3,2,1,0:T(8,128)(2,1)S(1)} %bitcast.35), channel_id=1, source_target_pairs={{0,1},{1,0},{2,3},{3,2},{4,5},{5,4},{6,7},{7,6},{8,9},{9,8},{10,11... | collective-permute-start | bytes 3145736 | tf_op jit(solution)/shard_map/ppermute | solution.py:83
  129.0 6.8 %collective-permute-start.8 = (bf16[2,2,4,64,512]{4,3,2,1,0:T(8,128)(2,1)S(1)}, bf16[2,2,4,64,512]{4,3,2,1,0:T(8,128)(2,1)S(1)}, u32[]{:S(2)}, u32[]{:S(2)}) collective-permute-start(bf16[2,2,4,64,512]{4,3,2,1,0:T(8,128)(2,1)S(1)} %bitcast.33), channel_id=1, source_target_pairs={{0,1},{1,0},{2,3},{3,2},{4,5},{5,4},{6,7},{7,6},{8,9},{9,8},{10,11... | collective-permute-start | bytes 3145736 | tf_op jit(solution)/shard_map/ppermute | solution.py:83
  136.2 15.1 %collective-permute-start.11 = (bf16[2,4,64,512]{3,2,1,0:T(8,128)(2,1)S(1)}, bf16[2,4,64,512]{3,2,1,0:T(8,128)(2,1)S(1)}, u32[]{:S(2)}, u32[]{:S(2)}) collective-permute-start(bf16[2,4,64,512]{3,2,1,0:T(8,128)(2,1)S(1)} %get-tuple-element.111), channel_id=1, source_target_pairs={{0,2},{2,0},{4,6},{6,4},{8,10},{10,8},{12,14},{14,12},{16,18},{18,... | collective-permute-start | bytes 1572872 | tf_op jit(solution)/shard_map/ppermute | solution.py:83
  137.8 13.6 %collective-permute-start.12 = (bf16[2,4,64,512]{3,2,1,0:T(8,128)(2,1)S(1)}, bf16[2,4,64,512]{3,2,1,0:T(8,128)(2,1)S(1)}, u32[]{:S(2)}, u32[]{:S(2)}) collective-permute-start(bf16[2,4,64,512]{3,2,1,0:T(8,128)(2,1)S(1)} %get-tuple-element.113), channel_id=1, source_target_pairs={{0,4},{2,6},{4,0},{6,2},{8,12},{10,14},{12,8},{14,10},{16,20},{18,... | collective-permute-start | bytes 1572872 | tf_op jit(solution)/shard_map/ppermute | solution.py:83
  143.1 9.2 %copy-start.21 = (f32[16,64,512]{2,1,0:T(8,128)}, f32[16,64,512]{2,1,0:T(8,128)S(1)}, u32[]{:S(2)}) copy-start(f32[16,64,512]{2,1,0:T(8,128)S(1)} %get-tuple-element.109.refs_4_) | copy-start | bytes 6291460
  143.1 27.8 %collective-permute-start.10 = (bf16[2,2,4,64,512]{4,3,2,1,0:T(8,128)(2,1)S(1)}, bf16[2,2,4,64,512]{4,3,2,1,0:T(8,128)(2,1)S(1)}, u32[]{:S(2)}, u32[]{:S(2)}) collective-permute-start(bf16[2,2,4,64,512]{4,3,2,1,0:T(8,128)(2,1)S(1)} %bitcast.29), channel_id=1, source_target_pairs={{0,1},{1,0},{2,3},{3,2},{4,5},{5,4},{6,7},{7,6},{8,9},{9,8},{10,11... | collective-permute-start | bytes 3145736 | tf_op jit(solution)/shard_map/ppermute | solution.py:83
  151.4 3.7 %copy-start.5 = (bf16[512,1536]{1,0:T(8,128)(2,1)S(1)}, bf16[512,1536]{1,0:T(8,128)(2,1)}, u32[]{:S(2)}) copy-start(bf16[512,1536]{1,0:T(8,128)(2,1)} %refs_4_.3) | copy-start | bytes 4718596
  151.4 3.7 %copy-start.7 = (bf16[128,8,512]{2,1,0:T(8,128)(2,1)S(1)}, bf16[128,8,512]{2,1,0:T(8,128)(2,1)}, u32[]{:S(2)}) copy-start(bf16[128,8,512]{2,1,0:T(8,128)(2,1)} %refs_0_.3) | copy-start | bytes 3145732
  153.1 8.8 %copy-start.25 = (f32[4,64,512]{2,1,0:T(8,128)}, f32[4,64,512]{2,1,0:T(8,128)S(1)}, u32[]{:S(2)}) copy-start(f32[4,64,512]{2,1,0:T(8,128)S(1)} %get-tuple-element.114.refs_7_.refs_0_) | copy-start | bytes 1572868
  153.1 9.5 %collective-permute-start.13 = (bf16[4,64,512]{2,1,0:T(8,128)(2,1)S(1)}, bf16[4,64,512]{2,1,0:T(8,128)(2,1)S(1)}, u32[]{:S(2)}, u32[]{:S(2)}) collective-permute-start(bf16[4,64,512]{2,1,0:T(8,128)(2,1)S(1)} %get-tuple-element.115), channel_id=1, source_target_pairs={{0,4},{2,6},{4,0},{6,2},{8,12},{10,14},{12,8},{14,10},{16,20},{18,... | collective-permute-start | bytes 786440 | tf_op jit(solution)/shard_map/ppermute | solution.py:83
  154.5 8.1 %collective-permute-start.14 = (bf16[4,64,512]{2,1,0:T(8,128)(2,1)}, bf16[4,64,512]{2,1,0:T(8,128)(2,1)}, u32[]{:S(2)}, u32[]{:S(2)}) collective-permute-start(bf16[4,64,512]{2,1,0:T(8,128)(2,1)} %get-tuple-element.117), channel_id=1, source_target_pairs={{0,2},{2,0},{4,6},{6,4},{8,10},{10,8},{12,14},{14,12},{16,18},{18,... | collective-permute-start | bytes 786440 | tf_op jit(solution)/shard_map/ppermute | solution.py:83
  164.7 6.3 %copy-start.22 = (f32[16,64,512]{2,1,0:T(8,128)S(1)}, f32[16,64,512]{2,1,0:T(8,128)}, u32[]{:S(2)}) copy-start(f32[16,64,512]{2,1,0:T(8,128)} %copy-done.21) | copy-start | bytes 6291460
  166.6 4.6 %copy-start.37 = (f32[128,512]{1,0:T(8,128)}, f32[128,512]{1,0:T(8,128)S(1)}, u32[]{:S(2)}) copy-start(f32[128,512]{1,0:T(8,128)S(1)} %get-tuple-element.120.refs_2_.refs_0_) | copy-start | bytes 786436
  166.6 17.5 %collective-permute-start.16 = (bf16[128,512]{1,0:T(8,128)(2,1)}, bf16[128,512]{1,0:T(8,128)(2,1)S(1)}, u32[]{:S(2)}, u32[]{:S(2)}) collective-permute-start(bf16[128,512]{1,0:T(8,128)(2,1)} %get-tuple-element.124), channel_id=1, source_target_pairs={{0,8},{2,10},{4,12},{6,14},{8,0},{10,2},{12,4},{14,6},{16,24},{18,... | collective-permute-start | bytes 393224 | tf_op jit(solution)/shard_map/ppermute | solution.py:83
  168.4 15.6 %collective-permute-start.17 = (bf16[128,512]{1,0:T(8,128)(2,1)}, bf16[128,512]{1,0:T(8,128)(2,1)S(1)}, u32[]{:S(2)}, u32[]{:S(2)}) collective-permute-start(bf16[128,512]{1,0:T(8,128)(2,1)} %get-tuple-element.125), channel_id=1, source_target_pairs={{0,16},{2,18},{4,20},{6,22},{8,24},{10,26},{12,28},{14,30},{16,0},... | collective-permute-start | bytes 393224 | tf_op jit(solution)/shard_map/ppermute | solution.py:83
  170.4 13.7 %collective-permute-start.18 = (bf16[128,512]{1,0:T(8,128)(2,1)}, bf16[128,512]{1,0:T(8,128)(2,1)S(1)}, u32[]{:S(2)}, u32[]{:S(2)}) collective-permute-start(bf16[128,512]{1,0:T(8,128)(2,1)} %get-tuple-element.126), channel_id=1, source_target_pairs={{0,24},{2,26},{4,28},{6,30},{8,16},{10,18},{12,20},{14,22},{16,8},... | collective-permute-start | bytes 393224 | tf_op jit(solution)/shard_map/ppermute | solution.py:83
  172.2 16.4 %collective-permute-start.15 = (bf16[2,4,64,512]{3,2,1,0:T(8,128)(2,1)S(1)}, bf16[2,4,64,512]{3,2,1,0:T(8,128)(2,1)S(1)}, u32[]{:S(2)}, u32[]{:S(2)}) collective-permute-start(bf16[2,4,64,512]{3,2,1,0:T(8,128)(2,1)S(1)} %get-tuple-element.123), channel_id=1, source_target_pairs={{0,2},{2,0},{4,6},{6,4},{8,10},{10,8},{12,14},{14,12},{16,18},{18,... | collective-permute-start | bytes 1572872 | tf_op jit(solution)/shard_map/ppermute | solution.py:83
  179.4 4.7 %copy-start.38 = (f32[128,512]{1,0:T(8,128)S(1)}, f32[128,512]{1,0:T(8,128)}, u32[]{:S(2)}) copy-start(f32[128,512]{1,0:T(8,128)} %copy-done.37) | copy-start | bytes 786436
  184.2 16.0 %collective-permute-start.20 = (bf16[128,512]{1,0:T(8,128)(2,1)S(1)}, bf16[128,512]{1,0:T(8,128)(2,1)S(1)}, u32[]{:S(2)}, u32[]{:S(2)}) collective-permute-start(bf16[128,512]{1,0:T(8,128)(2,1)S(1)} %exchange.26.refs_2_.refs_0_), channel_id=1, source_target_pairs={{0,8},{2,10},{4,12},{6,14},{8,0},{10,2},{12,4},{14,6},{16,24},{18,... | collective-permute-start | bytes 393224 | tf_op jit(solution)/shard_map/ppermute | solution.py:83
  185.0 15.1 %collective-permute-start.21 = (bf16[128,512]{1,0:T(8,128)(2,1)S(1)}, bf16[128,512]{1,0:T(8,128)(2,1)S(1)}, u32[]{:S(2)}, u32[]{:S(2)}) collective-permute-start(bf16[128,512]{1,0:T(8,128)(2,1)S(1)} %exchange.26.refs_2_.refs_0_), channel_id=1, source_target_pairs={{0,16},{2,18},{4,20},{6,22},{8,24},{10,26},{12,28},{14,30},{16,0},... | collective-permute-start | bytes 393224 | tf_op jit(solution)/shard_map/ppermute | solution.py:83
  188.1 12.0 %collective-permute-start.22 = (bf16[128,512]{1,0:T(8,128)(2,1)S(1)}, bf16[128,512]{1,0:T(8,128)(2,1)S(1)}, u32[]{:S(2)}, u32[]{:S(2)}) collective-permute-start(bf16[128,512]{1,0:T(8,128)(2,1)S(1)} %exchange.26.refs_2_.refs_0_), channel_id=1, source_target_pairs={{0,24},{2,26},{4,28},{6,30},{8,16},{10,18},{12,20},{14,22},{16,8},... | collective-permute-start | bytes 393224 | tf_op jit(solution)/shard_map/ppermute | solution.py:83
  188.7 15.7 %collective-permute-start.19 = (bf16[4,64,512]{2,1,0:T(8,128)(2,1)S(1)}, bf16[4,64,512]{2,1,0:T(8,128)(2,1)S(1)}, u32[]{:S(2)}, u32[]{:S(2)}) collective-permute-start(bf16[4,64,512]{2,1,0:T(8,128)(2,1)S(1)} %get-tuple-element.129), channel_id=1, source_target_pairs={{0,4},{2,6},{4,0},{6,2},{8,12},{10,14},{12,8},{14,10},{16,20},{18,... | collective-permute-start | bytes 786440 | tf_op jit(solution)/shard_map/ppermute | solution.py:83
  202.4 12.8 %collective-permute-start.26 = (bf16[4,64,512]{2,1,0:T(8,128)(2,1)S(1)}, bf16[4,64,512]{2,1,0:T(8,128)(2,1)S(1)}, u32[]{:S(2)}, u32[]{:S(2)}) collective-permute-start(bf16[4,64,512]{2,1,0:T(8,128)(2,1)S(1)} %get-tuple-element.143.refs_0_), channel_id=1, source_target_pairs={{0,4},{2,6},{4,0},{6,2},{8,12},{10,14},{12,8},{14,10},{16,20},{18,... | collective-permute-start | bytes 786440 | tf_op jit(solution)/shard_map/ppermute | solution.py:83
  203.8 11.4 %collective-permute-start.27 = (bf16[4,64,512]{2,1,0:T(8,128)(2,1)S(1)}, bf16[4,64,512]{2,1,0:T(8,128)(2,1)S(1)}, u32[]{:S(2)}, u32[]{:S(2)}) collective-permute-start(bf16[4,64,512]{2,1,0:T(8,128)(2,1)S(1)} %get-tuple-element.142.refs_2_), channel_id=1, source_target_pairs={{0,2},{2,0},{4,6},{6,4},{8,10},{10,8},{12,14},{14,12},{16,18},{18,... | collective-permute-start | bytes 786440 | tf_op jit(solution)/shard_map/ppermute | solution.py:83
  217.4 17.2 %collective-permute-start.31 = (bf16[2,4,64,512]{3,2,1,0:T(8,128)(2,1)S(1)}, bf16[2,4,64,512]{3,2,1,0:T(8,128)(2,1)S(1)}, u32[]{:S(2)}, u32[]{:S(2)}) collective-permute-start(bf16[2,4,64,512]{3,2,1,0:T(8,128)(2,1)S(1)} %get-tuple-element.136.refs_4_.refs_0_), channel_id=1, source_target_pairs={{0,2},{2,0},{4,6},{6,4},{8,10},{10,8},{12,14},{14,12},{16,18},{18,... | collective-permute-start | bytes 1572872 | tf_op jit(solution)/shard_map/ppermute | solution.py:83
  218.8 15.8 %collective-permute-start.32 = (bf16[2,4,64,512]{3,2,1,0:T(8,128)(2,1)S(1)}, bf16[2,4,64,512]{3,2,1,0:T(8,128)(2,1)S(1)}, u32[]{:S(2)}, u32[]{:S(2)}) collective-permute-start(bf16[2,4,64,512]{3,2,1,0:T(8,128)(2,1)S(1)} %get-tuple-element.137.refs_2_), channel_id=1, source_target_pairs={{0,4},{2,6},{4,0},{6,2},{8,12},{10,14},{12,8},{14,10},{16,20},{18,... | collective-permute-start | bytes 1572872 | tf_op jit(solution)/shard_map/ppermute | solution.py:83
  219.6 4.9 %collective-permute-start.23 = (bf16[64,512]{1,0:T(8,128)(2,1)S(1)}, bf16[64,512]{1,0:T(8,128)(2,1)S(1)}, u32[]{:S(2)}, u32[]{:S(2)}) collective-permute-start(bf16[64,512]{1,0:T(8,128)(2,1)S(1)} %get-tuple-element.133), channel_id=1, source_target_pairs={{0,8},{2,10},{4,12},{6,14},{8,0},{10,2},{12,4},{14,6},{16,24},{18,... | collective-permute-start | bytes 196616 | tf_op jit(solution)/shard_map/ppermute | solution.py:83
  219.8 6.0 %collective-permute-start.24 = (bf16[64,512]{1,0:T(8,128)(2,1)S(1)}, bf16[64,512]{1,0:T(8,128)(2,1)S(1)}, u32[]{:S(2)}, u32[]{:S(2)}) collective-permute-start(bf16[64,512]{1,0:T(8,128)(2,1)S(1)} %get-tuple-element.134), channel_id=1, source_target_pairs={{0,16},{2,18},{4,20},{6,22},{8,24},{10,26},{12,28},{14,30},{16,0},... | collective-permute-start | bytes 196616 | tf_op jit(solution)/shard_map/ppermute | solution.py:83
  223.3 6.9 %collective-permute-start.25 = (bf16[64,512]{1,0:T(8,128)(2,1)S(1)}, bf16[64,512]{1,0:T(8,128)(2,1)S(1)}, u32[]{:S(2)}, u32[]{:S(2)}) collective-permute-start(bf16[64,512]{1,0:T(8,128)(2,1)S(1)} %get-tuple-element.135), channel_id=1, source_target_pairs={{0,24},{2,26},{4,28},{6,30},{8,16},{10,18},{12,20},{14,22},{16,8},... | collective-permute-start | bytes 196616 | tf_op jit(solution)/shard_map/ppermute | solution.py:83
  230.2 4.6 %collective-permute-start.28 = (bf16[64,512]{1,0:T(8,128)(2,1)S(1)}, bf16[64,512]{1,0:T(8,128)(2,1)S(1)}, u32[]{:S(2)}, u32[]{:S(2)}) collective-permute-start(bf16[64,512]{1,0:T(8,128)(2,1)S(1)} %exchange.31.refs_4_.refs_0_), channel_id=1, source_target_pairs={{0,8},{2,10},{4,12},{6,14},{8,0},{10,2},{12,4},{14,6},{16,24},{18,... | collective-permute-start | bytes 196616 | tf_op jit(solution)/shard_map/ppermute | solution.py:83
  230.3 5.2 %collective-permute-start.29 = (bf16[64,512]{1,0:T(8,128)(2,1)S(1)}, bf16[64,512]{1,0:T(8,128)(2,1)S(1)}, u32[]{:S(2)}, u32[]{:S(2)}) collective-permute-start(bf16[64,512]{1,0:T(8,128)(2,1)S(1)} %exchange.31.refs_4_.refs_0_), channel_id=1, source_target_pairs={{0,16},{2,18},{4,20},{6,22},{8,24},{10,26},{12,28},{14,30},{16,0},... | collective-permute-start | bytes 196616 | tf_op jit(solution)/shard_map/ppermute | solution.py:83
  232.0 6.1 %collective-permute-start.30 = (bf16[64,512]{1,0:T(8,128)(2,1)S(1)}, bf16[64,512]{1,0:T(8,128)(2,1)S(1)}, u32[]{:S(2)}, u32[]{:S(2)}) collective-permute-start(bf16[64,512]{1,0:T(8,128)(2,1)S(1)} %exchange.31.refs_4_.refs_0_), channel_id=1, source_target_pairs={{0,24},{2,26},{4,28},{6,30},{8,16},{10,18},{12,20},{14,22},{16,8},... | collective-permute-start | bytes 196616 | tf_op jit(solution)/shard_map/ppermute | solution.py:83
  238.1 6.4 %collective-permute-start.33 = (bf16[4,64,512]{2,1,0:T(8,128)(2,1)S(1)}, bf16[4,64,512]{2,1,0:T(8,128)(2,1)S(1)}, u32[]{:S(2)}, u32[]{:S(2)}) collective-permute-start(bf16[4,64,512]{2,1,0:T(8,128)(2,1)S(1)} %exchange.33.refs_0_.refs_2_), channel_id=1, source_target_pairs={{0,4},{2,6},{4,0},{6,2},{8,12},{10,14},{12,8},{14,10},{16,20},{18,... | collective-permute-start | bytes 786440 | tf_op jit(solution)/shard_map/ppermute | solution.py:83
  239.6 18.9 %collective-permute-start.37 = (bf16[2,2,4,64,512]{4,3,2,1,0:T(8,128)(2,1)S(1)}, bf16[2,2,4,64,512]{4,3,2,1,0:T(8,128)(2,1)}, u32[]{:S(2)}, u32[]{:S(2)}) collective-permute-start(bf16[2,2,4,64,512]{4,3,2,1,0:T(8,128)(2,1)S(1)} %get-tuple-element.138.refs_4_), channel_id=1, source_target_pairs={{0,1},{1,0},{2,3},{3,2},{4,5},{5,4},{6,7},{7,6},{8,9},{9,8},{10,11... | collective-permute-start | bytes 3145736 | tf_op jit(solution)/shard_map/ppermute | solution.py:83
  244.6 9.6 %collective-permute-start.34 = (bf16[2,4,64,512]{3,2,1,0:T(8,128)(2,1)S(1)}, bf16[2,4,64,512]{3,2,1,0:T(8,128)(2,1)}, u32[]{:S(2)}, u32[]{:S(2)}) collective-permute-start(bf16[2,4,64,512]{3,2,1,0:T(8,128)(2,1)S(1)} %exchange.34.refs_0_.refs_2_), channel_id=1, source_target_pairs={{0,2},{2,0},{4,6},{6,4},{8,10},{10,8},{12,14},{14,12},{16,18},{18,... | collective-permute-start | bytes 1572872 | tf_op jit(solution)/shard_map/ppermute | solution.py:83
  245.9 17.0 %collective-permute-start.36 = (bf16[2,2,4,64,512]{4,3,2,1,0:T(8,128)(2,1)S(1)}, bf16[2,2,4,64,512]{4,3,2,1,0:T(8,128)(2,1)}, u32[]{:S(2)}, u32[]{:S(2)}) collective-permute-start(bf16[2,2,4,64,512]{4,3,2,1,0:T(8,128)(2,1)S(1)} %get-tuple-element.139), channel_id=1, source_target_pairs={{0,1},{1,0},{2,3},{3,2},{4,5},{5,4},{6,7},{7,6},{8,9},{9,8},{10,11... | collective-permute-start | bytes 3145736 | tf_op jit(solution)/shard_map/ppermute | solution.py:83
  245.9 10.7 %collective-permute-start.38 = (f32[512,256]{1,0:T(8,128)S(1)}, f32[512,256]{1,0:T(8,128)}, u32[]{:S(2)}, u32[]{:S(2)}) collective-permute-start(f32[512,256]{1,0:T(8,128)S(1)} %get-tuple-element.127.refs_4_), channel_id=1, source_target_pairs={{0,1},{1,0},{2,3},{3,2},{4,5},{5,4},{6,7},{7,6},{8,9},{9,8},{10,11... | collective-permute-start | bytes 1572872 | tf_op jit(solution)/shard_map/ppermute | solution.py:83
  255.3 14.2 %collective-permute-start.35 = (bf16[2,2,4,64,512]{4,3,2,1,0:T(8,128)(2,1)S(1)}, bf16[2,2,4,64,512]{4,3,2,1,0:T(8,128)(2,1)S(1)}, u32[]{:S(2)}, u32[]{:S(2)}) collective-permute-start(bf16[2,2,4,64,512]{4,3,2,1,0:T(8,128)(2,1)S(1)} %exchange.35.refs_3_), channel_id=1, source_target_pairs={{0,1},{1,0},{2,3},{3,2},{4,5},{5,4},{6,7},{7,6},{8,9},{9,8},{10,11... | collective-permute-start | bytes 3145736 | tf_op jit(solution)/shard_map/ppermute | solution.py:83
  (36 other events, 57.8 us)
Sparse Core Ops, SparseCore 0:
  83.5 66.0 all-gather.4
  162.7 59.6 all-gather.6

commit v2 on v1

--- a/solution.py
+++ b/solution.py
@@ -46,6 +46,9 @@
     return value.reshape((-1,) + value.shape[-2:])
 
 
+FAR = True
+
+
 class Line:
     def __init__(self):
         self.last = []
@@ -53,27 +56,33 @@
     def run(self, body, name, micros, grid, ins, outs, prefetch=(), alias=None, room=32 * MIB):
         count = len(prefetch) + len(ins)
         extra = self.last + ([] if alias is None else [alias])
+        token = (8, 128)
 
         def wrapped(*refs):
-            body(*refs[:count], *refs[count + len(extra) :])
-
-        results = pl.pallas_call(
+            refs[-1][...] = jnp.zeros(token, F32)
+            body(*refs[:count], *refs[count + len(extra) : -1])
+
+        *results, last = pl.pallas_call(
             wrapped,
             grid_spec=pltpu.PrefetchScalarGridSpec(
                 num_scalar_prefetch=len(prefetch),
                 grid=grid,
                 in_specs=[spec for _, spec in ins] + [pl.BlockSpec(memory_space=pl.ANY)] * len(extra),
-                out_specs=[spec for _, _, spec in outs],
+                out_specs=[spec for _, _, spec, *_ in outs] + [pl.BlockSpec(token, lambda *_: (0, 0))],
             ),
-            out_shape=[jax.ShapeDtypeStruct(shape, dtype) for shape, dtype, _ in outs],
+            out_shape=[
+                pltpu.HBM(shape, dtype) if far else jax.ShapeDtypeStruct(shape, dtype)
+                for shape, dtype, _, *far in outs
+            ]
+            + [jax.ShapeDtypeStruct(token, F32)],
             input_output_aliases={} if alias is None else {count + len(extra) - 1: 0},
             compiler_params=pltpu.CompilerParams(vmem_limit_bytes=room),
             cost_estimate=pl.CostEstimate(
-                flops=int(micros * 1e9), bytes_accessed=int(micros * 3e6), transcendentals=0
+                flops=int(micros * 3e9), bytes_accessed=int(micros * 9e6), transcendentals=0
             ),
             name=name,
         )(*prefetch, *(value for value, _ in ins), *extra)
-        self.last = [min(results, key=lambda value: value.size)]
+        self.last = [last]
         return results
 
 
@@ -121,7 +130,7 @@
     return line.run(
         functools.partial(stage_body, [1 + len(received) for _, received in sums], cuts),
         "exchange",
-        2,
+        0.5,
         (),
         [(value, spec(value.shape)) for value in values],
         [(shape, dtype, spec(shape)) for shape, dtype in shapes],
@@ -191,6 +200,46 @@
     yield
 
 
+def gather_halves(line, value, levels, out):
+    rows, width = value.shape
+    half = width // 2
+    for place, level in reversed(list(enumerate(levels[3:]))):
+        got = [swap(value, level, k) for k in range(1, level[1])]
+        yield
+        parts = [(part, []) for part in [value, *got]]
+        numbers = list(range(level[1]))
+        if place:
+            value = stage(line, parts, [stacked(numbers, value, 0)])[0]
+        else:
+            lead = (level[1],) + value.shape[:-2]
+
+            def source(index, cols):
+                return [(index[0], index[1:], cols, 0, 0)]
+
+            outs = [
+                (lead, rows, half, BF16, functools.partial(source, cols=cols))
+                for cols in (slice(0, half), slice(half, width))
+            ]
+            value_a, value_b = stage(line, parts, outs)
+    got_a, got_b = swap(value_a, levels[2]), swap(value_b, levels[1])
+    yield
+    sums = [(part, []) for part in (value_a, got_a, value_b, got_b)]
+    outs = [stacked([0, 1], value_a, 0), stacked([2, 3], value_b, 0)]
+    value_a, value_b = stage(line, sums, outs)
+    got_a, got_b = swap(value_a, levels[1]), swap(value_b, levels[2])
+    yield
+    sums = [(part, []) for part in (value_a, got_a, value_b, got_b)]
+    lead = (2,) + value_a.shape[:-2]
+
+    def joined(index):
+        left, right = index[0], index[1]
+        return [(left, index[1:], ALL, 0, 0), (2 + right, (left,) + index[2:], ALL, 0, half)]
+
+    value = stage(line, sums, [(lead, rows, width, BF16, joined)])[0]
+    out += [value, swap(value, levels[0])]
+    yield
+
+
 def finish(line, sums, far, rows):
     for level in far:
         outs = [((), rows, PANEL, dtype, lambda index: [(0, (), ALL, 0, 0)]) for dtype in (F32, BF16)]
@@ -212,13 +261,7 @@
     for value in finish(line, sums, far, rows):
         if value is None:
             yield
-    for level in near[:0:-1]:
-        got = [swap(value, level, k) for k in range(1, level[1])]
-        yield
-        numbers = list(range(level[1]))
-        value = stage(line, [(part, []) for part in [value, *got]], [stacked(numbers, value, 0)])[0]
-    out += [value, swap(value, near[0])]
-    yield
+    yield from gather_halves(line, value, near, out)
 
 
 def all_sum_two(line, keep_a, send_a, keep_b, send_b, near, far, out):
@@ -299,7 +342,9 @@
 
 def scatter_some(first, ids_ref, grad, proj_ref, table_ref, pooled_ref):
     rows = table_ref.shape[0]
-    part = nt(selector(ids_ref[...], first + pl.program_id(0) * rows, rows), grad).astype(BF16)
+    base = first + pl.program_id(0) * rows
+    picks = [selector(ids_ref[row : row + 1], base, rows) for row in range(ids_ref.shape[0])]
+    part = nt(jnp.concatenate(picks, axis=1), grad).astype(BF16)
     table_ref[...] = part
     pooled_ref[...] = nt(part, proj_ref[...]).astype(pooled_ref.dtype)
 
@@ -318,7 +363,7 @@
 
 def scatter_rows(line, ids, grad, w_proj, first, count, dtype):
     features = grad.shape[0]
-    tokens = ids.shape[1]
+    tokens = ids.size
     width = w_proj.shape[0]
     rows = min(512, count)
     flat = (features, tokens)
@@ -328,64 +373,68 @@
         "scatter_rows",
         14,
         (count // rows,),
-        [(ids, fixed((1, tokens))), (grad, fixed(grad.shape)), (w_proj, fixed(w_proj.shape))],
-        [
-            ((count, features), BF16, rows_of(rows, features)),
+        [(ids, fixed(ids.shape)), (grad, pl.BlockSpec(memory_space=pltpu.VMEM)), (w_proj, fixed(w_proj.shape))],
+        [
+            ((count, features), BF16, rows_of(rows, features), FAR),
             ((count, width), dtype, rows_of(rows, width)),
         ]
-        + ([(flat, BF16, fixed(flat))] if fresh else []),
+        + ([(flat, BF16, pl.BlockSpec(memory_space=pltpu.VMEM))] if fresh else []),
         room=44 * MIB,
     )
 
 
-def table_body(steps, each, owners_ref, pooled_ref, proj_ref, own_ref, other_ref, table_ref, grad_ref):
+def table_body(steps, own_ref, other_ref, proj_ref, part_own_ref, part_other_ref, table_ref, grad_ref):
     step = pl.program_id(0)
-    slots = own_ref.shape[0] // each
 
     @pl.when(step == 0)
     def _():
         grad_ref[...] = jnp.zeros_like(grad_ref)
 
-    parts = []
-    for j in range(slots):
-        base = pl.multiple_of(owners_ref[step * slots + j] * each, each)
-        parts.append(pooled_ref[pl.ds(base, each)])
-    pooled = jnp.concatenate(parts, axis=0)
-    cols = lax.dot_general(
-        proj_ref[...], pooled, (((0,), (1,)), ((), ())), preferred_element_type=F32
-    )
-    table_ref[...] = cols.astype(BF16)
+    def one(pooled_ref, part_ref):
+        pooled = pooled_ref[...]
+        cols = lax.dot_general(
+            proj_ref[...], pooled, (((0,), (1,)), ((), ())), preferred_element_type=F32
+        )
+        table_ref[...] = cols.astype(BF16)
+        grad_ref[...] += tn(pooled, part_ref[...])
 
     @pl.when(step < steps)
     def _():
-        grad_ref[...] += tn(pooled, own_ref[...])
+        one(own_ref, part_own_ref)
 
     @pl.when(step >= steps)
     def _():
-        grad_ref[...] += tn(pooled, other_ref[...])
-
-
-def table_and_grad(line, owners, pooled, w_proj, part_own, part_other):
-    vocab, width = pooled.shape
+        one(other_ref, part_other_ref)
+
+
+def table_and_grad(line, own, other, w_proj, part_own, part_other):
+    count, width = own.shape
     features = w_proj.shape[1]
-    rows = min(1024, vocab // 2)
-    steps = vocab // 2 // rows
-    return line.run(
-        functools.partial(table_body, steps, vocab // owners.shape[0]),
+    rows = min(1024, count)
+    steps = count // rows
+
+    def first(cols):
+        return pl.BlockSpec((rows, cols), lambda i, *_: (jnp.minimum(i, steps - 1), 0))
+
+    def second(cols):
+        return pl.BlockSpec((rows, cols), lambda i, *_: (jnp.maximum(i - steps, 0), 0))
+
+    return line.run(
+        functools.partial(table_body, steps),
         "table_and_grad",
-        7,
+        5,
         (2 * steps,),
         [
-            (pooled, fixed(pooled.shape)),
+            (own, first(width)),
+            (other, second(width)),
             (w_proj, fixed(w_proj.shape)),
-            (part_own, pl.BlockSpec((rows, features), lambda i, *_: (jnp.minimum(i, steps - 1), 0))),
-            (part_other, pl.BlockSpec((rows, features), lambda i, *_: (jnp.maximum(i - steps, 0), 0))),
-        ],
-        [
-            ((features, vocab), BF16, pl.BlockSpec((features, rows), lambda i, *_: (0, i))),
+            (part_own, first(features)),
+            (part_other, second(features)),
+        ],
+        [
+            ((features, 2 * count), BF16, pl.BlockSpec((features, rows), lambda i, *_: (0, i))),
             ((width, features), F32, fixed((width, features))),
         ],
-        [owners],
     )
 
 
@@ -406,23 +455,24 @@
     out_ref[...] = total.astype(BF16).reshape(out_ref.shape)
 
 
-def lookup(line, ids, tables, half, before=None):
+def lookup(line, ids, tables, part, count, before=None):
     rows, text_len = ids.shape
     features, vocab = tables[0].shape
-    block = math.gcd(text_len // 2, 256)
-    steps = text_len // 2 // block
+    block = math.gcd(text_len // count, 256)
+    steps = text_len // count // block
     return line.run(
         functools.partial(lookup_body, min(vocab, 4096)),
         "lookup",
-        13,
+        6,
         (steps,),
-        [(ids, pl.BlockSpec((rows, block), lambda i, *_: (0, i + half * steps)))]
+        [(ids, pl.BlockSpec((rows, block), lambda i, *_: (0, i + part * steps)))]
         + [(table, fixed(table.shape)) for table in tables],
         [
             (
                 (features, rows, text_len),
                 BF16,
-                pl.BlockSpec((features, rows, block), lambda i, *_: (0, 0, i + half * steps)),
+                pl.BlockSpec((features, rows, block), lambda i, *_: (0, 0, i + part * steps)),
+                FAR,
             )
         ],
         alias=before,
@@ -430,22 +480,24 @@
 
 
 PANEL = 512
-
-
-def store_slots(slots_ref, first, part, keep_ref, send_ref):
-    rows = keep_ref.shape[1]
+EXTRA = 16
+
+
+def store_slots(slots_ref, first, part, keep_ref, send_ref, rows=None, base=0):
+    rows = rows or keep_ref.shape[1]
     half = keep_ref.shape[0]
+    where = slice(base, base + rows)
     for j in range(part.shape[0] // rows):
         slot = slots_ref[first + j]
         piece = part[j * rows : (j + 1) * rows]
 
         @pl.when(slot < half)
         def _():
-            keep_ref[slot] = piece
+            keep_ref[slot, where] = piece
 
         @pl.when(slot >= half)
         def _():
-            send_ref[slot - half] = piece.astype(BF16)
+            send_ref[slot - half, where] = piece.astype(BF16)
 
 
 def weight_body(slots_ref, left_ref, right_ref, keep_ref, send_ref):
@@ -453,17 +505,40 @@
     store_slots(slots_ref, pl.program_id(0) * (part.shape[0] // keep_ref.shape[1]), part, keep_ref, send_ref)
 
 
-def two_weights_body(last, slots_ref, left_ref, right_ref, left2_ref, right2_ref, keep_ref, send_ref):
+def tall_body(steps, slots_ref, first_ref, second_ref, right_ref, keep_ref, send_ref):
     step = pl.program_id(0)
-    each = left_ref.shape[1] // keep_ref.shape[1]
+    each = PANEL // keep_ref.shape[1]
+
+    @pl.when(step < steps)
+    def _():
+        store_slots(slots_ref, step * each, tn(first_ref[...], right_ref[...]), keep_ref, send_ref)
+
+    @pl.when(step >= steps)
+    def _():
+        store_slots(slots_ref, step * each, tn(second_ref[...], right_ref[...]), keep_ref, send_ref)
+
+
+def two_weights_body(
+    last, slots_ref, left_ref, right_ref, left2_ref, right2_ref, small_ref, keep_ref, send_ref
+):
+    step = pl.program_id(0)
+    rows = keep_ref.shape[1] - EXTRA
+    each = left_ref.shape[1] // rows
 
     @pl.when(step < last)
     def _():
-        store_slots(slots_ref, step * each, tn(left_ref[...], right_ref[...]), keep_ref, send_ref)
+        store_slots(slots_ref, step * each, tn(left_ref[...], right_ref[...]), keep_ref, send_ref, rows)
 
     @pl.when(step == last)
     def _():
-        store_slots(slots_ref, step * each, tn(left2_ref[...], right2_ref[...]), keep_ref, send_ref)
+        part = tn(left2_ref[...], right2_ref[...])
+        store_slots(slots_ref, step * each, part, keep_ref, send_ref, rows)
+        top = lax.broadcasted_iota(jnp.int32, (EXTRA, 1), 0) == 0
+        for chunk in range(2 * keep_ref.shape[0]):
+            piece = jnp.zeros((EXTRA, PANEL), F32)
+            if chunk < small_ref.shape[0]:
+                piece = jnp.where(top, small_ref[chunk : chunk + 1], 0.0)
+            store_slots(slots_ref, chunk, piece, keep_ref, send_ref, EXTRA, rows)
 
 
 def slot_outs(count, rows):
@@ -475,15 +550,20 @@
     return pl.BlockSpec((depth, PANEL), lambda i, *_: (0, i))
 
 
-def tall_weight(line, slots, left, right):
-    depth, height = left.shape
-    return line.run(
-        weight_body,
+def tall_weight(line, slots, lefts, right):
+    depth, half = lefts[0].shape
+    steps = half // PANEL
+    return line.run(
+        functools.partial(tall_body, steps),
         "tall_weight",
-        6,
-        (height // PANEL,),
-        [(left, panel_of(depth)), (right, fixed(right.shape))],
-        slot_outs(slots.shape[0], height // slots.shape[0]),
+        3,
+        (2 * steps,),
+        [
+            (lefts[0], pl.BlockSpec((depth, PANEL), lambda i, *_: (0, jnp.minimum(i, steps - 1)))),
+            (lefts[1], pl.BlockSpec((depth, PANEL), lambda i, *_: (0, jnp.maximum(i - steps, 0)))),
+            (right, fixed(right.shape)),
+        ],
+        slot_outs(slots.shape[0], 2 * half // slots.shape[0]),
         [slots],
     )
 
@@ -501,55 +581,69 @@
     )
 
 
-def two_weights(line, slots, left, right, left2, right2):
+def two_weights(line, slots, left, right, left2, right2, small):
     depth, cols = right.shape
     last = cols // PANEL
     return line.run(
         functools.partial(two_weights_body, last),
         "two_weights",
-        8,
+        5,
         (last + 1,),
         [
             (left, fixed(left.shape)),
             (right, pl.BlockSpec((depth, PANEL), lambda i, *_: (0, jnp.minimum(i, last - 1)))),
             (left2, fixed(left2.shape)),
             (right2, fixed(right2.shape)),
-        ],
-        slot_outs(slots.shape[0], (last + 1) * left.shape[1] // slots.shape[0]),
+            (small, fixed(small.shape)),
+        ],
+        slot_outs(slots.shape[0], (last + 1) * left.shape[1] // slots.shape[0] + EXTRA),
         [slots],
     )
 
 
-def load_slots(slots_ref, first, own_ref, other_ref, out_ref):
-    half, rows, _ = own_ref.shape
+def load_slots(slots_ref, first, own_ref, other_ref, out_ref, rows):
+    half = own_ref.shape[0]
     for j in range(out_ref.shape[0] // rows):
         slot = slots_ref[first + j]
 
         @pl.when(slot < half)
         def _():
-            out_ref[j * rows : (j + 1) * rows] = own_ref[slot].astype(F32)
+            out_ref[j * rows : (j + 1) * rows] = own_ref[slot, :rows].astype(F32)
 
         @pl.when(slot >= half)
         def _():
-            out_ref[j * rows : (j + 1) * rows] = other_ref[slot - half].astype(F32)
+            out_ref[j * rows : (j + 1) * rows] = other_ref[slot - half, :rows].astype(F32)
 
 
 def unpack_body(slots_ref, own_ref, other_ref, out_ref):
-    each = out_ref.shape[0] // own_ref.shape[1]
-    load_slots(slots_ref, pl.program_id(0) * each, own_ref, other_ref, out_ref)
-
-
-def unpack_two_body(last, slots_ref, own_ref, other_ref, out_ref, out2_ref):
+    rows = own_ref.shape[1]
+    each = out_ref.shape[0] // rows
+    load_slots(slots_ref, pl.program_id(0) * each, own_ref, other_ref, out_ref, rows)
+
+
+def unpack_two_body(last, slots_ref, own_ref, other_ref, out_ref, out2_ref, small_ref):
     step = pl.program_id(0)
-    each = out_ref.shape[0] // own_ref.shape[1]
+    half, rows, _ = own_ref.shape
+    rows -= EXTRA
+    each = out_ref.shape[0] // rows
 
     @pl.when(step < last)
     def _():
-        load_slots(slots_ref, step * each, own_ref, other_ref, out_ref)
+        load_slots(slots_ref, step * each, own_ref, other_ref, out_ref, rows)
 
     @pl.when(step == last)
     def _():
-        load_slots(slots_ref, step * each, own_ref, other_ref, out2_ref)
+        load_slots(slots_ref, step * each, own_ref, other_ref, out2_ref, rows)
+        for chunk in range(small_ref.shape[0]):
+            slot = slots_ref[chunk]
+
+            @pl.when(slot < half)
+            def _():
+                small_ref[chunk : chunk + 1] = own_ref[slot, rows:].astype(F32)[:1]
+
+            @pl.when(slot >= half)
+            def _():
+                small_ref[chunk : chunk + 1] = other_ref[slot - half, rows:].astype(F32)[:1]
 
 
 def unpack(line, slots, own, other, height, cols):
@@ -562,12 +656,12 @@
         5,
         (height * cols // (tile * PANEL),),
         [(own, fixed(own.shape)), (other, fixed(other.shape))],
-        [((height, cols), F32, pl.BlockSpec((tile if tall else height, PANEL), index))],
+        [((height, cols), F32, pl.BlockSpec((tile if tall else height, PANEL), index), FAR)],
         [slots],
     )[0]
 
 
-def unpack_two(line, slots, own, other, height, cols):
+def unpack_two(line, slots, own, other, height, cols, small):
     last = cols // PANEL
     return line.run(
         functools.partial(unpack_two_body, last),
@@ -580,8 +674,10 @@
                 (height, cols),
                 F32,
                 pl.BlockSpec((height, PANEL), lambda i, *_: (0, jnp.minimum(i, last - 1))),
+                FAR,
             ),
-            ((height, PANEL), F32, fixed((height, PANEL))),
+            ((height, PANEL), F32, fixed((height, PANEL)), FAR),
+            (small, F32, fixed(small)),
         ],
         [slots],
     )
@@ -707,7 +803,7 @@
         + [(value, fixed(value.shape)) for value in whole],
         [
             ((total, width), BF16, rows_of(rows, width)),
-            ((total, 3 * width), BF16, rows_of(rows, 3 * width)),
+            ((total, 3 * width), BF16, rows_of(rows, 3 * width), FAR),
             ((total, width), BF16, rows_of(rows, width)),
             ((total, width), F32, rows_of(rows, width)),
             ((total, width), BF16, rows_of(rows, width)),
@@ -717,9 +813,10 @@
 
 def ffn_body(
     slots,
+    last,
     length_rows_ref,
     lengths_ref,
-    middle_ref,
+    before_ref,
     normed_ref,
     w_up_ref,
     w_down_ref,
@@ -727,18 +824,20 @@
     hidden_ref,
     pooled_ref,
 ):
-    rows, width = middle_ref.shape
+    rows, width = normed_ref.shape
     some = rows // slots
-    weights = slot_weights(length_rows_ref[...], slots)
     row = lax.broadcasted_iota(jnp.int32, (some, rows), 1)
     entry = lax.broadcasted_iota(jnp.int32, (some, rows), 0)
     lengths = lengths_ref[...]
     valid = (row // slots == entry) & (row % slots <= lengths)
     valid = jnp.where(valid, 1.0, 0.0).astype(BF16)
     scale = 1.0 / (lengths + 1).astype(F32)
-    pooled = jnp.sum((middle_ref[...] * weights).reshape(some, slots, width), axis=1)
+    pooled = before_ref[...]
+    if not last:
+        weights = slot_weights(length_rows_ref[...], slots)
+        pooled = jnp.sum((pooled * weights).reshape(some, slots, width), axis=1)
     ff = w_up_ref.shape[1]
-    step = ff // 4
+    step = ff // 2
     for low in range(0, ff, step):
         up = mm(normed_ref[...], w_up_ref[:, low : low + step])
         square = up * up
@@ -754,33 +853,33 @@
         hidden_ref[:, low : low + step] = high
         w_down = w_down_ref[low : low + step]
         pooled += mm(high, w_down) + mm(rest, w_down)
-    pooled_ref[...] = pooled.astype(BF16)
-
-
-def ffn_forward(line, length_rows, lengths, middle, normed, w_up, w_down):
-    total, width = middle.shape
+    pooled_ref[...] = pooled.astype(pooled_ref.dtype)
+
+
+def ffn_forward(line, length_rows, lengths, before, normed, w_up, w_down, last):
+    total, width = normed.shape
     entries = lengths.shape[0]
     slots = total // entries
     rows = math.gcd(total, 256)
     some = rows // slots
-    ff = w_up.shape[1]
-    return line.run(
-        functools.partial(ffn_body, slots),
+    ff = w_up.shape[1] // 2
+    return line.run(
+        functools.partial(ffn_body, slots, last),
         "ffn_forward",
-        12,
+        7,
         (total // rows,),
         [
             (length_rows, rows_of(rows, 1)),
             (lengths, rows_of(some, 1)),
-            (middle, rows_of(rows, width)),
+            (before, rows_of(some if last else rows, width)),
             (normed, rows_of(rows, width)),
-            (w_up, fixed(w_up.shape)),
-            (w_down, fixed(w_down.shape)),
-        ],
-        [
-            ((total, ff), F32, rows_of(rows, ff)),
+            (w_up, pl.BlockSpec((width, ff), lambda i, *_: (0, int(last)))),
+            (w_down, pl.BlockSpec((ff, width), lambda i, *_: (int(last), 0))),
+        ],
+        [
+            ((total, ff), F32, rows_of(rows, ff), FAR),
             ((entries, ff), BF16, rows_of(some, ff)),
-            ((entries, width), BF16, rows_of(some, width)),
+            ((entries, width), BF16 if last else F32, rows_of(some, width)),
         ],
     )
 
@@ -789,7 +888,8 @@
     slots,
     pooled_grad_ref,
     lengths_ref,
-    slope_ref,
+    slope_a_ref,
+    slope_b_ref,
     middle_ref,
     gain_ffn_ref,
     w_up_ref,
@@ -810,7 +910,8 @@
     grad_normed = jnp.zeros((rows, width), F32)
     for low in range(0, ff, step):
         grad_hidden = nt(grad_ffn, w_down_ref[low : low + step])
-        grad_up = (slope_ref[:, low : low + step] * grad_hidden).astype(BF16)
+        slope_ref, inner = (slope_a_ref, low) if low < ff // 2 else (slope_b_ref, low - ff // 2)
+        grad_up = (slope_ref[:, inner : inner + step] * grad_hidden).astype(BF16)
         grad_up_ref[:, low : low + step] = grad_up
         grad_normed += nt(grad_up, w_up_ref[:, low : low + step])
     unit, rate = center(middle_ref[...])
@@ -826,7 +927,7 @@
     gain_grad_ref[...] += gain_grad
 
 
-def ffn_back(line, pooled_grad, lengths, slope, middle, gain_ffn, w_up, w_down):
+def ffn_back(line, pooled_grad, lengths, slopes, middle, gain_ffn, w_up, w_down):
     total, width = middle.shape
     entries = pooled_grad.shape[0]
     slots = total // entries
@@ -841,7 +942,7 @@
         [
             (pooled_grad, rows_of(some, width)),
             (lengths, rows_of(rows, 1)),
-            (slope, rows_of(rows, ff)),
+            *((slope, rows_of(rows, ff // 2)) for slope in slopes),
             (middle, rows_of(rows, width)),
             (gain_ffn, fixed(gain_ffn.shape)),
             (w_up, fixed(w_up.shape)),
@@ -920,9 +1021,9 @@
     w_qkv_ref,
     grad_mixed_ref,
     grad_middle_ref,
+    gain_ffn_grad_ref,
     grad_pieces_ref,
-    gain_grad_ref,
-    script_grad_ref,
+    small_ref,
 ):
     start, onehot = start_of(pieces_ref, scripts_ref, script_table_ref)
     grad_normed = nt(grad_mixed_ref[...], w_qkv_ref[...])
@@ -931,24 +1032,27 @@
     grad_pieces = grad_middle_ref[...] + grad
     grad_pieces_ref[...] = grad_pieces.reshape(grad_pieces_ref.shape)
 
+    groups = onehot.shape[1]
+
     @pl.when(pl.program_id(0) == 0)
     def _():
-        gain_grad_ref[...] = jnp.zeros_like(gain_grad_ref)
-        script_grad_ref[...] = jnp.zeros_like(script_grad_ref)
-
-    gain_grad_ref[...] += gain_grad
-    script_grad_ref[...] += lax.dot_general(
+        small_ref[...] = jnp.zeros_like(small_ref)
+        small_ref[groups + 1 : groups + 2] = gain_ffn_grad_ref[...]
+
+    small_ref[groups : groups + 1] += gain_grad
+    small_ref[:groups] += lax.dot_general(
         onehot, grad_pieces, (((0,), (0,)), ((), ())), precision=highest
     )
 
 
 def attn_back(
-    line, pieces, scripts, script_table, gain_attn, w_qkv, grad_mixed, grad_middle
+    line, pieces, scripts, script_table, gain_attn, w_qkv, grad_mixed, grad_middle, gain_ffn_grad
 ):
     entries, slots, width = pieces.shape
     total = entries * slots
     rows = math.gcd(total, 256)
     some = rows // slots
+    small = ((script_table.shape[0] + 2 + 7) // 8 * 8, width)
     return line.run(
         attn_back_body,
         "attn_back",
@@ -962,11 +1066,11 @@
             (w_qkv, fixed(w_qkv.shape)),
             (grad_mixed, rows_of(rows, 3 * width)),
             (grad_middle, rows_of(rows, width)),
-        ],
-        [
-            ((entries, slots, width), F32, pl.BlockSpec((some, slots, width), lambda i, *_: (i, 0, 0))),
-            ((1, width), F32, fixed((1, width))),
-            (script_table.shape, F32, fixed(script_table.shape)),
+            (gain_ffn_grad, fixed(gain_ffn_grad.shape)),
+        ],
+        [
+            ((entries, slots, width), F32, pl.BlockSpec((some, slots, width), lambda i, *_: (i, 0, 0)), FAR),
+            (small, F32, fixed(small)),
         ],
     )
 
@@ -1019,16 +1123,15 @@
         shape = tuple(size for _, size, _ in some[1:]) + keep.shape[-2:]
         return keep.reshape(shape), send.reshape(shape)
 
-    flat_ids = slot_ids.reshape(1, tokens)
     flat_grad = out_grad
     parts, pooled_grads = [], []
     for chunk in range(chunks):
         first = chunk * span
         part_send, send, *flat = scatter_rows(
-            line, flat_ids, flat_grad, w_proj, first + span // 2, span // 2, BF16
+            line, slot_ids, flat_grad, w_proj, first + span // 2, span // 2, BF16
         )
         flat_grad = flat[0] if flat else flat_grad
-        part_keep, keep = scatter_rows(line, flat_ids, flat_grad, w_proj, first, span // 2, F32)
+        part_keep, keep = scatter_rows(line, slot_ids, flat_grad, w_proj, first, span // 2, F32)
         parts.append((part_keep, part_send))
         shape = sizes[1:] + (each, width)
         pooling = sum_halves(line, keep.reshape(shape), send.reshape(shape), levels, pooled_grads)
@@ -1041,60 +1144,90 @@
         line, pieces, script_rows, length_rows, script_table, gain_attn, gain_ffn, w_qkv, w_out
     )
     next(pooling, None)
-    slope, hidden, pooled = ffn_forward(
-        line, length_rows, lengths[:, None], middle, normed_ffn, w_up, w_down
-    )
-    gathered = [
-        lax.all_gather(pooled[chunk * each :][:each], ("ent", "rep"), axis=0, tiled=True)
-        for chunk in range(chunks)
-    ]
+    length_cols = lengths[:, None]
+    slope_a, hidden_a, pooled = ffn_forward(
+        line, length_rows, length_cols, middle, normed_ffn, w_up, w_down, False
+    )
+    next(pooling, None)
+    slope_b, hidden_b, pooled = ffn_forward(
+        line, length_rows, length_cols, pooled, normed_ffn, w_up, w_down, True
+    )
     for _ in pooling:
         pass
     grad_pooled = jnp.concatenate(pooled_grads, axis=0) if chunks > 1 else pooled_grads[0]
 
-    down = tall_weight(line, slot_index, hidden, grad_pooled.astype(BF16))
+    held = [((), each, width, BF16, lambda index: [(0, (), ALL, 0, 0)])]
+    halves = [[] for _ in range(chunks)]
+    spreads = [
+        gather_halves(
+            line, stage(line, [(pooled[chunk * each :][:each], [])], held)[0], levels, halves[chunk]
+        )
+        for chunk in range(chunks)
+    ]
+
+    def spread_on():
+        if chunks == 1:
+            next(spreads[0])
+
+    spread_on()
+    down = tall_weight(line, slot_index, (hidden_a, hidden_b), grad_pooled.astype(BF16))
     grad_up, grad_middle, grad_branch, part_gain_ffn = ffn_back(
-        line, grad_pooled, length_rows, slope, middle, gain_ffn, w_up, w_down
-    )
+        line, grad_pooled, length_rows, (slope_a, slope_b), middle, gain_ffn, w_up, w_down
+    )
+    spread_on()
     up = wide_weight(line, slot_index, normed_ffn, grad_up)
     ffn_all, two_all = [], []
     ffn_sum = all_sum_two(line, *cut_up(*down, near), *cut_up(*up, near), near, far, ffn_all)
     next(ffn_sum)
+    spread_on()
     grad_mixed = heads_back(line, length_rows, w_out, mixed, grad_branch, slots)
     next(ffn_sum)
-    two = two_weights(line, slot_index, normed, grad_mixed, context, grad_branch)
+    grad_pieces, small = attn_back(
+        line,
+        pieces,
+        script_rows,
+        script_table,
+        gain_attn,
+        w_qkv,
+        grad_mixed,
+        grad_middle,
+        part_gain_ffn,
+    )
+    spread_on()
+    two = two_weights(line, slot_index, normed, grad_mixed, context, grad_branch, small)
     two_sum = all_sum(line, *cut_up(*two, near), near, far, two_all)
     next(two_sum)
-    next(ffn_sum)
-    grad_pieces, part_gain_attn, part_script = attn_back(
-        line, pieces, script_rows, script_table, gain_attn, w_qkv, grad_mixed, grad_middle
-    )
-    small = lax.all_gather(
-        jnp.concatenate([part_script, part_gain_attn, part_gain_ffn], axis=0), ("ent", "rep"), axis=0
-    )
-    small = jnp.sum(small, axis=0)
-    next(ffn_sum)
-    next(two_sum)
-    numbers = np.argsort(slot_of(np.arange(devices), levels)).astype(np.int32)
-    owners = jnp.asarray(numbers) ^ me
     tables, part_proj = [], None
     for chunk in range(chunks):
-        table, part = table_and_grad(line, owners, gathered[chunk], w_proj, *parts[chunk])
+        for _ in spreads[chunk]:
+            pass
+        own, other = halves[chunk]
+        table, part = table_and_grad(
+            line, own.reshape(span // 2, width), other.reshape(span // 2, width), w_proj, *parts[chunk]
+        )
         tables.append(table)
         part_proj = part if part_proj is None else part_proj + part
     grad_w_proj = part_proj + swap(part_proj, levels[0])
-    next(ffn_sum)
-    next(two_sum)
-    looked_up = lookup(line, slot_ids, tables, 0)
-    next(ffn_sum)
-    next(two_sum)
-    looked_up = lookup(line, slot_ids, tables, 1, looked_up)
-    going = [ffn_sum, two_sum]
-    while going:
-        going = [steps for steps in going if next(steps, 0) is None]
+    looked_up = None
+    order = [(ffn_sum, two_sum), (ffn_sum,), (two_sum,), (ffn_sum, two_sum), (ffn_sum,)]
+    for part, going in enumerate(order):
+        for steps in going:
+            next(steps, 0)
+        if part < 4:
+            looked_up = lookup(line, slot_ids, tables, part, 4, looked_up)
+    next(two_sum, 0)
+    next(ffn_sum, 0)
+    next(two_sum, 0)
+    for _ in ffn_sum:
+        pass
+    next(two_sum, 0)
     grad_w_down = unpack(line, slot_index, merge(ffn_all[0]), merge(ffn_all[1]), *w_down.shape)
     grad_w_up = unpack(line, slot_index, merge(ffn_all[2]), merge(ffn_all[3]), *w_up.shape)
-    grad_w_qkv, grad_w_out = unpack_two(line, slot_index, *map(merge, two_all), *w_qkv.shape)
+    for _ in two_sum:
+        pass
+    grad_w_qkv, grad_w_out, small = unpack_two(
+        line, slot_index, *map(merge, two_all), *w_qkv.shape, small.shape
+    )
     groups = script_table.shape[0]
     return (
         looked_up,

time: 283 us -> 226 us (0.80)
  local copies, waits for them, and re-layouts: 39.8 us -> 9.64 us
  between operations: 14.7 us -> 1.25 us
  waiting for transfers between devices: 46.5 us -> 35.5 us
  starting transfers between devices: 42.7 us -> 52.2 us
  Pallas kernels: 132 us -> 124 us
  other arithmetic: 6.14 us -> 1.91 us
    unnamed x119 -> x60, local copies, waits for them, and re-layouts: 37.9 us -> 7.75 us
    ppermute x39 -> x49, waiting for transfers between devices: 46.5 us -> 35.5 us  [swap(): lax.ppermute(value, name, [(i, i ^ k << shift) for i in range(count)])]
    ppermute x39 -> x49, starting transfers between devices: 42.7 us -> 52.2 us  [swap(): lax.ppermute(value, name, [(i, i ^ k << shift) for i in range(count)])]
    pallas_call x34 -> x41, Pallas kernels: 132 us -> 124 us  [run(): pl.pallas_call(wrapped, grid_spec=pltpu.PrefetchScalarGridSpec(num_scalar...]
  transfers between devices with their start and end apart: 41 -> 49, of which waited for: 14 -> 20; matrix products, arithmetic and copies ran while one was open for 2% -> 1% of each run, Pallas kernels for 35% -> 46%
where the time goes in v2:
time: 226 us; the launch traced here: 225 us
  Pallas kernels  124 us (55%)
  starting transfers between devices  52.2 us (23%)
  waiting for transfers between devices  35.5 us (16%)
  local copies, waits for them, and re-layouts  9.64 us (4%)
    pallas_call x41, Pallas kernels, run(): pl.pallas_call(wrapped, grid_spec=pltpu.PrefetchScalarGridSpec(num_scalar...  124 us
    ppermute x49, starting transfers between devices, swap(): lax.ppermute(value, name, [(i, i ^ k << shift) for i in range(count)])  52.2 us
    ppermute x49, waiting for transfers between devices, swap(): lax.ppermute(value, name, [(i, i ^ k << shift) for i in range(count)])  35.5 us
    unnamed x60, local copies, waits for them, and re-layouts  7.75 us
  transfers between devices with their start and end apart: 49, of which 20 were waited for; matrix products, arithmetic and copies ran while one was open for 1% of the time, Pallas kernels for 46%

profile of v2, /device:TPU:0, one launch (start us, length us, event | category | flops | bytes accessed | tf_op | source)
XLA Modules:
  0.0 225.0 jit_solution(9555075667902170752)
XLA Ops:
  0.6 1.0 fusion.2.refs_0_
  2.6 15.0 %scatter_rows.2 = (bf16[2048,256]{1,0:T(8,128)(2,1)}, bf16[2048,512]{1,0:T(8,128)(2,1)}, bf16[256,8192]{1,0:T(8,128)(2,1)S(1)}, f32[8,128]{1,0:T(8,128)S(1)}) custom-call(s32[4,2048]{1,0:T(4,128)S(1)} %fusion.2.refs_0_, bf16[256,4,2048]{2,1,0:T(4,128)(2,1)} %refs_1_.2, bf16[512,256]{1,0:T(8,128)(2,1)S(1)} %copy-done.8), custom_call_target="tpu_custom_call" | custom-call | flops 41999998976 | bytes 126000000 | tf_op jit(solution)/shard_map/scatter_rows/pallas_call | solution.py:65
  17.7 2.0 copy-done.26
  20.8 2.2 copy-done.27
  23.0 11.5 %scatter_rows.3 = (bf16[2048,256]{1,0:T(8,128)(2,1)}, f32[2048,512]{1,0:T(8,128)S(1)}, f32[8,128]{1,0:T(8,128)S(1)}) custom-call(s32[4,2048]{1,0:T(4,128)S(1)} %fusion.2.refs_0_, bf16[256,8192]{1,0:T(8,128)(2,1)S(1)} %copy-done.27, bf16[512,256]{1,0:T(8,128)(2,1)S(1)} %copy-done.9, f32[8,128]{1,0:T(8,128)S(1)} %get-tuple-element.142.refs_3_), custom_call_target="tpu_custom_call" | custom-call | flops 41999998976 | bytes 126000000 | tf_op jit(solution)/shard_map/scatter_rows/pallas_call | solution.py:65
  35.1 2.6 %collective-permute-start.1 = (bf16[2,4,128,256]{3,2,1,0:T(8,128)(2,1)S(1)}, bf16[2,4,128,256]{3,2,1,0:T(8,128)(2,1)S(1)}, u32[]{:S(2)}, u32[]{:S(2)}) collective-permute-start(bf16[2,4,128,256]{3,2,1,0:T(8,128)(2,1)S(1)} %get-tuple-element.150), channel_id=1, source_target_pairs={{0,2},{2,0},{4,6},{6,4},{8,10},{10,8},{12,14},{14,12},{16,18},{18,... | collective-permute-start | bytes 1572872 | tf_op jit(solution)/shard_map/ppermute | solution.py:92
  37.7 1.5 collective-permute-start.2
  39.2 11.3 %attn_forward.1 = (bf16[1024,512]{1,0:T(8,128)(2,1)S(1)}, bf16[1024,1536]{1,0:T(8,128)(2,1)}, bf16[1024,512]{1,0:T(8,128)(2,1)S(1)}, f32[1024,512]{1,0:T(8,128)S...) custom-call(bf16[128,8,512]{2,1,0:T(8,128)(2,1)S(1)} %copy-done.4, ...), custom_call_target="tpu_custom_call" | custom-call | flops 35999997952 | bytes 108000000 | tf_op jit(solution)/shard_map/attn_forward/pallas_call | solution.py:65
  50.5 1.2 collective-permute-done.2.refs_3_
  51.9 1.6 collective-permute-start.3
  54.0 8.0 %ffn_forward.2 = (f32[1024,1024]{1,0:T(8,128)}, bf16[128,1024]{1,0:T(8,128)(2,1)S(1)}, f32[128,512]{1,0:T(8,128)S(1)}, f32[8,128]{1,0:T(8,128)S(1)}) custom-call(s32[1024,1]{1,0:T(8,128)S(1)} %broadcast_in_dim_reshape.8.refs_2_.refs_0_.refs_1_, s32[128,1]{1,0:T(8,128)S(1)} %copy.33.refs_1_, f32[1024,512]{1,0:T(8,128)S(1)} %get-tuple-element.147.refs_2_.refs_4_, ...), custom_call_target="tpu_custom_call" | custom-call | flops 20999999488 | bytes 63000000 | tf_op jit(solution)/shard_map/ffn_forward/pallas_call | solution.py:65
  62.2 1.6 collective-permute-start.5
  63.8 2.6 %collective-permute-start.6 = (bf16[128,512]{1,0:T(8,128)(2,1)S(1)}, bf16[128,512]{1,0:T(8,128)(2,1)S(1)}, u32[]{:S(2)}, u32[]{:S(2)}) collective-permute-start(bf16[128,512]{1,0:T(8,128)(2,1)S(1)} %get-tuple-element.165), channel_id=1, source_target_pairs={{0,16},{2,18},{4,20},{6,22},{8,24},{10,26},{12,28},{14,30},{16,0},... | collective-permute-start | bytes 393224 | tf_op jit(solution)/shard_map/ppermute | solution.py:92
  66.6 8.0 %ffn_forward.3 = (f32[1024,1024]{1,0:T(8,128)}, bf16[128,1024]{1,0:T(8,128)(2,1)S(1)}, bf16[128,512]{1,0:T(8,128)(2,1)S(1)}, f32[8,128]{1,0:T(8,128)S(1)}) custom-call(s32[1024,1]{1,0:T(8,128)S(1)} %broadcast_in_dim_reshape.8.refs_2_.refs_0_.refs_1_, s32[128,1]{1,0:T(8,128)S(1)} %copy.33.refs_1_, f32[128,512]{1,0:T(8,128)S(1)} %get-tuple-element.155.refs_2_, ...), custom_call_target="tpu_custom_call" | custom-call | flops 20999999488 | bytes 63000000 | tf_op jit(solution)/shard_map/ffn_forward/pallas_call | solution.py:65
  74.6 2.0 collective-permute-done.6.refs_2_
  76.7 2.4 %collective-permute-start.10 = (bf16[128,512]{1,0:T(8,128)(2,1)S(1)}, bf16[128,512]{1,0:T(8,128)(2,1)S(1)}, u32[]{:S(2)}, u32[]{:S(2)}) collective-permute-start(bf16[128,512]{1,0:T(8,128)(2,1)S(1)} %get-tuple-element.169.refs_0_), channel_id=1, source_target_pairs={{0,24},{2,26},{4,28},{6,30},{8,16},{10,18},{12,20},{14,22},{16,8},... | collective-permute-start | bytes 393224 | tf_op jit(solution)/shard_map/ppermute | solution.py:92
  79.1 1.2 collective-permute-start.8
  81.2 2.5 %tall_weight.1 = (f32[16,64,512]{2,1,0:T(8,128)S(1)}, bf16[16,64,512]{2,1,0:T(8,128)(2,1)S(1)}, f32[8,128]{1,0:T(8,128)S(1)}) custom-call(s32[32]{0:T(128)S(1)} %iota_xor_fusion.refs_0_, bf16[128,1024]{1,0:T(8,128)(2,1)S(1)} %get-tuple-element.173.refs_1_, bf16[128,1024]{1,0:T(8,128)(2,1)S(1)} %get-tuple-element.174.refs_2_, ...), custom_call_target="tpu_custom_call" | custom-call | flops 8999999488 | bytes 27000000 | tf_op jit(solution)/shard_map/tall_weight/pallas_call | solution.py:65
  84.6 6.9 %ffn_back.1 = (bf16[1024,2048]{1,0:T(8,128)(2,1)S(1)}, f32[1024,512]{1,0:T(8,128)S(1)}, bf16[1024,512]{1,0:T(8,128)(2,1)S(1)}, f32[1,512]{1,0:T(1,128)S(1)}, f32[8,128]{1,0:T(8,128)S(1)}) custom-call(f32[128,512]{1,0:T(8,128)S(1)} %get-tuple-element.170.refs_0_, s32[1024,1]{1,0:T(8,128)S(1)} %broadcast_in_dim_reshape.8.refs_2_.refs_0_.refs_1_, ...), custom_call_target="tpu_custom_call" | custom-call | flops 44999999488 | bytes 135000000 | tf_op jit(solution)/shard_map/ffn_back/pallas_call | solution.py:65
  91.6 1.1 collective-permute-start.11
  93.4 4.4 %wide_weight.1 = (f32[16,64,512]{2,1,0:T(8,128)S(1)}, bf16[16,64,512]{2,1,0:T(8,128)(2,1)S(1)}, f32[8,128]{1,0:T(8,128)S(1)}) custom-call(s32[32]{0:T(128)S(1)} %iota_xor_fusion.refs_0_, bf16[1024,512]{1,0:T(8,128)(2,1)S(1)} %copy-done.24, bf16[1024,2048]{1,0:T(8,128)(2,1)S(1)} %get-tuple-element.180.refs_2_, f32[8,128]{1,0:T(8,128)S(1)} %get-tuple-element.181.refs_3_), custom_call_target="tpu_custom_call" | custom-call | flops 24000000000 | bytes 72000000 | tf_op jit(solution)/shard_map/wide_weight/pallas_call | solution.py:65
  97.9 1.7 collective-permute-done.11.refs_1_
  102.4 6.3 %heads_back.1 = (bf16[1024,1536]{1,0:T(8,128)(2,1)S(1)}, f32[8,128]{1,0:T(8,128)S(1)}) custom-call(s32[1024,1]{1,0:T(8,128)S(1)} %broadcast_in_dim_reshape.8.refs_2_.refs_0_.refs_1_, bf16[512,512]{1,0:T(8,128)(2,1)S(1)} %copy-done.7, bf16[1024,1536]{1,0:T(8,128)(2,1)S(1)} %copy-done.25, bf16[1024,512]{1,0:T(8,128)(2,1)S(1)} %get-tuple-element.186.refs_3_.refs_4_, ...), custom_call_target="tpu_custom_call" | custom-call | flops 38999998464 | bytes 117000000 | tf_op jit(solution)/shard_map/heads_back/pallas_call | solution.py:65
  109.1 1.0 copy-done.3
  110.4 6.8 %attn_back.1 = (f32[128,8,512]{2,1,0:T(8,128)}, f32[24,512]{1,0:T(8,128)S(1)}, f32[8,128]{1,0:T(8,128)S(1)}) custom-call(bf16[128,8,512]{2,1,0:T(8,128)(2,1)S(1)} %copy-done.5, s32[1024,1]{1,0:T(8,128)S(1)} %broadcast_in_dim_reshape.9.refs_1_, f32[16,512]{1,0:T(8,128)S(1)} %copy-done.11, f32[1,512]{1,0:T(1,128)S(1)} %bitcast.38, ...), custom_call_target="tpu_custom_call" | custom-call | flops 27000000512 | bytes 81000000 | tf_op jit(solution)/shard_map/attn_back/pallas_call | solution.py:65
  117.4 1.1 collective-permute-start.19
  118.5 1.1 collective-permute-start.20
  119.6 4.8 %two_weights.1 = (f32[16,80,512]{2,1,0:T(8,128)S(1)}, bf16[16,80,512]{2,1,0:T(8,128)(2,1)S(1)}, f32[8,128]{1,0:T(8,128)S(1)}) custom-call(s32[32]{0:T(128)S(1)} %iota_xor_fusion.refs_0_, bf16[1024,512]{1,0:T(8,128)(2,1)S(1)} %copy-done.20, bf16[1024,1536]{1,0:T(8,128)(2,1)S(1)} %get-tuple-element.188.refs_5_.refs_2_, bf16[1024,512]{1,0:T(8,128)(2,1)S(1)} %copy-done.22, ...), custom_call_target="tpu_custom_call" | custom-call | flops 15000000512 | bytes 45000000 | tf_op jit(solution)/shard_map/two_weights/pallas_call | solution.py:65
  124.5 3.3 %table_and_grad.1 = (bf16[256,4096]{1,0:T(8,128)(2,1)S(1)}, f32[512,256]{1,0:T(8,128)S(1)}, f32[8,128]{1,0:T(8,128)S(1)}) custom-call(bf16[2048,512]{1,0:T(8,128)(2,1)S(1)} %bitcast.24, bf16[2048,512]{1,0:T(8,128)(2,1)S(1)} %bitcast.25, bf16[512,256]{1,0:T(8,128)(2,1)S(1)} %copy-done.9, bf16[2048,256]{1,0:T(8,128)(2,1)S(1)} %copy-done.18, ...), custom_call_target="tpu_custom_call" | custom-call | flops 15000000512 | bytes 45000000 | tf_op jit(solution)/shard_map/table_and_grad/pallas_call | solution.py:65
  127.8 4.0 %collective-permute-done.19.refs_1_ = bf16[2,4,64,512]{3,2,1,0:T(8,128)(2,1)S(1)} collective-permute-done((bf16[2,4,64,512]{3,2,1,0:T(8,128)(2,1)S(1)}, bf16[2,4,64,512]{3,2,1,0:T(8,128)(2,1)S(1)}, u32[]{:S(2)}, u32[]{:S(2)}) %collective-permute-start.19) | collective-permute-done | bytes 524320 | tf_op jit(solution)/shard_map/ppermute | solution.py:92
  132.7 1.1 collective-permute-start.22
  135.0 1.2 collective-permute-start.21
  136.2 5.7 %lookup.4 = (bf16[256,4,2048]{2,1,0:T(4,128)(2,1)}, f32[8,128]{1,0:T(8,128)S(1)}) custom-call(s32[4,2048]{1,0:T(4,128)S(1)} %fusion.2.refs_0_, bf16[256,4096]{1,0:T(8,128)(2,1)S(1)} %get-tuple-element.206.refs_1_, f32[8,128]{1,0:T(8,128)S(1)} %get-tuple-element.221.refs_2_), custom_call_target="tpu_custom_call" | custom-call | flops 17999998976 | bytes 54000000 | tf_op jit(solution)/shard_map/lookup/pallas_call | solution.py:65
  141.9 1.2 collective-permute-done.23.refs_3_
  143.2 1.1 collective-permute-start.25
  144.4 2.0 collective-permute-start.26
  146.3 1.4 collective-permute-start.27
  147.7 5.7 %lookup.5 = (bf16[256,4,2048]{2,1,0:T(4,128)(2,1)}, f32[8,128]{1,0:T(8,128)S(1)}) custom-call(s32[4,2048]{1,0:T(4,128)S(1)} %fusion.2.refs_0_, bf16[256,4096]{1,0:T(8,128)(2,1)S(1)} %get-tuple-element.206.refs_1_, f32[8,128]{1,0:T(8,128)S(1)} %get-tuple-element.223.refs_2_, ...), custom_call_target="tpu_custom_call", output_to_operand_aliasing={{0}: (3, {})} | custom-call | flops 17999998976 | bytes 54000000 | tf_op jit(solution)/shard_map/lookup/pallas_call | solution.py:65
  153.4 1.8 collective-permute-done.21.refs_1_
  156.4 5.7 %lookup.6 = (bf16[256,4,2048]{2,1,0:T(4,128)(2,1)}, f32[8,128]{1,0:T(8,128)S(1)}) custom-call(s32[4,2048]{1,0:T(4,128)S(1)} %fusion.2.refs_0_, bf16[256,4096]{1,0:T(8,128)(2,1)S(1)} %get-tuple-element.206.refs_1_, f32[8,128]{1,0:T(8,128)S(1)} %get-tuple-element.232.refs_2_, ...), custom_call_target="tpu_custom_call", output_to_operand_aliasing={{0}: (3, {})} | custom-call | flops 17999998976 | bytes 54000000 | tf_op jit(solution)/shard_map/lookup/pallas_call | solution.py:65
  162.2 1.1 collective-permute-start.31
  163.3 1.9 collective-permute-start.32
  165.1 1.5 collective-permute-start.33
  166.7 5.7 %lookup.7 = (bf16[256,4,2048]{2,1,0:T(4,128)(2,1)}, f32[8,128]{1,0:T(8,128)S(1)}) custom-call(s32[4,2048]{1,0:T(4,128)S(1)} %fusion.2.refs_0_, bf16[256,4096]{1,0:T(8,128)(2,1)S(1)} %get-tuple-element.206.refs_1_, f32[8,128]{1,0:T(8,128)S(1)} %get-tuple-element.236.refs_2_, ...), custom_call_target="tpu_custom_call", output_to_operand_aliasing={{0}: (3, {})} | custom-call | flops 17999998976 | bytes 54000000 | tf_op jit(solution)/shard_map/lookup/pallas_call | solution.py:65
  172.4 1.8 collective-permute-done.32.refs_2_
  174.3 1.1 collective-permute-start.37
  176.3 2.0 collective-permute-start.28
  178.2 1.1 collective-permute-start.29
  179.3 1.5 collective-permute-start.30
  180.9 5.0 %collective-permute-done.29.refs_2_ = bf16[80,512]{1,0:T(8,128)(2,1)S(1)} collective-permute-done((bf16[80,512]{1,0:T(8,128)(2,1)S(1)}, bf16[80,512]{1,0:T(8,128)(2,1)S(1)}, u32[]{:S(2)}, u32[]{:S(2)}) %collective-permute-start.29) | collective-permute-done | bytes 81952 | tf_op jit(solution)/shard_map/ppermute | solution.py:92
  186.1 1.1 collective-permute-start.41
  187.2 1.0 collective-permute-start.42
  188.2 1.4 collective-permute-start.34
  189.7 1.5 collective-permute-start.35
  191.2 1.4 collective-permute-start.36
  192.7 3.3 %collective-permute-done.35.refs_2_ = bf16[80,512]{1,0:T(8,128)(2,1)S(1)} collective-permute-done((bf16[80,512]{1,0:T(8,128)(2,1)S(1)}, bf16[80,512]{1,0:T(8,128)(2,1)S(1)}, u32[]{:S(2)}, u32[]{:S(2)}) %collective-permute-start.35) | collective-permute-done | bytes 81952 | tf_op jit(solution)/shard_map/ppermute | solution.py:92
  196.0 1.6 collective-permute-done.36.refs_3_
  198.0 1.2 collective-permute-start.39
  200.0 4.6 %collective-permute-done.39.refs_1_ = bf16[4,80,256]{2,1,0:T(8,128)(2,1)S(1)} collective-permute-done((bf16[4,80,256]{2,1,0:T(8,128)(2,1)S(1)}, bf16[4,80,256]{2,1,0:T(8,128)(2,1)S(1)}, u32[]{:S(2)}, u32[]{:S(2)}) %collective-permute-start.39) | collective-permute-done | bytes 163872 | tf_op jit(solution)/shard_map/ppermute | solution.py:92
  206.4 1.2 collective-permute-start.44
  207.6 3.2 %unpack.2 = (f32[2048,512]{1,0:T(8,128)}, f32[8,128]{1,0:T(8,128)S(1)}) custom-call(s32[32]{0:T(128)S(1)} %iota_xor_fusion.refs_0_, bf16[16,64,512]{2,1,0:T(8,128)(2,1)S(1)} %bitcast.31, bf16[16,64,512]{2,1,0:T(8,128)(2,1)S(1)} %bitcast.32, f32[8,128]{1,0:T(8,128)S(1)} %get-tuple-element.261.refs_3_), custom_call_target="tpu_custom_call" | custom-call | flops 15000000512 | bytes 45000000 | tf_op jit(solution)/shard_map/unpack/pallas_call | solution.py:65
  210.7 3.2 %unpack.3 = (f32[512,2048]{1,0:T(8,128)}, f32[8,128]{1,0:T(8,128)S(1)}) custom-call(s32[32]{0:T(128)S(1)} %iota_xor_fusion.refs_0_, bf16[16,64,512]{2,1,0:T(8,128)(2,1)S(1)} %bitcast.30, bf16[16,64,512]{2,1,0:T(8,128)(2,1)S(1)} %bitcast.34, f32[8,128]{1,0:T(8,128)S(1)} %get-tuple-element.262.refs_3_), custom_call_target="tpu_custom_call" | custom-call | flops 15000000512 | bytes 45000000 | tf_op jit(solution)/shard_map/unpack/pallas_call | solution.py:65
  215.7 3.3 %collective-permute-done.48 = f32[512,256]{1,0:T(8,128)S(1)} collective-permute-done((f32[512,256]{1,0:T(8,128)S(1)}, f32[512,256]{1,0:T(8,128)S(1)}, u32[]{:S(2)}, u32[]{:S(2)}) %collective-permute-start.48) | collective-permute-done | bytes 524320 | tf_op jit(solution)/shard_map/ppermute | solution.py:92
  219.8 4.0 %unpack_two.1 = (f32[512,1536]{1,0:T(8,128)}, f32[512,512]{1,0:T(8,128)}, f32[24,512]{1,0:T(8,128)S(1)}, f32[8,128]{1,0:T(8,128)}) custom-call(s32[32]{0:T(128)S(1)} %iota_xor_fusion.refs_0_, bf16[16,80,512]{2,1,0:T(8,128)(2,1)S(1)} %bitcast.27, bf16[16,80,512]{2,1,0:T(8,128)(2,1)S(1)} %bitcast.28, f32[8,128]{1,0:T(8,128)S(1)} %get-tuple-element.265.refs_3_), custom_call_target="tpu_custom_call" | custom-call | flops 15000000512 | bytes 45000000 | tf_op jit(solution)/shard_map/unpack_two/pallas_call | solution.py:65
  (147 shorter events, 21.6 us)
Async XLA Ops:
  2.6 17.5 %copy-start.28 = (s32[128]{0:T(128)S(1)}, s32[128]{0:T(128)}, u32[]{:S(2)}) copy-start(s32[128]{0:T(128)} %param.14) | copy-start | bytes 1540
  2.6 17.8 %copy-start.29 = (s32[128]{0:T(128)S(1)}, s32[128]{0:T(128)}, u32[]{:S(2)}) copy-start(s32[128]{0:T(128)} %param.15) | copy-start | bytes 1540
  2.6 18.2 %copy-start.9 = (bf16[512,256]{1,0:T(8,128)(2,1)S(1)}, bf16[512,256]{1,0:T(8,128)(2,1)}, u32[]{:S(2)}) copy-start(bf16[512,256]{1,0:T(8,128)(2,1)} %refs_2_.7) | copy-start | bytes 786436
  19.7 14.9 %collective-permute-start = (bf16[2,2,4,128,512]{4,3,2,1,0:T(8,128)(2,1)}, bf16[2,2,4,128,512]{4,3,2,1,0:T(8,128)(2,1)S(1)}, u32[]{:S(2)}, u32[]{:S(2)}) collective-permute-start(bf16[2,2,4,128,512]{4,3,2,1,0:T(8,128)(2,1)} %bitcast.4), channel_id=1, source_target_pairs={{0,1},{1,0},{2,3},{3,2},{4,5},{5,4},{6,7},{7,6},{8,9},{9,8},{10,11... | collective-permute-start | bytes 6291464 | tf_op jit(solution)/shard_map/ppermute | solution.py:92
  34.5 4.6 %copy-start.2 = (bf16[512,1536]{1,0:T(8,128)(2,1)S(1)}, bf16[512,1536]{1,0:T(8,128)(2,1)}, u32[]{:S(2)}) copy-start(bf16[512,1536]{1,0:T(8,128)(2,1)} %refs_4_.5) | copy-start | bytes 4718596
  34.5 4.6 %copy-start.4 = (bf16[128,8,512]{2,1,0:T(8,128)(2,1)S(1)}, bf16[128,8,512]{2,1,0:T(8,128)(2,1)}, u32[]{:S(2)}) copy-start(bf16[128,8,512]{2,1,0:T(8,128)(2,1)} %refs_0_.3) | copy-start | bytes 3145732
  34.5 4.6 %copy-start.6 = (bf16[512,512]{1,0:T(8,128)(2,1)S(1)}, bf16[512,512]{1,0:T(8,128)(2,1)}, u32[]{:S(2)}) copy-start(bf16[512,512]{1,0:T(8,128)(2,1)} %refs_1_.3) | copy-start | bytes 1572868
  34.5 4.6 %copy-start.10 = (f32[16,512]{1,0:T(8,128)S(1)}, f32[16,512]{1,0:T(8,128)}, u32[]{:S(2)}) copy-start(f32[16,512]{1,0:T(8,128)} %refs_2_.6) | copy-start | bytes 98308
  34.6 4.6 %copy-start.12 = (f32[512]{0:T(512)S(1)}, f32[512]{0:T(512)}, u32[]{:S(2)}) copy-start(f32[512]{0:T(512)} %param.18) | copy-start | bytes 6148
  34.6 4.6 %copy-start.13 = (f32[512]{0:T(512)S(1)}, f32[512]{0:T(512)}, u32[]{:S(2)}) copy-start(f32[512]{0:T(512)} %param.17) | copy-start | bytes 6148
  35.1 15.4 %collective-permute-start.1 = (bf16[2,4,128,256]{3,2,1,0:T(8,128)(2,1)S(1)}, bf16[2,4,128,256]{3,2,1,0:T(8,128)(2,1)S(1)}, u32[]{:S(2)}, u32[]{:S(2)}) collective-permute-start(bf16[2,4,128,256]{3,2,1,0:T(8,128)(2,1)S(1)} %get-tuple-element.150), channel_id=1, source_target_pairs={{0,2},{2,0},{4,6},{6,4},{8,10},{10,8},{12,14},{14,12},{16,18},{18,... | collective-permute-start | bytes 1572872 | tf_op jit(solution)/shard_map/ppermute | solution.py:92
  37.7 14.0 %collective-permute-start.2 = (bf16[2,4,128,256]{3,2,1,0:T(8,128)(2,1)S(1)}, bf16[2,4,128,256]{3,2,1,0:T(8,128)(2,1)S(1)}, u32[]{:S(2)}, u32[]{:S(2)}) collective-permute-start(bf16[2,4,128,256]{3,2,1,0:T(8,128)(2,1)S(1)} %get-tuple-element.152), channel_id=1, source_target_pairs={{0,4},{2,6},{4,0},{6,2},{8,12},{10,14},{12,8},{14,10},{16,20},{18,... | collective-permute-start | bytes 1572872 | tf_op jit(solution)/shard_map/ppermute | solution.py:92
  50.5 16.1 %copy-start.23 = (bf16[1024,512]{1,0:T(8,128)(2,1)}, bf16[1024,512]{1,0:T(8,128)(2,1)S(1)}, u32[]{:S(2)}) copy-start(bf16[1024,512]{1,0:T(8,128)(2,1)S(1)} %get-tuple-element.148.refs_3_.refs_1_) | copy-start | bytes 3145732
  51.9 10.1 %collective-permute-start.3 = (bf16[4,128,256]{2,1,0:T(8,128)(2,1)S(1)}, bf16[4,128,256]{2,1,0:T(8,128)(2,1)S(1)}, u32[]{:S(2)}, u32[]{:S(2)}) collective-permute-start(bf16[4,128,256]{2,1,0:T(8,128)(2,1)S(1)} %get-tuple-element.157), channel_id=1, source_target_pairs={{0,4},{2,6},{4,0},{6,2},{8,12},{10,14},{12,8},{14,10},{16,20},{18,... | collective-permute-start | bytes 786440 | tf_op jit(solution)/shard_map/ppermute | solution.py:92
  53.5 8.5 %collective-permute-start.4 = (bf16[4,128,256]{2,1,0:T(8,128)(2,1)S(1)}, bf16[4,128,256]{2,1,0:T(8,128)(2,1)S(1)}, u32[]{:S(2)}, u32[]{:S(2)}) collective-permute-start(bf16[4,128,256]{2,1,0:T(8,128)(2,1)S(1)} %get-tuple-element.159), channel_id=1, source_target_pairs={{0,2},{2,0},{4,6},{6,4},{8,10},{10,8},{12,14},{14,12},{16,18},{18,... | collective-permute-start | bytes 786440 | tf_op jit(solution)/shard_map/ppermute | solution.py:92
  62.2 12.4 %collective-permute-start.5 = (bf16[128,512]{1,0:T(8,128)(2,1)S(1)}, bf16[128,512]{1,0:T(8,128)(2,1)S(1)}, u32[]{:S(2)}, u32[]{:S(2)}) collective-permute-start(bf16[128,512]{1,0:T(8,128)(2,1)S(1)} %get-tuple-element.164), channel_id=1, source_target_pairs={{0,8},{2,10},{4,12},{6,14},{8,0},{10,2},{12,4},{14,6},{16,24},{18,... | collective-permute-start | bytes 393224 | tf_op jit(solution)/shard_map/ppermute | solution.py:92
  63.8 12.8 %collective-permute-start.6 = (bf16[128,512]{1,0:T(8,128)(2,1)S(1)}, bf16[128,512]{1,0:T(8,128)(2,1)S(1)}, u32[]{:S(2)}, u32[]{:S(2)}) collective-permute-start(bf16[128,512]{1,0:T(8,128)(2,1)S(1)} %get-tuple-element.165), channel_id=1, source_target_pairs={{0,16},{2,18},{4,20},{6,22},{8,24},{10,26},{12,28},{14,30},{16,0},... | collective-permute-start | bytes 393224 | tf_op jit(solution)/shard_map/ppermute | solution.py:92
  66.4 10.2 %collective-permute-start.7 = (bf16[128,512]{1,0:T(8,128)(2,1)S(1)}, bf16[128,512]{1,0:T(8,128)(2,1)S(1)}, u32[]{:S(2)}, u32[]{:S(2)}) collective-permute-start(bf16[128,512]{1,0:T(8,128)(2,1)S(1)} %get-tuple-element.166), channel_id=1, source_target_pairs={{0,24},{2,26},{4,28},{6,30},{8,16},{10,18},{12,20},{14,22},{16,8},... | collective-permute-start | bytes 393224 | tf_op jit(solution)/shard_map/ppermute | solution.py:92
  76.7 14.8 %collective-permute-start.10 = (bf16[128,512]{1,0:T(8,128)(2,1)S(1)}, bf16[128,512]{1,0:T(8,128)(2,1)S(1)}, u32[]{:S(2)}, u32[]{:S(2)}) collective-permute-start(bf16[128,512]{1,0:T(8,128)(2,1)S(1)} %get-tuple-element.169.refs_0_), channel_id=1, source_target_pairs={{0,24},{2,26},{4,28},{6,30},{8,16},{10,18},{12,20},{14,22},{16,8},... | collective-permute-start | bytes 393224 | tf_op jit(solution)/shard_map/ppermute | solution.py:92
  79.1 12.4 %collective-permute-start.8 = (bf16[128,512]{1,0:T(8,128)(2,1)S(1)}, bf16[128,512]{1,0:T(8,128)(2,1)S(1)}, u32[]{:S(2)}, u32[]{:S(2)}) collective-permute-start(bf16[128,512]{1,0:T(8,128)(2,1)S(1)} %get-tuple-element.169.refs_0_), channel_id=1, source_target_pairs={{0,8},{2,10},{4,12},{6,14},{8,0},{10,2},{12,4},{14,6},{16,24},{18,... | collective-permute-start | bytes 393224 | tf_op jit(solution)/shard_map/ppermute | solution.py:92
  80.3 11.3 %collective-permute-start.9 = (bf16[128,512]{1,0:T(8,128)(2,1)S(1)}, bf16[128,512]{1,0:T(8,128)(2,1)S(1)}, u32[]{:S(2)}, u32[]{:S(2)}) collective-permute-start(bf16[128,512]{1,0:T(8,128)(2,1)S(1)} %get-tuple-element.169.refs_0_), channel_id=1, source_target_pairs={{0,16},{2,18},{4,20},{6,22},{8,24},{10,26},{12,28},{14,30},{16,0},... | collective-permute-start | bytes 393224 | tf_op jit(solution)/shard_map/ppermute | solution.py:92
  81.2 2.6 %copy-start.15 = (f32[1024,1024]{1,0:T(8,128)S(1)}, f32[1024,1024]{1,0:T(8,128)}, u32[]{:S(2)}) copy-start(f32[1024,1024]{1,0:T(8,128)} %get-tuple-element.171.refs_2_) | copy-start | bytes 12582916
  81.2 3.5 %copy-start.16 = (f32[1024,1024]{1,0:T(8,128)S(1)}, f32[1024,1024]{1,0:T(8,128)}, u32[]{:S(2)}) copy-start(f32[1024,1024]{1,0:T(8,128)} %get-tuple-element.172.refs_3_) | copy-start | bytes 12582916
  83.7 25.0 %collective-permute-start.15 = (bf16[2,2,4,64,512]{4,3,2,1,0:T(8,128)(2,1)S(1)}, bf16[2,2,4,64,512]{4,3,2,1,0:T(8,128)(2,1)S(1)}, u32[]{:S(2)}, u32[]{:S(2)}) collective-permute-start(bf16[2,2,4,64,512]{4,3,2,1,0:T(8,128)(2,1)S(1)} %bitcast.29), channel_id=1, source_target_pairs={{0,1},{1,0},{2,3},{3,2},{4,5},{5,4},{6,7},{7,6},{8,9},{9,8},{10,11... | collective-permute-start | bytes 3145736 | tf_op jit(solution)/shard_map/ppermute | solution.py:92
  91.6 7.9 %collective-permute-start.11 = (bf16[4,128,256]{2,1,0:T(8,128)(2,1)S(1)}, bf16[4,128,256]{2,1,0:T(8,128)(2,1)S(1)}, u32[]{:S(2)}, u32[]{:S(2)}) collective-permute-start(bf16[4,128,256]{2,1,0:T(8,128)(2,1)S(1)} %get-tuple-element.178.refs_0_), channel_id=1, source_target_pairs={{0,4},{2,6},{4,0},{6,2},{8,12},{10,14},{12,8},{14,10},{16,20},{18,... | collective-permute-start | bytes 786440 | tf_op jit(solution)/shard_map/ppermute | solution.py:92
  92.8 7.6 %collective-permute-start.12 = (bf16[4,128,256]{2,1,0:T(8,128)(2,1)S(1)}, bf16[4,128,256]{2,1,0:T(8,128)(2,1)S(1)}, u32[]{:S(2)}, u32[]{:S(2)}) collective-permute-start(bf16[4,128,256]{2,1,0:T(8,128)(2,1)S(1)} %get-tuple-element.179.refs_2_), channel_id=1, source_target_pairs={{0,2},{2,0},{4,6},{6,4},{8,10},{10,8},{12,14},{14,12},{16,18},{18,... | collective-permute-start | bytes 786440 | tf_op jit(solution)/shard_map/ppermute | solution.py:92
  97.8 10.9 %collective-permute-start.16 = (bf16[2,2,4,64,512]{4,3,2,1,0:T(8,128)(2,1)S(1)}, bf16[2,2,4,64,512]{4,3,2,1,0:T(8,128)(2,1)S(1)}, u32[]{:S(2)}, u32[]{:S(2)}) collective-permute-start(bf16[2,2,4,64,512]{4,3,2,1,0:T(8,128)(2,1)S(1)} %bitcast.33), channel_id=1, source_target_pairs={{0,1},{1,0},{2,3},{3,2},{4,5},{5,4},{6,7},{7,6},{8,9},{9,8},{10,11... | collective-permute-start | bytes 3145736 | tf_op jit(solution)/shard_map/ppermute | solution.py:92
  100.4 16.7 %collective-permute-start.13 = (bf16[2,4,128,256]{3,2,1,0:T(8,128)(2,1)S(1)}, bf16[2,4,128,256]{3,2,1,0:T(8,128)(2,1)S(1)}, u32[]{:S(2)}, u32[]{:S(2)}) collective-permute-start(bf16[2,4,128,256]{3,2,1,0:T(8,128)(2,1)S(1)} %get-tuple-element.183.refs_0_), channel_id=1, source_target_pairs={{0,2},{2,0},{4,6},{6,4},{8,10},{10,8},{12,14},{14,12},{16,18},{18,... | collective-permute-start | bytes 1572872 | tf_op jit(solution)/shard_map/ppermute | solution.py:92
  101.1 16.0 %collective-permute-start.14 = (bf16[2,4,128,256]{3,2,1,0:T(8,128)(2,1)S(1)}, bf16[2,4,128,256]{3,2,1,0:T(8,128)(2,1)S(1)}, u32[]{:S(2)}, u32[]{:S(2)}) collective-permute-start(bf16[2,4,128,256]{3,2,1,0:T(8,128)(2,1)S(1)} %get-tuple-element.184.refs_2_), channel_id=1, source_target_pairs={{0,4},{2,6},{4,0},{6,2},{8,12},{10,14},{12,8},{14,10},{16,20},{18,... | collective-permute-start | bytes 1572872 | tf_op jit(solution)/shard_map/ppermute | solution.py:92
  117.2 2.4 %copy-start.20 = (bf16[1024,512]{1,0:T(8,128)(2,1)S(1)}, bf16[1024,512]{1,0:T(8,128)(2,1)}, u32[]{:S(2)}) copy-start(bf16[1024,512]{1,0:T(8,128)(2,1)} %copy-done.19) | copy-start | bytes 3145732
  117.3 7.1 %collective-permute-start.17 = (bf16[2,2,4,128,512]{4,3,2,1,0:T(8,128)(2,1)S(1)}, bf16[2,2,4,128,512]{4,3,2,1,0:T(8,128)(2,1)S(1)}, u32[]{:S(2)}, u32[]{:S(2)}) collective-permute-start(bf16[2,2,4,128,512]{4,3,2,1,0:T(8,128)(2,1)S(1)} %get-tuple-element.198), channel_id=1, source_target_pairs={{0,1},{1,0},{2,3},{3,2},{4,5},{5,4},{6,7},{7,6},{8,9},{9,8},{10,11... | collective-permute-start | bytes 6291464 | tf_op jit(solution)/shard_map/ppermute | solution.py:92
  117.4 14.3 %collective-permute-start.19 = (bf16[2,4,64,512]{3,2,1,0:T(8,128)(2,1)S(1)}, bf16[2,4,64,512]{3,2,1,0:T(8,128)(2,1)S(1)}, u32[]{:S(2)}, u32[]{:S(2)}) collective-permute-start(bf16[2,4,64,512]{3,2,1,0:T(8,128)(2,1)S(1)} %get-tuple-element.210), channel_id=1, source_target_pairs={{0,2},{2,0},{4,6},{6,4},{8,10},{10,8},{12,14},{14,12},{16,18},{18,... | collective-permute-start | bytes 1572872 | tf_op jit(solution)/shard_map/ppermute | solution.py:92
  118.5 14.0 %collective-permute-start.20 = (bf16[2,4,64,512]{3,2,1,0:T(8,128)(2,1)S(1)}, bf16[2,4,64,512]{3,2,1,0:T(8,128)(2,1)S(1)}, u32[]{:S(2)}, u32[]{:S(2)}) collective-permute-start(bf16[2,4,64,512]{3,2,1,0:T(8,128)(2,1)S(1)} %get-tuple-element.212), channel_id=1, source_target_pairs={{0,4},{2,6},{4,0},{6,2},{8,12},{10,14},{12,8},{14,10},{16,20},{18,... | collective-permute-start | bytes 1572872 | tf_op jit(solution)/shard_map/ppermute | solution.py:92
  119.6 4.9 %copy-start.17 = (bf16[2048,256]{1,0:T(8,128)(2,1)S(1)}, bf16[2048,256]{1,0:T(8,128)(2,1)}, u32[]{:S(2)}) copy-start(bf16[2048,256]{1,0:T(8,128)(2,1)} %get-tuple-element.200.refs_4_) | copy-start | bytes 3145732
  119.6 4.9 %copy-start.18 = (bf16[2048,256]{1,0:T(8,128)(2,1)S(1)}, bf16[2048,256]{1,0:T(8,128)(2,1)}, u32[]{:S(2)}) copy-start(bf16[2048,256]{1,0:T(8,128)(2,1)} %get-tuple-element.199.refs_3_) | copy-start | bytes 3145732
  124.4 10.4 %collective-permute-start.18 = (bf16[2,2,4,80,512]{4,3,2,1,0:T(8,128)(2,1)S(1)}, bf16[2,2,4,80,512]{4,3,2,1,0:T(8,128)(2,1)S(1)}, u32[]{:S(2)}, u32[]{:S(2)}) collective-permute-start(bf16[2,2,4,80,512]{4,3,2,1,0:T(8,128)(2,1)S(1)} %bitcast.26), channel_id=1, source_target_pairs={{0,1},{1,0},{2,3},{3,2},{4,5},{5,4},{6,7},{7,6},{8,9},{9,8},{10,11... | collective-permute-start | bytes 3932168 | tf_op jit(solution)/shard_map/ppermute | solution.py:92
  132.7 9.2 %collective-permute-start.22 = (bf16[4,64,512]{2,1,0:T(8,128)(2,1)S(1)}, bf16[4,64,512]{2,1,0:T(8,128)(2,1)S(1)}, u32[]{:S(2)}, u32[]{:S(2)}) collective-permute-start(bf16[4,64,512]{2,1,0:T(8,128)(2,1)S(1)} %get-tuple-element.218), channel_id=1, source_target_pairs={{0,4},{2,6},{4,0},{6,2},{8,12},{10,14},{12,8},{14,10},{16,20},{18,... | collective-permute-start | bytes 786440 | tf_op jit(solution)/shard_map/ppermute | solution.py:92
  133.9 9.2 %collective-permute-start.23 = (bf16[4,64,512]{2,1,0:T(8,128)(2,1)S(1)}, bf16[4,64,512]{2,1,0:T(8,128)(2,1)S(1)}, u32[]{:S(2)}, u32[]{:S(2)}) collective-permute-start(bf16[4,64,512]{2,1,0:T(8,128)(2,1)S(1)} %get-tuple-element.220), channel_id=1, source_target_pairs={{0,2},{2,0},{4,6},{6,4},{8,10},{10,8},{12,14},{14,12},{16,18},{18,... | collective-permute-start | bytes 786440 | tf_op jit(solution)/shard_map/ppermute | solution.py:92
  135.0 20.2 %collective-permute-start.21 = (bf16[2,4,80,512]{3,2,1,0:T(8,128)(2,1)S(1)}, bf16[2,4,80,512]{3,2,1,0:T(8,128)(2,1)S(1)}, u32[]{:S(2)}, u32[]{:S(2)}) collective-permute-start(bf16[2,4,80,512]{3,2,1,0:T(8,128)(2,1)S(1)} %get-tuple-element.216), channel_id=1, source_target_pairs={{0,2},{2,0},{4,6},{6,4},{8,10},{10,8},{12,14},{14,12},{16,18},{18,... | collective-permute-start | bytes 1966088 | tf_op jit(solution)/shard_map/ppermute | solution.py:92
  143.2 18.9 %collective-permute-start.25 = (bf16[128,512]{1,0:T(8,128)(2,1)S(1)}, bf16[128,512]{1,0:T(8,128)(2,1)S(1)}, u32[]{:S(2)}, u32[]{:S(2)}) collective-permute-start(bf16[128,512]{1,0:T(8,128)(2,1)S(1)} %get-tuple-element.229), channel_id=1, source_target_pairs={{0,8},{2,10},{4,12},{6,14},{8,0},{10,2},{12,4},{14,6},{16,24},{18,... | collective-permute-start | bytes 393224 | tf_op jit(solution)/shard_map/ppermute | solution.py:92
  144.4 17.7 %collective-permute-start.26 = (bf16[128,512]{1,0:T(8,128)(2,1)S(1)}, bf16[128,512]{1,0:T(8,128)(2,1)S(1)}, u32[]{:S(2)}, u32[]{:S(2)}) collective-permute-start(bf16[128,512]{1,0:T(8,128)(2,1)S(1)} %get-tuple-element.230), channel_id=1, source_target_pairs={{0,16},{2,18},{4,20},{6,22},{8,24},{10,26},{12,28},{14,30},{16,0},... | collective-permute-start | bytes 393224 | tf_op jit(solution)/shard_map/ppermute | solution.py:92
  146.3 15.8 %collective-permute-start.27 = (bf16[128,512]{1,0:T(8,128)(2,1)S(1)}, bf16[128,512]{1,0:T(8,128)(2,1)S(1)}, u32[]{:S(2)}, u32[]{:S(2)}) collective-permute-start(bf16[128,512]{1,0:T(8,128)(2,1)S(1)} %get-tuple-element.231), channel_id=1, source_target_pairs={{0,24},{2,26},{4,28},{6,30},{8,16},{10,18},{12,20},{14,22},{16,8},... | collective-permute-start | bytes 393224 | tf_op jit(solution)/shard_map/ppermute | solution.py:92
  155.4 11.3 %collective-permute-start.24 = (bf16[4,80,512]{2,1,0:T(8,128)(2,1)S(1)}, bf16[4,80,512]{2,1,0:T(8,128)(2,1)S(1)}, u32[]{:S(2)}, u32[]{:S(2)}) collective-permute-start(bf16[4,80,512]{2,1,0:T(8,128)(2,1)S(1)} %get-tuple-element.227), channel_id=1, source_target_pairs={{0,4},{2,6},{4,0},{6,2},{8,12},{10,14},{12,8},{14,10},{16,20},{18,... | collective-permute-start | bytes 983048 | tf_op jit(solution)/shard_map/ppermute | solution.py:92
  162.2 10.3 %collective-permute-start.31 = (bf16[128,512]{1,0:T(8,128)(2,1)S(1)}, bf16[128,512]{1,0:T(8,128)(2,1)S(1)}, u32[]{:S(2)}, u32[]{:S(2)}) collective-permute-start(bf16[128,512]{1,0:T(8,128)(2,1)S(1)} %get-tuple-element.244.refs_0_), channel_id=1, source_target_pairs={{0,8},{2,10},{4,12},{6,14},{8,0},{10,2},{12,4},{14,6},{16,24},{18,... | collective-permute-start | bytes 393224 | tf_op jit(solution)/shard_map/ppermute | solution.py:92
  163.3 10.9 %collective-permute-start.32 = (bf16[128,512]{1,0:T(8,128)(2,1)S(1)}, bf16[128,512]{1,0:T(8,128)(2,1)S(1)}, u32[]{:S(2)}, u32[]{:S(2)}) collective-permute-start(bf16[128,512]{1,0:T(8,128)(2,1)S(1)} %get-tuple-element.244.refs_0_), channel_id=1, source_target_pairs={{0,16},{2,18},{4,20},{6,22},{8,24},{10,26},{12,28},{14,30},{16,0},... | collective-permute-start | bytes 393224 | tf_op jit(solution)/shard_map/ppermute | solution.py:92
  165.1 9.0 %collective-permute-start.33 = (bf16[128,512]{1,0:T(8,128)(2,1)S(1)}, bf16[128,512]{1,0:T(8,128)(2,1)S(1)}, u32[]{:S(2)}, u32[]{:S(2)}) collective-permute-start(bf16[128,512]{1,0:T(8,128)(2,1)S(1)} %get-tuple-element.244.refs_0_), channel_id=1, source_target_pairs={{0,24},{2,26},{4,28},{6,30},{8,16},{10,18},{12,20},{14,22},{16,8},... | collective-permute-start | bytes 393224 | tf_op jit(solution)/shard_map/ppermute | solution.py:92
  174.3 11.7 %collective-permute-start.37 = (bf16[4,64,512]{2,1,0:T(8,128)(2,1)S(1)}, bf16[4,64,512]{2,1,0:T(8,128)(2,1)S(1)}, u32[]{:S(2)}, u32[]{:S(2)}) collective-permute-start(bf16[4,64,512]{2,1,0:T(8,128)(2,1)S(1)} %get-tuple-element.273.refs_0_), channel_id=1, source_target_pairs={{0,4},{2,6},{4,0},{6,2},{8,12},{10,14},{12,8},{14,10},{16,20},{18,... | collective-permute-start | bytes 786440 | tf_op jit(solution)/shard_map/ppermute | solution.py:92
  175.4 10.6 %collective-permute-start.38 = (bf16[4,64,512]{2,1,0:T(8,128)(2,1)S(1)}, bf16[4,64,512]{2,1,0:T(8,128)(2,1)S(1)}, u32[]{:S(2)}, u32[]{:S(2)}) collective-permute-start(bf16[4,64,512]{2,1,0:T(8,128)(2,1)S(1)} %get-tuple-element.272.refs_2_), channel_id=1, source_target_pairs={{0,2},{2,0},{4,6},{6,4},{8,10},{10,8},{12,14},{14,12},{16,18},{18,... | collective-permute-start | bytes 786440 | tf_op jit(solution)/shard_map/ppermute | solution.py:92
  176.3 4.7 %collective-permute-start.28 = (bf16[80,512]{1,0:T(8,128)(2,1)S(1)}, bf16[80,512]{1,0:T(8,128)(2,1)S(1)}, u32[]{:S(2)}, u32[]{:S(2)}) collective-permute-start(bf16[80,512]{1,0:T(8,128)(2,1)S(1)} %get-tuple-element.241), channel_id=1, source_target_pairs={{0,8},{2,10},{4,12},{6,14},{8,0},{10,2},{12,4},{14,6},{16,24},{18,... | collective-permute-start | bytes 245768 | tf_op jit(solution)/shard_map/ppermute | solution.py:92
  178.2 7.7 %collective-permute-start.29 = (bf16[80,512]{1,0:T(8,128)(2,1)S(1)}, bf16[80,512]{1,0:T(8,128)(2,1)S(1)}, u32[]{:S(2)}, u32[]{:S(2)}) collective-permute-start(bf16[80,512]{1,0:T(8,128)(2,1)S(1)} %get-tuple-element.242), channel_id=1, source_target_pairs={{0,16},{2,18},{4,20},{6,22},{8,24},{10,26},{12,28},{14,30},{16,0},... | collective-permute-start | bytes 245768 | tf_op jit(solution)/shard_map/ppermute | solution.py:92
  179.3 6.6 %collective-permute-start.30 = (bf16[80,512]{1,0:T(8,128)(2,1)S(1)}, bf16[80,512]{1,0:T(8,128)(2,1)S(1)}, u32[]{:S(2)}, u32[]{:S(2)}) collective-permute-start(bf16[80,512]{1,0:T(8,128)(2,1)S(1)} %get-tuple-element.243), channel_id=1, source_target_pairs={{0,24},{2,26},{4,28},{6,30},{8,16},{10,18},{12,20},{14,22},{16,8},... | collective-permute-start | bytes 245768 | tf_op jit(solution)/shard_map/ppermute | solution.py:92
  186.1 11.5 %collective-permute-start.41 = (bf16[2,4,64,512]{3,2,1,0:T(8,128)(2,1)S(1)}, bf16[2,4,64,512]{3,2,1,0:T(8,128)(2,1)S(1)}, u32[]{:S(2)}, u32[]{:S(2)}) collective-permute-start(bf16[2,4,64,512]{3,2,1,0:T(8,128)(2,1)S(1)} %get-tuple-element.253.refs_0_), channel_id=1, source_target_pairs={{0,2},{2,0},{4,6},{6,4},{8,10},{10,8},{12,14},{14,12},{16,18},{18,... | collective-permute-start | bytes 1572872 | tf_op jit(solution)/shard_map/ppermute | solution.py:92
  187.2 10.6 %collective-permute-start.42 = (bf16[2,4,64,512]{3,2,1,0:T(8,128)(2,1)S(1)}, bf16[2,4,64,512]{3,2,1,0:T(8,128)(2,1)S(1)}, u32[]{:S(2)}, u32[]{:S(2)}) collective-permute-start(bf16[2,4,64,512]{3,2,1,0:T(8,128)(2,1)S(1)} %get-tuple-element.254.refs_2_), channel_id=1, source_target_pairs={{0,4},{2,6},{4,0},{6,2},{8,12},{10,14},{12,8},{14,10},{16,20},{18,... | collective-permute-start | bytes 1572872 | tf_op jit(solution)/shard_map/ppermute | solution.py:92
  188.2 4.4 %collective-permute-start.34 = (bf16[80,512]{1,0:T(8,128)(2,1)S(1)}, bf16[80,512]{1,0:T(8,128)(2,1)S(1)}, u32[]{:S(2)}, u32[]{:S(2)}) collective-permute-start(bf16[80,512]{1,0:T(8,128)(2,1)S(1)} %get-tuple-element.247.refs_0_), channel_id=1, source_target_pairs={{0,8},{2,10},{4,12},{6,14},{8,0},{10,2},{12,4},{14,6},{16,24},{18,... | collective-permute-start | bytes 245768 | tf_op jit(solution)/shard_map/ppermute | solution.py:92
  189.7 6.3 %collective-permute-start.35 = (bf16[80,512]{1,0:T(8,128)(2,1)S(1)}, bf16[80,512]{1,0:T(8,128)(2,1)S(1)}, u32[]{:S(2)}, u32[]{:S(2)}) collective-permute-start(bf16[80,512]{1,0:T(8,128)(2,1)S(1)} %get-tuple-element.247.refs_0_), channel_id=1, source_target_pairs={{0,16},{2,18},{4,20},{6,22},{8,24},{10,26},{12,28},{14,30},{16,0},... | collective-permute-start | bytes 245768 | tf_op jit(solution)/shard_map/ppermute | solution.py:92
  191.2 6.3 %collective-permute-start.36 = (bf16[80,512]{1,0:T(8,128)(2,1)S(1)}, bf16[80,512]{1,0:T(8,128)(2,1)S(1)}, u32[]{:S(2)}, u32[]{:S(2)}) collective-permute-start(bf16[80,512]{1,0:T(8,128)(2,1)S(1)} %get-tuple-element.247.refs_0_), channel_id=1, source_target_pairs={{0,24},{2,26},{4,28},{6,30},{8,16},{10,18},{12,20},{14,22},{16,8},... | collective-permute-start | bytes 245768 | tf_op jit(solution)/shard_map/ppermute | solution.py:92
  197.9 9.6 %collective-permute-start.46 = (bf16[2,2,4,64,512]{4,3,2,1,0:T(8,128)(2,1)S(1)}, bf16[2,2,4,64,512]{4,3,2,1,0:T(8,128)(2,1)S(1)}, u32[]{:S(2)}, u32[]{:S(2)}) collective-permute-start(bf16[2,2,4,64,512]{4,3,2,1,0:T(8,128)(2,1)S(1)} %get-tuple-element.260), channel_id=1, source_target_pairs={{0,1},{1,0},{2,3},{3,2},{4,5},{5,4},{6,7},{7,6},{8,9},{9,8},{10,11... | collective-permute-start | bytes 3145736 | tf_op jit(solution)/shard_map/ppermute | solution.py:92
  198.0 6.6 %collective-permute-start.39 = (bf16[4,80,256]{2,1,0:T(8,128)(2,1)S(1)}, bf16[4,80,256]{2,1,0:T(8,128)(2,1)S(1)}, u32[]{:S(2)}, u32[]{:S(2)}) collective-permute-start(bf16[4,80,256]{2,1,0:T(8,128)(2,1)S(1)} %get-tuple-element.251.refs_0_), channel_id=1, source_target_pairs={{0,4},{2,6},{4,0},{6,2},{8,12},{10,14},{12,8},{14,10},{16,20},{18,... | collective-permute-start | bytes 491528 | tf_op jit(solution)/shard_map/ppermute | solution.py:92
  199.2 6.3 %collective-permute-start.40 = (bf16[4,80,256]{2,1,0:T(8,128)(2,1)S(1)}, bf16[4,80,256]{2,1,0:T(8,128)(2,1)S(1)}, u32[]{:S(2)}, u32[]{:S(2)}) collective-permute-start(bf16[4,80,256]{2,1,0:T(8,128)(2,1)S(1)} %get-tuple-element.252.refs_2_), channel_id=1, source_target_pairs={{0,2},{2,0},{4,6},{6,4},{8,10},{10,8},{12,14},{14,12},{16,18},{18,... | collective-permute-start | bytes 491528 | tf_op jit(solution)/shard_map/ppermute | solution.py:92
  200.0 10.8 %collective-permute-start.45 = (bf16[2,2,4,64,512]{4,3,2,1,0:T(8,128)(2,1)S(1)}, bf16[2,2,4,64,512]{4,3,2,1,0:T(8,128)(2,1)S(1)}, u32[]{:S(2)}, u32[]{:S(2)}) collective-permute-start(bf16[2,2,4,64,512]{4,3,2,1,0:T(8,128)(2,1)S(1)} %get-tuple-element.259), channel_id=1, source_target_pairs={{0,1},{1,0},{2,3},{3,2},{4,5},{5,4},{6,7},{7,6},{8,9},{9,8},{10,11... | collective-permute-start | bytes 3145736 | tf_op jit(solution)/shard_map/ppermute | solution.py:92
  205.6 9.0 %collective-permute-start.43 = (bf16[2,4,80,256]{3,2,1,0:T(8,128)(2,1)S(1)}, bf16[2,4,80,256]{3,2,1,0:T(8,128)(2,1)S(1)}, u32[]{:S(2)}, u32[]{:S(2)}) collective-permute-start(bf16[2,4,80,256]{3,2,1,0:T(8,128)(2,1)S(1)} %get-tuple-element.257.refs_0_), channel_id=1, source_target_pairs={{0,2},{2,0},{4,6},{6,4},{8,10},{10,8},{12,14},{14,12},{16,18},{18,... | collective-permute-start | bytes 983048 | tf_op jit(solution)/shard_map/ppermute | solution.py:92
  206.4 8.7 %collective-permute-start.44 = (bf16[2,4,80,256]{3,2,1,0:T(8,128)(2,1)S(1)}, bf16[2,4,80,256]{3,2,1,0:T(8,128)(2,1)S(1)}, u32[]{:S(2)}, u32[]{:S(2)}) collective-permute-start(bf16[2,4,80,256]{3,2,1,0:T(8,128)(2,1)S(1)} %get-tuple-element.258.refs_2_), channel_id=1, source_target_pairs={{0,4},{2,6},{4,0},{6,2},{8,12},{10,14},{12,8},{14,10},{16,20},{18,... | collective-permute-start | bytes 983048 | tf_op jit(solution)/shard_map/ppermute | solution.py:92
  215.1 4.7 %collective-permute-start.47 = (bf16[2,2,4,80,512]{4,3,2,1,0:T(8,128)(2,1)S(1)}, bf16[2,2,4,80,512]{4,3,2,1,0:T(8,128)(2,1)S(1)}, u32[]{:S(2)}, u32[]{:S(2)}) collective-permute-start(bf16[2,2,4,80,512]{4,3,2,1,0:T(8,128)(2,1)S(1)} %get-tuple-element.264), channel_id=1, source_target_pairs={{0,1},{1,0},{2,3},{3,2},{4,5},{5,4},{6,7},{7,6},{8,9},{9,8},{10,11... | collective-permute-start | bytes 3932168 | tf_op jit(solution)/shard_map/ppermute | solution.py:92
  215.2 3.8 %collective-permute-start.48 = (f32[512,256]{1,0:T(8,128)S(1)}, f32[512,256]{1,0:T(8,128)S(1)}, u32[]{:S(2)}, u32[]{:S(2)}) collective-permute-start(f32[512,256]{1,0:T(8,128)S(1)} %get-tuple-element.271), channel_id=1, source_target_pairs={{0,1},{1,0},{2,3},{3,2},{4,5},{5,4},{6,7},{7,6},{8,9},{9,8},{10,11... | collective-permute-start | bytes 1572872 | tf_op jit(solution)/shard_map/ppermute | solution.py:92
  (15 other events, 27.2 us)

commit v3 on v2

--- a/solution.py
+++ b/solution.py
@@ -53,14 +53,15 @@
     def __init__(self):
         self.last = []
 
-    def run(self, body, name, micros, grid, ins, outs, prefetch=(), alias=None, room=32 * MIB):
+    def run(self, body, name, micros, grid, ins, outs, prefetch=(), alias=None, room=24 * MIB, scratch=()):
         count = len(prefetch) + len(ins)
         extra = self.last + ([] if alias is None else [alias])
         token = (8, 128)
 
         def wrapped(*refs):
-            refs[-1][...] = jnp.zeros(token, F32)
-            body(*refs[:count], *refs[count + len(extra) : -1])
+            held = len(refs) - len(scratch)
+            refs[held - 1][...] = jnp.zeros(token, F32)
+            body(*refs[:count], *refs[count + len(extra) : held - 1], *refs[held:])
 
         *results, last = pl.pallas_call(
             wrapped,
@@ -69,6 +70,7 @@
                 grid=grid,
                 in_specs=[spec for _, spec in ins] + [pl.BlockSpec(memory_space=pl.ANY)] * len(extra),
                 out_specs=[spec for _, _, spec, *_ in outs] + [pl.BlockSpec(token, lambda *_: (0, 0))],
+                scratch_shapes=scratch,
             ),
             out_shape=[
                 pltpu.HBM(shape, dtype) if far else jax.ShapeDtypeStruct(shape, dtype)
@@ -96,22 +98,26 @@
     return [swap(value, level, k) for k, value in enumerate(values, 1)]
 
 
+ALL = slice(None)
+BELOW = 16
+
+
 def stage_body(layout, cuts, *refs):
     sums, position = [], 0
     for number in layout:
         sums.append(refs[position : position + number])
         position += number
 
-    def piece(number, index, cols):
-        total = sums[number][0][index][:, cols]
+    def piece(number, index, cols, rows=ALL):
+        total = sums[number][0][index][rows, cols]
         for ref in sums[number][1:]:
-            total = total.astype(F32) + ref[index][:, cols].astype(F32)
+            total = total.astype(F32) + ref[index][rows, cols].astype(F32)
         return total
 
     for out_ref, sources in zip(refs[position:], cuts):
         for target, parts in sources:
-            for number, index, cols, row, col in parts:
-                value = piece(number, index, cols).astype(out_ref.dtype)
+            for number, index, cols, row, col, *rows in parts:
+                value = piece(number, index, cols, *rows).astype(out_ref.dtype)
                 where = target + (slice(row, row + value.shape[0]), slice(col, col + value.shape[1]))
                 out_ref[where] = value
 
@@ -138,9 +144,6 @@
     )
 
 
-ALL = slice(None)
-
-
 def split(number, value, axis, cols=ALL, width=None):
     lead = value.shape[:-2]
     rest = lead[:axis] + lead[axis + 1 :]
@@ -164,7 +167,17 @@
     return (shape, value.shape[-2], value.shape[-1], value.dtype, source)
 
 
-def sum_halves(line, keep, send, levels, out):
+def finish(line, sums, far, shape, dtype):
+    whole = [(0, (), ALL, 0, 0)]
+    for level in far:
+        outs = [((), *shape, kind, lambda index: whole) for kind in (F32, BF16)]
+        keep, send = stage(line, sums, outs)
+        sums = [(keep, [swap(send, level, k) for k in range(1, level[1])])]
+        yield
+    yield stage(line, sums, [((), *shape, dtype, lambda index: whole)])[0]
+
+
+def sum_halves(line, keep, send, levels, out, far=(), dtype=F32):
     received = swap(send, levels[0])
     yield
     rows, width = keep.shape[-2:]
@@ -196,8 +209,10 @@
         keep, *sends = stage(line, sums, outs)
         sums = [(keep, swaps(sends, level))]
         yield
-    out += stage(line, sums, [((), rows, width, F32, lambda index: [(0, (), ALL, 0, 0)])])
-    yield
+    for value in finish(line, sums, far, (rows, width), dtype):
+        if value is None:
+            yield
+    out.append(value)
 
 
 def gather_halves(line, value, levels, out):
@@ -240,31 +255,13 @@
     yield
 
 
-def finish(line, sums, far, rows):
-    for level in far:
-        outs = [((), rows, PANEL, dtype, lambda index: [(0, (), ALL, 0, 0)]) for dtype in (F32, BF16)]
-        keep, send = stage(line, sums, outs)
-        sums = [(keep, [swap(send, level, k) for k in range(1, level[1])])]
-        yield
-    yield stage(line, sums, [((), rows, PANEL, BF16, lambda index: [(0, (), ALL, 0, 0)])])[0]
-
-
 def all_sum(line, keep, send, near, far, out):
-    received = swap(send, near[0])
-    yield
-    rows = keep.shape[-2]
-    sums = [(keep, [received])]
-    for level in near[1:]:
-        keep, *sends = stage(line, sums, split(0, keep, 0))
-        sums = [(keep, swaps(sends, level))]
-        yield
-    for value in finish(line, sums, far, rows):
-        if value is None:
-            yield
-    yield from gather_halves(line, value, near, out)
-
-
-def all_sum_two(line, keep_a, send_a, keep_b, send_b, near, far, out):
+    mine = []
+    yield from sum_halves(line, keep, send, near, mine, far, BF16)
+    yield from gather_halves(line, mine[0], near, out)
+
+
+def all_sum_two(line, keep_a, send_a, keep_b, send_b, extra, near, far, out):
     got_a, got_b = swap(send_a, near[0]), swap(send_b, near[0])
     yield
     rows = keep_a.shape[-2]
@@ -276,15 +273,19 @@
     keep_a, send_a, keep_b, send_b = stage(line, [(keep_a, [got_a]), (keep_b, [got_b])], outs)
     sums = [(keep_a, [swap(send_a, near[2])]), (keep_b, [swap(send_b, near[1])])]
     yield
+    below = extra()
+    added = below.shape[0]
     for place, level in enumerate(near[3:]):
         if place == 0:
             lead = keep_a.shape[1:-2]
+            sums = sums + [(below, [])]
 
             def source(index, k):
-                return [(0, (k,) + index, ALL, 0, 0), (1, (k,) + index, ALL, rows, 0)]
+                places = [(0, (k,) + index, 0), (1, (k,) + index, rows), (2, (), 2 * rows)]
+                return [(number, where, ALL, row, 0) for number, where, row in places]
 
             outs = [
-                (lead, 2 * rows, PANEL, F32 if k == 0 else BF16, functools.partial(source, k=k))
+                (lead, 2 * rows + added, PANEL, F32 if k == 0 else BF16, functools.partial(source, k=k))
                 for k in range(level[1])
             ]
         else:
@@ -292,15 +293,38 @@
         keep, *sends = stage(line, sums, outs)
         sums = [(keep, swaps(sends, level))]
         yield
-    for value in finish(line, sums, far, 2 * rows):
-        if value is None:
-            yield
+    for level in far:
+        outs = [((), 2 * rows + added, PANEL, kind, lambda index: [(0, (), ALL, 0, 0)]) for kind in (F32, BF16)]
+        keep, send = stage(line, sums, outs)
+        sums = [(keep, [swap(send, level, k) for k in range(1, level[1])])]
+        yield
+    outs = [
+        ((), size, PANEL, BF16, lambda index, part=part: [(0, (), ALL, 0, 0, part)])
+        for size, part in ((2 * rows, slice(0, 2 * rows)), (added, slice(2 * rows, 2 * rows + added)))
+    ]
+    value, below = stage(line, sums, outs)
     for place, level in reversed(list(enumerate(near[3:]))):
         got = [swap(value, level, k) for k in range(1, level[1])]
         yield
         numbers = list(range(level[1]))
-        value = stage(line, [(part, []) for part in [value, *got]], [stacked(numbers, value, 0)])[0]
-    value_a, value_b = value[..., :rows, :], value[..., rows:, :]
+        parts = [(part, []) for part in [value, *got]]
+        if place:
+            value = stage(line, parts, [stacked(numbers, value, 0)])[0]
+            continue
+        lead = (level[1],) + value.shape[:-2]
+
+        def first(index):
+            return [(index[0], index[1:], ALL, 0, 0, slice(0, rows))]
+
+        def second(index):
+            number = int(np.ravel_multi_index(index, lead)) * BELOW % added
+            return [
+                (index[0], index[1:], ALL, 0, 0, slice(rows, 2 * rows)),
+                (len(numbers), (), ALL, rows, 0, slice(number, number + BELOW)),
+            ]
+
+        outs = [(lead, rows, PANEL, BF16, first), (lead, rows + BELOW, PANEL, BF16, second)]
+        value_a, value_b = stage(line, parts + [(below, [])], outs)
     got_a, got_b = swap(value_a, near[2]), swap(value_b, near[1])
     yield
     sums = [(part, []) for part in (value_a, got_a, value_b, got_b)]
@@ -340,46 +364,39 @@
     return jnp.dot(left, right, preferred_element_type=F32)
 
 
-def scatter_some(first, ids_ref, grad, proj_ref, table_ref, pooled_ref):
+def scatter_body(first, ids_ref, grad_ref, proj_ref, table_ref, pooled_ref, flat_ref):
+    @pl.when(pl.program_id(0) == 0)
+    def _():
+        flat_ref[...] = grad_ref[...].reshape(flat_ref.shape)
+
     rows = table_ref.shape[0]
     base = first + pl.program_id(0) * rows
     picks = [selector(ids_ref[row : row + 1], base, rows) for row in range(ids_ref.shape[0])]
-    part = nt(jnp.concatenate(picks, axis=1), grad).astype(BF16)
+    part = nt(jnp.concatenate(picks, axis=1), flat_ref[...]).astype(BF16)
     table_ref[...] = part
     pooled_ref[...] = nt(part, proj_ref[...]).astype(pooled_ref.dtype)
 
 
-def scatter_first_body(first, ids_ref, grad_ref, proj_ref, table_ref, pooled_ref, flat_ref):
-    @pl.when(pl.program_id(0) == 0)
-    def _():
-        flat_ref[...] = grad_ref[...].reshape(flat_ref.shape)
-
-    scatter_some(first, ids_ref, flat_ref[...], proj_ref, table_ref, pooled_ref)
-
-
-def scatter_body(first, ids_ref, flat_ref, proj_ref, table_ref, pooled_ref):
-    scatter_some(first, ids_ref, flat_ref[...], proj_ref, table_ref, pooled_ref)
-
-
 def scatter_rows(line, ids, grad, w_proj, first, count, dtype):
     features = grad.shape[0]
-    tokens = ids.size
     width = w_proj.shape[0]
     rows = min(512, count)
-    flat = (features, tokens)
-    fresh = grad.ndim == 3
-    return line.run(
-        functools.partial(scatter_first_body if fresh else scatter_body, first),
+    return line.run(
+        functools.partial(scatter_body, first),
         "scatter_rows",
         14,
         (count // rows,),
-        [(ids, fixed(ids.shape)), (grad, pl.BlockSpec(memory_space=pltpu.VMEM)), (w_proj, fixed(w_proj.shape))],
+        [
+            (ids, fixed(ids.shape)),
+            (grad, pl.BlockSpec(memory_space=pltpu.VMEM)),
+            (w_proj, fixed(w_proj.shape)),
+        ],
         [
             ((count, features), BF16, rows_of(rows, features), FAR),
             ((count, width), dtype, rows_of(rows, width)),
-        ]
-        + ([(flat, BF16, pl.BlockSpec(memory_space=pltpu.VMEM))] if fresh else []),
-        room=44 * MIB,
+        ],
+        room=28 * MIB,
+        scratch=[pltpu.VMEM((features, ids.size), BF16)],
     )
 
 
@@ -455,23 +472,23 @@
     out_ref[...] = total.astype(BF16).reshape(out_ref.shape)
 
 
-def lookup(line, ids, tables, part, count, before=None):
+def lookup(line, ids, tables, part, before=None):
     rows, text_len = ids.shape
     features, vocab = tables[0].shape
-    block = math.gcd(text_len // count, 256)
-    steps = text_len // count // block
+    block = text_len // 8
+    first, last = part
     return line.run(
         functools.partial(lookup_body, min(vocab, 4096)),
         "lookup",
-        6,
-        (steps,),
-        [(ids, pl.BlockSpec((rows, block), lambda i, *_: (0, i + part * steps)))]
+        3 * (last - first),
+        (last - first,),
+        [(ids, pl.BlockSpec((rows, block), lambda i, *_: (0, i + first)))]
         + [(table, fixed(table.shape)) for table in tables],
         [
             (
                 (features, rows, text_len),
                 BF16,
-                pl.BlockSpec((features, rows, block), lambda i, *_: (0, 0, i + part * steps)),
+                pl.BlockSpec((features, rows, block), lambda i, *_: (0, 0, i + first)),
                 FAR,
             )
         ],
@@ -480,24 +497,21 @@
 
 
 PANEL = 512
-EXTRA = 16
-
-
-def store_slots(slots_ref, first, part, keep_ref, send_ref, rows=None, base=0):
-    rows = rows or keep_ref.shape[1]
-    half = keep_ref.shape[0]
-    where = slice(base, base + rows)
+
+
+def store_slots(slots_ref, first, part, keep_ref, send_ref):
+    half, rows, _ = keep_ref.shape
     for j in range(part.shape[0] // rows):
         slot = slots_ref[first + j]
         piece = part[j * rows : (j + 1) * rows]
 
         @pl.when(slot < half)
         def _():
-            keep_ref[slot, where] = piece
+            keep_ref[slot] = piece
 
         @pl.when(slot >= half)
         def _():
-            send_ref[slot - half, where] = piece.astype(BF16)
+            send_ref[slot - half] = piece.astype(BF16)
 
 
 def weight_body(slots_ref, left_ref, right_ref, keep_ref, send_ref):
@@ -518,27 +532,17 @@
         store_slots(slots_ref, step * each, tn(second_ref[...], right_ref[...]), keep_ref, send_ref)
 
 
-def two_weights_body(
-    last, slots_ref, left_ref, right_ref, left2_ref, right2_ref, small_ref, keep_ref, send_ref
-):
+def two_weights_body(last, slots_ref, left_ref, right_ref, left2_ref, right2_ref, keep_ref, send_ref):
     step = pl.program_id(0)
-    rows = keep_ref.shape[1] - EXTRA
-    each = left_ref.shape[1] // rows
+    each = left_ref.shape[1] // keep_ref.shape[1]
 
     @pl.when(step < last)
     def _():
-        store_slots(slots_ref, step * each, tn(left_ref[...], right_ref[...]), keep_ref, send_ref, rows)
+        store_slots(slots_ref, step * each, tn(left_ref[...], right_ref[...]), keep_ref, send_ref)
 
     @pl.when(step == last)
     def _():
-        part = tn(left2_ref[...], right2_ref[...])
-        store_slots(slots_ref, step * each, part, keep_ref, send_ref, rows)
-        top = lax.broadcasted_iota(jnp.int32, (EXTRA, 1), 0) == 0
-        for chunk in range(2 * keep_ref.shape[0]):
-            piece = jnp.zeros((EXTRA, PANEL), F32)
-            if chunk < small_ref.shape[0]:
-                piece = jnp.where(top, small_ref[chunk : chunk + 1], 0.0)
-            store_slots(slots_ref, chunk, piece, keep_ref, send_ref, EXTRA, rows)
+        store_slots(slots_ref, step * each, tn(left2_ref[...], right2_ref[...]), keep_ref, send_ref)
 
 
 def slot_outs(count, rows):
@@ -581,7 +585,7 @@
     )
 
 
-def two_weights(line, slots, left, right, left2, right2, small):
+def two_weights(line, slots, left, right, left2, right2):
     depth, cols = right.shape
     last = cols // PANEL
     return line.run(
@@ -594,9 +598,8 @@
             (right, pl.BlockSpec((depth, PANEL), lambda i, *_: (0, jnp.minimum(i, last - 1)))),
             (left2, fixed(left2.shape)),
             (right2, fixed(right2.shape)),
-            (small, fixed(small.shape)),
-        ],
-        slot_outs(slots.shape[0], (last + 1) * left.shape[1] // slots.shape[0] + EXTRA),
+        ],
+        slot_outs(slots.shape[0], (last + 1) * left.shape[1] // slots.shape[0]),
         [slots],
     )
 
@@ -621,10 +624,56 @@
     load_slots(slots_ref, pl.program_id(0) * each, own_ref, other_ref, out_ref, rows)
 
 
-def unpack_two_body(last, slots_ref, own_ref, other_ref, out_ref, out2_ref, small_ref):
+def unpack(line, slots, own, other, height):
+    tile = min(512, height)
+    return line.run(
+        unpack_body,
+        "unpack",
+        5,
+        (height // tile,),
+        [(own, fixed(own.shape)), (other, fixed(other.shape))],
+        [((height, PANEL), F32, pl.BlockSpec((tile, PANEL), lambda i, *_: (i, 0)), FAR)],
+        [slots],
+    )[0]
+
+
+def unpack_extra_body(rows, inner, slots_ref, own_ref, other_ref, out_ref, *extra_refs):
+    each = out_ref.shape[0] // rows
+    load_slots(slots_ref, pl.program_id(0) * each, own_ref, other_ref, out_ref, rows)
+
+    @pl.when(pl.program_id(0) == 0)
+    def _():
+        needed = sum(ref.shape[0] for ref in extra_refs)
+        sums = []
+        for place in range((needed + BELOW - 1) // BELOW):
+            total = jnp.zeros((BELOW, PANEL), F32)
+            for ref in (own_ref, other_ref):
+                for slot in range(place, ref.shape[0], inner):
+                    total += ref[slot, rows:].astype(F32)
+            sums.append(total)
+        total = jnp.concatenate(sums, axis=0)
+        first = 0
+        for ref in extra_refs:
+            ref[...] = total[first : first + ref.shape[0]]
+            first += ref.shape[0]
+
+
+def unpack_extra(line, slots, own, other, height, cols, extra, inner):
+    return line.run(
+        functools.partial(unpack_extra_body, height * cols // PANEL // slots.shape[0], inner),
+        "unpack",
+        5,
+        (cols // PANEL,),
+        [(own, fixed(own.shape)), (other, fixed(other.shape))],
+        [((height, cols), F32, pl.BlockSpec((height, PANEL), lambda i, *_: (0, i)), FAR)]
+        + [((rows, PANEL), F32, fixed((rows, PANEL))) for rows in extra],
+        [slots],
+    )
+
+
+def unpack_two_body(last, slots_ref, own_ref, other_ref, out_ref, out2_ref):
     step = pl.program_id(0)
-    half, rows, _ = own_ref.shape
-    rows -= EXTRA
+    rows = own_ref.shape[1]
     each = out_ref.shape[0] // rows
 
     @pl.when(step < last)
@@ -634,34 +683,9 @@
     @pl.when(step == last)
     def _():
         load_slots(slots_ref, step * each, own_ref, other_ref, out2_ref, rows)
-        for chunk in range(small_ref.shape[0]):
-            slot = slots_ref[chunk]
-
-            @pl.when(slot < half)
-            def _():
-                small_ref[chunk : chunk + 1] = own_ref[slot, rows:].astype(F32)[:1]
-
-            @pl.when(slot >= half)
-            def _():
-                small_ref[chunk : chunk + 1] = other_ref[slot - half, rows:].astype(F32)[:1]
-
-
-def unpack(line, slots, own, other, height, cols):
-    tall = cols == PANEL
-    tile = 512
-    index = (lambda i, *_: (i, 0)) if tall else (lambda i, *_: (0, i))
-    return line.run(
-        unpack_body,
-        "unpack",
-        5,
-        (height * cols // (tile * PANEL),),
-        [(own, fixed(own.shape)), (other, fixed(other.shape))],
-        [((height, cols), F32, pl.BlockSpec((tile if tall else height, PANEL), index), FAR)],
-        [slots],
-    )[0]
-
-
-def unpack_two(line, slots, own, other, height, cols, small):
+
+
+def unpack_two(line, slots, own, other, height, cols):
     last = cols // PANEL
     return line.run(
         functools.partial(unpack_two_body, last),
@@ -677,7 +701,6 @@
                 FAR,
             ),
             ((height, PANEL), F32, fixed((height, PANEL)), FAR),
-            (small, F32, fixed(small)),
         ],
         [slots],
     )
@@ -1052,7 +1075,7 @@
     total = entries * slots
     rows = math.gcd(total, 256)
     some = rows // slots
-    small = ((script_table.shape[0] + 2 + 7) // 8 * 8, width)
+    small = ((script_table.shape[0] + 2 + 15) // 16 * 16, width)
     return line.run(
         attn_back_body,
         "attn_back",
@@ -1073,6 +1096,9 @@
             (small, F32, fixed(small)),
         ],
     )
+
+
+PLAN = ("f t T f", "03 t f", "36 t f", "68 t f t", "w t E F", "Q")
 
 
 def per_device(
@@ -1123,15 +1149,13 @@
         shape = tuple(size for _, size, _ in some[1:]) + keep.shape[-2:]
         return keep.reshape(shape), send.reshape(shape)
 
-    flat_grad = out_grad
     parts, pooled_grads = [], []
     for chunk in range(chunks):
         first = chunk * span
-        part_send, send, *flat = scatter_rows(
-            line, slot_ids, flat_grad, w_proj, first + span // 2, span // 2, BF16
+        part_send, send = scatter_rows(
+            line, slot_ids, out_grad, w_proj, first + span // 2, span // 2, BF16
         )
-        flat_grad = flat[0] if flat else flat_grad
-        part_keep, keep = scatter_rows(line, slot_ids, flat_grad, w_proj, first, span // 2, F32)
+        part_keep, keep = scatter_rows(line, slot_ids, out_grad, w_proj, first, span // 2, F32)
         parts.append((part_keep, part_send))
         shape = sizes[1:] + (each, width)
         pooling = sum_halves(line, keep.reshape(shape), send.reshape(shape), levels, pooled_grads)
@@ -1176,13 +1200,19 @@
     )
     spread_on()
     up = wide_weight(line, slot_index, normed_ffn, grad_up)
-    ffn_all, two_all = [], []
-    ffn_sum = all_sum_two(line, *cut_up(*down, near), *cut_up(*up, near), near, far, ffn_all)
+    small, ffn_all, two_all = [], [], []
+    ffn_sum = all_sum_two(
+        line, *cut_up(*down, near), *cut_up(*up, near), lambda: small[0], near, far, ffn_all
+    )
     next(ffn_sum)
     spread_on()
     grad_mixed = heads_back(line, length_rows, w_out, mixed, grad_branch, slots)
     next(ffn_sum)
-    grad_pieces, small = attn_back(
+    two = two_weights(line, slot_index, normed, grad_mixed, context, grad_branch)
+    two_sum = all_sum(line, *cut_up(*two, near), near, far, two_all)
+    next(two_sum)
+    spread_on()
+    grad_pieces, part_small = attn_back(
         line,
         pieces,
         script_rows,
@@ -1193,48 +1223,72 @@
         grad_middle,
         part_gain_ffn,
     )
-    spread_on()
-    two = two_weights(line, slot_index, normed, grad_mixed, context, grad_branch, small)
-    two_sum = all_sum(line, *cut_up(*two, near), near, far, two_all)
-    next(two_sum)
-    tables, part_proj = [], None
-    for chunk in range(chunks):
-        for _ in spreads[chunk]:
+    small.append(part_small)
+    results = {}
+
+    def make_table():
+        tables, total = [], None
+        for chunk in range(chunks):
+            for _ in spreads[chunk]:
+                pass
+            own, other = (value.reshape(span // 2, width) for value in halves[chunk])
+            table, part = table_and_grad(line, own, other, w_proj, *parts[chunk])
+            tables.append(table)
+            total = part if total is None else total + part
+        results["tables"] = tables
+        results["proj"] = total, swap(total, levels[0])
+
+    def look_up(first, last):
+        before = results.get("looked_up")
+        results["looked_up"] = lookup(line, slot_ids, results["tables"], (first, last), before)
+
+    def add_proj():
+        total, other = results["proj"]
+        whole = [((), width, features, F32, lambda index: [(0, (), ALL, 0, 0)])]
+        results["w_proj"] = stage(line, [(total, [other])], whole)[0]
+
+    def end_ffn():
+        results["w_down"] = unpack(line, slot_index, *map(merge, ffn_all[:2]), w_down.shape[0])
+        results["w_up"], *results["small"] = unpack_extra(
+            line,
+            slot_index,
+            *map(merge, ffn_all[2:]),
+            *w_up.shape,
+            (script_table.shape[0], 1, 1),
+            math.prod(sizes[3:cut]),
+        )
+
+    def end_two():
+        for _ in two_sum:
             pass
-        own, other = halves[chunk]
-        table, part = table_and_grad(
-            line, own.reshape(span // 2, width), other.reshape(span // 2, width), w_proj, *parts[chunk]
+        results["w_qkv"], results["w_out"] = unpack_two(
+            line, slot_index, *map(merge, two_all), *w_qkv.shape
         )
-        tables.append(table)
-        part_proj = part if part_proj is None else part_proj + part
-    grad_w_proj = part_proj + swap(part_proj, levels[0])
-    looked_up = None
-    order = [(ffn_sum, two_sum), (ffn_sum,), (two_sum,), (ffn_sum, two_sum), (ffn_sum,)]
-    for part, going in enumerate(order):
-        for steps in going:
-            next(steps, 0)
-        if part < 4:
-            looked_up = lookup(line, slot_ids, tables, part, 4, looked_up)
-    next(two_sum, 0)
-    next(ffn_sum, 0)
-    next(two_sum, 0)
-    for _ in ffn_sum:
-        pass
-    next(two_sum, 0)
-    grad_w_down = unpack(line, slot_index, merge(ffn_all[0]), merge(ffn_all[1]), *w_down.shape)
-    grad_w_up = unpack(line, slot_index, merge(ffn_all[2]), merge(ffn_all[3]), *w_up.shape)
-    for _ in two_sum:
-        pass
-    grad_w_qkv, grad_w_out, small = unpack_two(
-        line, slot_index, *map(merge, two_all), *w_qkv.shape, small.shape
-    )
-    groups = script_table.shape[0]
+
+    acts = {
+        "f": lambda: next(ffn_sum, 0),
+        "t": lambda: next(two_sum, 0),
+        "T": make_table,
+        "w": add_proj,
+        "E": lambda: list(ffn_sum),
+        "F": end_ffn,
+        "Q": end_two,
+    }
+    for act in (act for part in PLAN for act in part.split()):
+        if act.isdigit():
+            look_up(int(act[0]), int(act[1]))
+        else:
+            acts[act]()
+    looked_up, grad_w_proj = results["looked_up"], results["w_proj"]
+    grad_w_down, grad_w_up = results["w_down"], results["w_up"]
+    grad_w_qkv, grad_w_out = results["w_qkv"], results["w_out"]
+    grad_script, grad_gain_attn, grad_gain_ffn = results["small"]
     return (
         looked_up,
         grad_pieces,
-        small[:groups],
-        small[groups],
-        small[groups + 1],
+        grad_script,
+        grad_gain_attn.reshape(width),
+        grad_gain_ffn.reshape(width),
         grad_w_qkv,
         grad_w_out,
         grad_w_up,

time: 226 us -> 211 us (0.934)
  waiting for transfers between devices: 35.5 us -> 20.9 us
  starting transfers between devices: 52.2 us -> 56.6 us
    ppermute x49 -> x51, waiting for transfers between devices: 35.5 us -> 20.9 us  [swap(): lax.ppermute(value, name, [(i, i ^ k << shift) for i in range(count)])]
    ppermute x49 -> x51, starting transfers between devices: 52.2 us -> 56.6 us  [swap(): lax.ppermute(value, name, [(i, i ^ k << shift) for i in range(count)])]
    unnamed x60 -> x46, local copies, waits for them, and re-layouts: 7.75 us -> 7.51 us
  transfers between devices with their start and end apart: 49 -> 51, of which waited for: 20 -> 13; matrix products, arithmetic and copies ran while one was open for 1% -> 0% of each run, Pallas kernels for 46% -> 50%
where the time goes in v3:
time: 211 us; the launch traced here: 210 us
  Pallas kernels  122 us (58%)
  starting transfers between devices  56.6 us (27%)
  waiting for transfers between devices  20.9 us (10%)
  local copies, waits for them, and re-layouts  8.16 us (4%)
    pallas_call x41, Pallas kernels, run(): pl.pallas_call(wrapped, grid_spec=pltpu.PrefetchScalarGridSpec(num_scalar...  122 us
    ppermute x51, starting transfers between devices, swap(): lax.ppermute(value, name, [(i, i ^ k << shift) for i in range(count)])  56.6 us
    ppermute x51, waiting for transfers between devices, swap(): lax.ppermute(value, name, [(i, i ^ k << shift) for i in range(count)])  20.9 us
    unnamed x46, local copies, waits for them, and re-layouts  7.51 us
  transfers between devices with their start and end apart: 51, of which 13 were waited for; matrix products, arithmetic and copies ran while one was open for 0% of the time, Pallas kernels for 50%

profile of v3, /device:TPU:0, one launch (start us, length us, event | category | flops | bytes accessed | tf_op | source)
XLA Modules:
  0.0 210.4 jit_solution(14029840444720125027)
XLA Ops:
  0.6 1.0 fusion.2.refs_0_
  1.7 2.2 %copy-done = bf16[256,4,2048]{2,1,0:T(4,128)(2,1)S(1)} copy-done((bf16[256,4,2048]{2,1,0:T(4,128)(2,1)S(1)}, bf16[256,4,2048]{2,1,0:T(4,128)(2,1)}, u32[]{:S(2)}) %copy-start) | copy-done | bytes 4194328
  3.9 0.9 copy-done.9
  4.8 12.8 %scatter_rows.2 = (bf16[2048,256]{1,0:T(8,128)(2,1)}, bf16[2048,512]{1,0:T(8,128)(2,1)}, f32[8,128]{1,0:T(8,128)S(1)}) custom-call(s32[4,2048]{1,0:T(4,128)S(1)} %fusion.2.refs_0_, bf16[256,4,2048]{2,1,0:T(4,128)(2,1)S(1)} %copy-done, bf16[512,256]{1,0:T(8,128)(2,1)S(1)} %copy-done.9), custom_call_target="tpu_custom_call" | custom-call | flops 41999998976 | bytes 126000000 | tf_op jit(solution)/shard_map/scatter_rows/pallas_call | solution.py:66
  18.8 2.2 %copy-done.1 = bf16[256,4,2048]{2,1,0:T(4,128)(2,1)S(1)} copy-done((bf16[256,4,2048]{2,1,0:T(4,128)(2,1)S(1)}, bf16[256,4,2048]{2,1,0:T(4,128)(2,1)}, u32[]{:S(2)}) %copy-start.1) | copy-done | bytes 4194328
  21.0 12.4 %scatter_rows.3 = (bf16[2048,256]{1,0:T(8,128)(2,1)}, f32[2048,512]{1,0:T(8,128)S(1)}, f32[8,128]{1,0:T(8,128)S(1)}) custom-call(s32[4,2048]{1,0:T(4,128)S(1)} %fusion.2.refs_0_, bf16[256,4,2048]{2,1,0:T(4,128)(2,1)S(1)} %copy-done.1, bf16[512,256]{1,0:T(8,128)(2,1)S(1)} %copy-done.10, f32[8,128]{1,0:T(8,128)S(1)} %get-tuple-element.148.refs_3_), custom_call_target="tpu_custom_call" | custom-call | flops 41999998976 | bytes 126000000 | tf_op jit(solution)/shard_map/scatter_rows/pallas_call | solution.py:66
  33.9 2.5 %collective-permute-start.1 = (bf16[2,4,128,256]{3,2,1,0:T(8,128)(2,1)S(1)}, bf16[2,4,128,256]{3,2,1,0:T(8,128)(2,1)S(1)}, u32[]{:S(2)}, u32[]{:S(2)}) collective-permute-start(bf16[2,4,128,256]{3,2,1,0:T(8,128)(2,1)S(1)} %get-tuple-element.156), channel_id=1, source_target_pairs={{0,2},{2,0},{4,6},{6,4},{8,10},{10,8},{12,14},{14,12},{16,18},{18,... | collective-permute-start | bytes 1572872 | tf_op jit(solution)/shard_map/ppermute | solution.py:94
  36.5 1.5 collective-permute-start.2
  38.0 11.2 %attn_forward.1 = (bf16[1024,512]{1,0:T(8,128)(2,1)S(1)}, bf16[1024,1536]{1,0:T(8,128)(2,1)}, bf16[1024,512]{1,0:T(8,128)(2,1)S(1)}, f32[1024,512]{1,0:T(8,128)S...) custom-call(bf16[128,8,512]{2,1,0:T(8,128)(2,1)S(1)} %copy-done.6, ...), custom_call_target="tpu_custom_call" | custom-call | flops 35999997952 | bytes 108000000 | tf_op jit(solution)/shard_map/attn_forward/pallas_call | solution.py:66
  49.3 1.3 collective-permute-done.2.refs_3_
  50.8 1.6 collective-permute-start.3
  52.9 8.0 %ffn_forward.2 = (f32[1024,1024]{1,0:T(8,128)}, bf16[128,1024]{1,0:T(8,128)(2,1)S(1)}, f32[128,512]{1,0:T(8,128)S(1)}, f32[8,128]{1,0:T(8,128)S(1)}) custom-call(s32[1024,1]{1,0:T(8,128)S(1)} %broadcast_in_dim_reshape.8.refs_2_.refs_0_.refs_1_, s32[128,1]{1,0:T(8,128)S(1)} %copy.32.refs_1_, f32[1024,512]{1,0:T(8,128)S(1)} %get-tuple-element.153.refs_2_.refs_4_, ...), custom_call_target="tpu_custom_call" | custom-call | flops 20999999488 | bytes 63000000 | tf_op jit(solution)/shard_map/ffn_forward/pallas_call | solution.py:66
  61.0 1.6 collective-permute-start.5
  62.6 2.6 %collective-permute-start.6 = (bf16[128,512]{1,0:T(8,128)(2,1)S(1)}, bf16[128,512]{1,0:T(8,128)(2,1)S(1)}, u32[]{:S(2)}, u32[]{:S(2)}) collective-permute-start(bf16[128,512]{1,0:T(8,128)(2,1)S(1)} %get-tuple-element.171), channel_id=1, source_target_pairs={{0,16},{2,18},{4,20},{6,22},{8,24},{10,26},{12,28},{14,30},{16,0},... | collective-permute-start | bytes 393224 | tf_op jit(solution)/shard_map/ppermute | solution.py:94
  65.4 8.0 %ffn_forward.3 = (f32[1024,1024]{1,0:T(8,128)}, bf16[128,1024]{1,0:T(8,128)(2,1)S(1)}, bf16[128,512]{1,0:T(8,128)(2,1)S(1)}, f32[8,128]{1,0:T(8,128)S(1)}) custom-call(s32[1024,1]{1,0:T(8,128)S(1)} %broadcast_in_dim_reshape.8.refs_2_.refs_0_.refs_1_, s32[128,1]{1,0:T(8,128)S(1)} %copy.32.refs_1_, f32[128,512]{1,0:T(8,128)S(1)} %get-tuple-element.161.refs_2_, ...), custom_call_target="tpu_custom_call" | custom-call | flops 20999999488 | bytes 63000000 | tf_op jit(solution)/shard_map/ffn_forward/pallas_call | solution.py:66
  73.4 1.6 collective-permute-done.6.refs_2_
  75.1 2.5 %collective-permute-start.10 = (bf16[128,512]{1,0:T(8,128)(2,1)S(1)}, bf16[128,512]{1,0:T(8,128)(2,1)S(1)}, u32[]{:S(2)}, u32[]{:S(2)}) collective-permute-start(bf16[128,512]{1,0:T(8,128)(2,1)S(1)} %get-tuple-element.175.refs_0_), channel_id=1, source_target_pairs={{0,24},{2,26},{4,28},{6,30},{8,16},{10,18},{12,20},{14,22},{16,8},... | collective-permute-start | bytes 393224 | tf_op jit(solution)/shard_map/ppermute | solution.py:94
  77.6 1.1 collective-permute-start.8
  79.6 2.7 %tall_weight.1 = (f32[16,64,512]{2,1,0:T(8,128)S(1)}, bf16[16,64,512]{2,1,0:T(8,128)(2,1)S(1)}, f32[8,128]{1,0:T(8,128)S(1)}) custom-call(s32[32]{0:T(128)S(1)} %iota_xor_fusion.refs_0_, bf16[128,1024]{1,0:T(8,128)(2,1)S(1)} %get-tuple-element.179.refs_1_, bf16[128,1024]{1,0:T(8,128)(2,1)S(1)} %get-tuple-element.180.refs_2_, ...), custom_call_target="tpu_custom_call" | custom-call | flops 8999999488 | bytes 27000000 | tf_op jit(solution)/shard_map/tall_weight/pallas_call | solution.py:66
  83.1 6.8 %ffn_back.1 = (bf16[1024,2048]{1,0:T(8,128)(2,1)S(1)}, f32[1024,512]{1,0:T(8,128)S(1)}, bf16[1024,512]{1,0:T(8,128)(2,1)S(1)}, f32[1,512]{1,0:T(1,128)S(1)}, f32[8,128]{1,0:T(8,128)S(1)}) custom-call(f32[128,512]{1,0:T(8,128)S(1)} %get-tuple-element.176.refs_0_, s32[1024,1]{1,0:T(8,128)S(1)} %broadcast_in_dim_reshape.8.refs_2_.refs_0_.refs_1_, ...), custom_call_target="tpu_custom_call" | custom-call | flops 44999999488 | bytes 135000000 | tf_op jit(solution)/shard_map/ffn_back/pallas_call | solution.py:66
  90.0 1.6 collective-permute-start.11
  92.2 4.4 %wide_weight.1 = (f32[16,64,512]{2,1,0:T(8,128)S(1)}, bf16[16,64,512]{2,1,0:T(8,128)(2,1)S(1)}, f32[8,128]{1,0:T(8,128)S(1)}) custom-call(s32[32]{0:T(128)S(1)} %iota_xor_fusion.refs_0_, bf16[1024,512]{1,0:T(8,128)(2,1)S(1)} %get-tuple-element.154.refs_3_.refs_1_, bf16[1024,2048]{1,0:T(8,128)(2,1)S(1)} %get-tuple-element.186.refs_2_, ...), custom_call_target="tpu_custom_call" | custom-call | flops 24000000000 | bytes 72000000 | tf_op jit(solution)/shard_map/wide_weight/pallas_call | solution.py:66
  96.7 1.4 collective-permute-done.11.refs_1_
  98.1 1.3 collective-permute-done.12.refs_3_
  101.2 6.3 %heads_back.1 = (bf16[1024,1536]{1,0:T(8,128)(2,1)S(1)}, f32[8,128]{1,0:T(8,128)S(1)}) custom-call(s32[1024,1]{1,0:T(8,128)S(1)} %broadcast_in_dim_reshape.8.refs_2_.refs_0_.refs_1_, bf16[512,512]{1,0:T(8,128)(2,1)S(1)} %copy-done.8, bf16[1024,1536]{1,0:T(8,128)(2,1)S(1)} %copy-done.20, bf16[1024,512]{1,0:T(8,128)(2,1)S(1)} %get-tuple-element.193.refs_3_.refs_4_, ...), custom_call_target="tpu_custom_call" | custom-call | flops 38999998464 | bytes 117000000 | tf_op jit(solution)/shard_map/heads_back/pallas_call | solution.py:66
  108.7 1.5 collective-permute-start.20
  110.2 4.3 %two_weights.1 = (f32[16,64,512]{2,1,0:T(8,128)S(1)}, bf16[16,64,512]{2,1,0:T(8,128)(2,1)S(1)}, f32[8,128]{1,0:T(8,128)S(1)}) custom-call(s32[32]{0:T(128)S(1)} %iota_xor_fusion.refs_0_, bf16[1024,512]{1,0:T(8,128)(2,1)S(1)} %get-tuple-element.191.refs_1_, bf16[1024,1536]{1,0:T(8,128)(2,1)S(1)} %get-tuple-element.195.refs_2_.refs_5_, ...), custom_call_target="tpu_custom_call" | custom-call | flops 15000000512 | bytes 45000000 | tf_op jit(solution)/shard_map/two_weights/pallas_call | solution.py:66
  115.4 1.0 copy-done.5
  116.6 6.8 %attn_back.1 = (f32[128,8,512]{2,1,0:T(8,128)}, f32[32,512]{1,0:T(8,128)S(1)}, f32[8,128]{1,0:T(8,128)S(1)}) custom-call(bf16[128,8,512]{2,1,0:T(8,128)(2,1)S(1)} %copy-done.7, s32[1024,1]{1,0:T(8,128)S(1)} %broadcast_in_dim_reshape.9.refs_1_, f32[16,512]{1,0:T(8,128)S(1)} %copy-done.12, f32[1,512]{1,0:T(1,128)S(1)} %bitcast.38, ...), custom_call_target="tpu_custom_call" | custom-call | flops 27000000512 | bytes 81000000 | tf_op jit(solution)/shard_map/attn_back/pallas_call | solution.py:66
  123.7 1.0 collective-permute-start.21
  124.7 1.1 collective-permute-start.22
  126.0 1.0 collective-permute-start.26
  127.1 1.1 collective-permute-start.27
  128.2 3.3 %table_and_grad.1 = (bf16[256,4096]{1,0:T(8,128)(2,1)S(1)}, f32[512,256]{1,0:T(8,128)S(1)}, f32[8,128]{1,0:T(8,128)S(1)}) custom-call(bf16[2048,512]{1,0:T(8,128)(2,1)S(1)} %bitcast.24, bf16[2048,512]{1,0:T(8,128)(2,1)S(1)} %bitcast.25, bf16[512,256]{1,0:T(8,128)(2,1)S(1)} %copy-done.10, bf16[2048,256]{1,0:T(8,128)(2,1)S(1)} %copy-done.19, ...), custom_call_target="tpu_custom_call" | custom-call | flops 15000000512 | bytes 45000000 | tf_op jit(solution)/shard_map/table_and_grad/pallas_call | solution.py:66
  131.4 1.5 collective-permute-done.21.refs_1_
  133.0 1.0 collective-permute-done.22.refs_3_
  134.1 1.1 collective-permute-start.23
  135.2 2.0 collective-permute-start.24
  137.2 1.4 collective-permute-start.25
  138.6 8.1 %lookup.3 = (bf16[256,4,2048]{2,1,0:T(4,128)(2,1)}, f32[8,128]{1,0:T(8,128)S(1)}) custom-call(s32[4,2048]{1,0:T(4,128)S(1)} %fusion.2.refs_0_, bf16[256,4096]{1,0:T(8,128)(2,1)S(1)} %get-tuple-element.219.refs_1_, f32[8,128]{1,0:T(8,128)S(1)} %get-tuple-element.234.refs_2_), custom_call_target="tpu_custom_call" | custom-call | flops 27000000512 | bytes 81000000 | tf_op jit(solution)/shard_map/lookup/pallas_call | solution.py:66
  146.8 1.1 collective-permute-start.31
  148.0 1.5 collective-permute-start.32
  149.5 1.1 collective-permute-start.28
  150.7 1.9 collective-permute-start.29
  152.6 1.4 collective-permute-start.30
  154.0 8.2 %lookup.4 = (bf16[256,4,2048]{2,1,0:T(4,128)(2,1)}, f32[8,128]{1,0:T(8,128)S(1)}) custom-call(s32[4,2048]{1,0:T(4,128)S(1)} %fusion.2.refs_0_, bf16[256,4096]{1,0:T(8,128)(2,1)S(1)} %get-tuple-element.219.refs_1_, f32[8,128]{1,0:T(8,128)S(1)} %get-tuple-element.243.refs_2_, ...), custom_call_target="tpu_custom_call", output_to_operand_aliasing={{0}: (3, {})} | custom-call | flops 27000000512 | bytes 81000000 | tf_op jit(solution)/shard_map/lookup/pallas_call | solution.py:66
  162.5 2.8 %collective-permute-start.36 = (bf16[64,512]{1,0:T(8,128)(2,1)S(1)}, bf16[64,512]{1,0:T(8,128)(2,1)S(1)}, u32[]{:S(2)}, u32[]{:S(2)}) collective-permute-start(bf16[64,512]{1,0:T(8,128)(2,1)S(1)} %get-tuple-element.255), channel_id=1, source_target_pairs={{0,16},{2,18},{4,20},{6,22},{8,24},{10,26},{12,28},{14,30},{16,0},... | collective-permute-start | bytes 196616 | tf_op jit(solution)/shard_map/ppermute | solution.py:94
  165.3 1.4 collective-permute-start.37
  167.4 1.0 collective-permute-start.33
  168.3 5.7 %lookup.5 = (bf16[256,4,2048]{2,1,0:T(4,128)(2,1)}, f32[8,128]{1,0:T(8,128)S(1)}) custom-call(s32[4,2048]{1,0:T(4,128)S(1)} %fusion.2.refs_0_, bf16[256,4096]{1,0:T(8,128)(2,1)S(1)} %get-tuple-element.219.refs_1_, f32[8,128]{1,0:T(8,128)S(1)} %get-tuple-element.247.refs_2_, ...), custom_call_target="tpu_custom_call", output_to_operand_aliasing={{0}: (3, {})} | custom-call | flops 17999998976 | bytes 54000000 | tf_op jit(solution)/shard_map/lookup/pallas_call | solution.py:66
  174.2 1.1 collective-permute-start.39
  175.3 1.5 collective-permute-start.38
  176.8 3.0 %collective-permute-start.41 = (bf16[64,512]{1,0:T(8,128)(2,1)S(1)}, bf16[64,512]{1,0:T(8,128)(2,1)S(1)}, u32[]{:S(2)}, u32[]{:S(2)}) collective-permute-start(bf16[64,512]{1,0:T(8,128)(2,1)S(1)} %get-tuple-element.261.refs_0_), channel_id=1, source_target_pairs={{0,16},{2,18},{4,20},{6,22},{8,24},{10,26},{12,28},{14,30},{16,0},... | collective-permute-start | bytes 196616 | tf_op jit(solution)/shard_map/ppermute | solution.py:94
  179.8 2.3 %collective-permute-start.42 = (bf16[64,512]{1,0:T(8,128)(2,1)S(1)}, bf16[64,512]{1,0:T(8,128)(2,1)S(1)}, u32[]{:S(2)}, u32[]{:S(2)}) collective-permute-start(bf16[64,512]{1,0:T(8,128)(2,1)S(1)} %get-tuple-element.261.refs_0_), channel_id=1, source_target_pairs={{0,24},{2,26},{4,28},{6,30},{8,16},{10,18},{12,20},{14,22},{16,8},... | collective-permute-start | bytes 196616 | tf_op jit(solution)/shard_map/ppermute | solution.py:94
  182.1 2.6 %collective-permute-done.41.refs_2_ = bf16[64,512]{1,0:T(8,128)(2,1)S(1)} collective-permute-done((bf16[64,512]{1,0:T(8,128)(2,1)S(1)}, bf16[64,512]{1,0:T(8,128)(2,1)S(1)}, u32[]{:S(2)}, u32[]{:S(2)}) %collective-permute-start.41) | collective-permute-done | bytes 65568 | tf_op jit(solution)/shard_map/ppermute | solution.py:94
  184.7 1.3 collective-permute-done.42.refs_3_
  186.8 1.2 collective-permute-start.44
  188.8 5.3 %collective-permute-done.43.refs_1_ = bf16[4,64,256]{2,1,0:T(8,128)(2,1)S(1)} collective-permute-done((bf16[4,64,256]{2,1,0:T(8,128)(2,1)S(1)}, bf16[4,64,256]{2,1,0:T(8,128)(2,1)S(1)}, u32[]{:S(2)}, u32[]{:S(2)}) %collective-permute-start.43) | collective-permute-done | bytes 131104 | tf_op jit(solution)/shard_map/ppermute | solution.py:94
  194.5 1.2 collective-permute-start.48
  195.7 1.4 collective-permute-start.49
  197.1 3.2 %unpack.2 = (f32[2048,512]{1,0:T(8,128)}, f32[8,128]{1,0:T(8,128)S(1)}) custom-call(s32[32]{0:T(128)S(1)} %iota_xor_fusion.refs_0_, bf16[16,64,512]{2,1,0:T(8,128)(2,1)S(1)} %bitcast.31, bf16[16,64,512]{2,1,0:T(8,128)(2,1)S(1)} %bitcast.32, f32[8,128]{1,0:T(8,128)S(1)} %get-tuple-element.271.refs_3_), custom_call_target="tpu_custom_call" | custom-call | flops 15000000512 | bytes 45000000 | tf_op jit(solution)/shard_map/unpack/pallas_call | solution.py:66
  200.3 3.2 %unpack.3 = (f32[512,2048]{1,0:T(8,128)}, f32[16,512]{1,0:T(8,128)}, f32[1,512]{1,0:T(1,128)}, f32[1,512]{1,0:T(1,128)}, f32[8,128]{1,0:T(8,128)S(1)}) custom-call(s32[32]{0:T(128)S(1)} %iota_xor_fusion.refs_0_, bf16[16,80,512]{2,1,0:T(8,128)(2,1)S(1)} %bitcast.26, bf16[16,80,512]{2,1,0:T(8,128)(2,1)S(1)} %bitcast.27, f32[8,128]{1,0:T(8,128)S(1)} %get-tuple-element.272.refs_3_), custom_call_target="tpu_custom_call" | custom-call | flops 15000000512 | bytes 45000000 | tf_op jit(solution)/shard_map/unpack/pallas_call | solution.py:66
  204.2 2.6 %collective-permute-done.50 = bf16[2,2,4,64,512]{4,3,2,1,0:T(8,128)(2,1)S(1)} collective-permute-done((bf16[2,2,4,64,512]{4,3,2,1,0:T(8,128)(2,1)S(1)}, bf16[2,2,4,64,512]{4,3,2,1,0:T(8,128)(2,1)S(1)}, u32[]{:S(2)}, u32[]{:S(2)}) %collective-permute-start.50) | collective-permute-done | bytes 1048608 | tf_op jit(solution)/shard_map/ppermute | solution.py:94
  206.8 3.5 %unpack_two.1 = (f32[512,1536]{1,0:T(8,128)}, f32[512,512]{1,0:T(8,128)}, f32[8,128]{1,0:T(8,128)}) custom-call(s32[32]{0:T(128)S(1)} %iota_xor_fusion.refs_0_, bf16[16,64,512]{2,1,0:T(8,128)(2,1)S(1)} %bitcast.33, bf16[16,64,512]{2,1,0:T(8,128)(2,1)S(1)} %bitcast.34, f32[8,128]{1,0:T(8,128)S(1)} %get-tuple-element.280.refs_3_), custom_call_target="tpu_custom_call" | custom-call | flops 15000000512 | bytes 45000000 | tf_op jit(solution)/shard_map/unpack_two/pallas_call | solution.py:66
  (133 shorter events, 14.0 us)
Async XLA Ops:
  4.8 13.2 %copy-start.21 = (s32[128]{0:T(128)S(1)}, s32[128]{0:T(128)}, u32[]{:S(2)}) copy-start(s32[128]{0:T(128)} %param.14) | copy-start | bytes 1540
  4.8 13.5 %copy-start.22 = (s32[128]{0:T(128)S(1)}, s32[128]{0:T(128)}, u32[]{:S(2)}) copy-start(s32[128]{0:T(128)} %param.15) | copy-start | bytes 1540
  4.8 14.0 %copy-start.10 = (bf16[512,256]{1,0:T(8,128)(2,1)S(1)}, bf16[512,256]{1,0:T(8,128)(2,1)}, u32[]{:S(2)}) copy-start(bf16[512,256]{1,0:T(8,128)(2,1)} %refs_2_.7) | copy-start | bytes 786436
  17.6 15.8 %collective-permute-start = (bf16[2,2,4,128,512]{4,3,2,1,0:T(8,128)(2,1)}, bf16[2,2,4,128,512]{4,3,2,1,0:T(8,128)(2,1)S(1)}, u32[]{:S(2)}, u32[]{:S(2)}) collective-permute-start(bf16[2,2,4,128,512]{4,3,2,1,0:T(8,128)(2,1)} %bitcast.4), channel_id=1, source_target_pairs={{0,1},{1,0},{2,3},{3,2},{4,5},{5,4},{6,7},{7,6},{8,9},{9,8},{10,11... | collective-permute-start | bytes 6291464 | tf_op jit(solution)/shard_map/ppermute | solution.py:94
  33.4 4.6 %copy-start.4 = (bf16[512,1536]{1,0:T(8,128)(2,1)S(1)}, bf16[512,1536]{1,0:T(8,128)(2,1)}, u32[]{:S(2)}) copy-start(bf16[512,1536]{1,0:T(8,128)(2,1)} %refs_4_.5) | copy-start | bytes 4718596
  33.4 4.6 %copy-start.6 = (bf16[128,8,512]{2,1,0:T(8,128)(2,1)S(1)}, bf16[128,8,512]{2,1,0:T(8,128)(2,1)}, u32[]{:S(2)}) copy-start(bf16[128,8,512]{2,1,0:T(8,128)(2,1)} %refs_0_.3) | copy-start | bytes 3145732
  33.4 4.6 %copy-start.8 = (bf16[512,512]{1,0:T(8,128)(2,1)S(1)}, bf16[512,512]{1,0:T(8,128)(2,1)}, u32[]{:S(2)}) copy-start(bf16[512,512]{1,0:T(8,128)(2,1)} %refs_1_.5) | copy-start | bytes 1572868
  33.4 4.6 %copy-start.11 = (f32[16,512]{1,0:T(8,128)S(1)}, f32[16,512]{1,0:T(8,128)}, u32[]{:S(2)}) copy-start(f32[16,512]{1,0:T(8,128)} %refs_2_.6) | copy-start | bytes 98308
  33.4 4.6 %copy-start.13 = (f32[512]{0:T(512)S(1)}, f32[512]{0:T(512)}, u32[]{:S(2)}) copy-start(f32[512]{0:T(512)} %param.18) | copy-start | bytes 6148
  33.4 4.6 %copy-start.14 = (f32[512]{0:T(512)S(1)}, f32[512]{0:T(512)}, u32[]{:S(2)}) copy-start(f32[512]{0:T(512)} %param.17) | copy-start | bytes 6148
  33.9 15.3 %collective-permute-start.1 = (bf16[2,4,128,256]{3,2,1,0:T(8,128)(2,1)S(1)}, bf16[2,4,128,256]{3,2,1,0:T(8,128)(2,1)S(1)}, u32[]{:S(2)}, u32[]{:S(2)}) collective-permute-start(bf16[2,4,128,256]{3,2,1,0:T(8,128)(2,1)S(1)} %get-tuple-element.156), channel_id=1, source_target_pairs={{0,2},{2,0},{4,6},{6,4},{8,10},{10,8},{12,14},{14,12},{16,18},{18,... | collective-permute-start | bytes 1572872 | tf_op jit(solution)/shard_map/ppermute | solution.py:94
  36.5 14.1 %collective-permute-start.2 = (bf16[2,4,128,256]{3,2,1,0:T(8,128)(2,1)S(1)}, bf16[2,4,128,256]{3,2,1,0:T(8,128)(2,1)S(1)}, u32[]{:S(2)}, u32[]{:S(2)}) collective-permute-start(bf16[2,4,128,256]{3,2,1,0:T(8,128)(2,1)S(1)} %get-tuple-element.158), channel_id=1, source_target_pairs={{0,4},{2,6},{4,0},{6,2},{8,12},{10,14},{12,8},{14,10},{16,20},{18,... | collective-permute-start | bytes 1572872 | tf_op jit(solution)/shard_map/ppermute | solution.py:94
  50.5 2.3 %copy-start.2 = (bf16[512,2048]{1,0:T(8,128)(2,1)S(1)}, bf16[512,2048]{1,0:T(8,128)(2,1)}, u32[]{:S(2)}) copy-start(bf16[512,2048]{1,0:T(8,128)(2,1)} %refs_6_.3) | copy-start | bytes 6291460
  50.5 2.3 %copy-start.3 = (bf16[2048,512]{1,0:T(8,128)(2,1)S(1)}, bf16[2048,512]{1,0:T(8,128)(2,1)}, u32[]{:S(2)}) copy-start(bf16[2048,512]{1,0:T(8,128)(2,1)} %refs_7_.3) | copy-start | bytes 6291460
  50.8 10.1 %collective-permute-start.3 = (bf16[4,128,256]{2,1,0:T(8,128)(2,1)S(1)}, bf16[4,128,256]{2,1,0:T(8,128)(2,1)S(1)}, u32[]{:S(2)}, u32[]{:S(2)}) collective-permute-start(bf16[4,128,256]{2,1,0:T(8,128)(2,1)S(1)} %get-tuple-element.163), channel_id=1, source_target_pairs={{0,4},{2,6},{4,0},{6,2},{8,12},{10,14},{12,8},{14,10},{16,20},{18,... | collective-permute-start | bytes 786440 | tf_op jit(solution)/shard_map/ppermute | solution.py:94
  52.3 8.5 %collective-permute-start.4 = (bf16[4,128,256]{2,1,0:T(8,128)(2,1)S(1)}, bf16[4,128,256]{2,1,0:T(8,128)(2,1)S(1)}, u32[]{:S(2)}, u32[]{:S(2)}) collective-permute-start(bf16[4,128,256]{2,1,0:T(8,128)(2,1)S(1)} %get-tuple-element.165), channel_id=1, source_target_pairs={{0,2},{2,0},{4,6},{6,4},{8,10},{10,8},{12,14},{14,12},{16,18},{18,... | collective-permute-start | bytes 786440 | tf_op jit(solution)/shard_map/ppermute | solution.py:94
  61.0 12.4 %collective-permute-start.5 = (bf16[128,512]{1,0:T(8,128)(2,1)S(1)}, bf16[128,512]{1,0:T(8,128)(2,1)S(1)}, u32[]{:S(2)}, u32[]{:S(2)}) collective-permute-start(bf16[128,512]{1,0:T(8,128)(2,1)S(1)} %get-tuple-element.170), channel_id=1, source_target_pairs={{0,8},{2,10},{4,12},{6,14},{8,0},{10,2},{12,4},{14,6},{16,24},{18,... | collective-permute-start | bytes 393224 | tf_op jit(solution)/shard_map/ppermute | solution.py:94
  62.6 12.4 %collective-permute-start.6 = (bf16[128,512]{1,0:T(8,128)(2,1)S(1)}, bf16[128,512]{1,0:T(8,128)(2,1)S(1)}, u32[]{:S(2)}, u32[]{:S(2)}) collective-permute-start(bf16[128,512]{1,0:T(8,128)(2,1)S(1)} %get-tuple-element.171), channel_id=1, source_target_pairs={{0,16},{2,18},{4,20},{6,22},{8,24},{10,26},{12,28},{14,30},{16,0},... | collective-permute-start | bytes 393224 | tf_op jit(solution)/shard_map/ppermute | solution.py:94
  65.2 9.8 %collective-permute-start.7 = (bf16[128,512]{1,0:T(8,128)(2,1)S(1)}, bf16[128,512]{1,0:T(8,128)(2,1)S(1)}, u32[]{:S(2)}, u32[]{:S(2)}) collective-permute-start(bf16[128,512]{1,0:T(8,128)(2,1)S(1)} %get-tuple-element.172), channel_id=1, source_target_pairs={{0,24},{2,26},{4,28},{6,30},{8,16},{10,18},{12,20},{14,22},{16,8},... | collective-permute-start | bytes 393224 | tf_op jit(solution)/shard_map/ppermute | solution.py:94
  75.1 14.8 %collective-permute-start.10 = (bf16[128,512]{1,0:T(8,128)(2,1)S(1)}, bf16[128,512]{1,0:T(8,128)(2,1)S(1)}, u32[]{:S(2)}, u32[]{:S(2)}) collective-permute-start(bf16[128,512]{1,0:T(8,128)(2,1)S(1)} %get-tuple-element.175.refs_0_), channel_id=1, source_target_pairs={{0,24},{2,26},{4,28},{6,30},{8,16},{10,18},{12,20},{14,22},{16,8},... | collective-permute-start | bytes 393224 | tf_op jit(solution)/shard_map/ppermute | solution.py:94
  77.6 12.3 %collective-permute-start.8 = (bf16[128,512]{1,0:T(8,128)(2,1)S(1)}, bf16[128,512]{1,0:T(8,128)(2,1)S(1)}, u32[]{:S(2)}, u32[]{:S(2)}) collective-permute-start(bf16[128,512]{1,0:T(8,128)(2,1)S(1)} %get-tuple-element.175.refs_0_), channel_id=1, source_target_pairs={{0,8},{2,10},{4,12},{6,14},{8,0},{10,2},{12,4},{14,6},{16,24},{18,... | collective-permute-start | bytes 393224 | tf_op jit(solution)/shard_map/ppermute | solution.py:94
  78.7 11.2 %collective-permute-start.9 = (bf16[128,512]{1,0:T(8,128)(2,1)S(1)}, bf16[128,512]{1,0:T(8,128)(2,1)S(1)}, u32[]{:S(2)}, u32[]{:S(2)}) collective-permute-start(bf16[128,512]{1,0:T(8,128)(2,1)S(1)} %get-tuple-element.175.refs_0_), channel_id=1, source_target_pairs={{0,16},{2,18},{4,20},{6,22},{8,24},{10,26},{12,28},{14,30},{16,0},... | collective-permute-start | bytes 393224 | tf_op jit(solution)/shard_map/ppermute | solution.py:94
  79.6 2.8 %copy-start.16 = (f32[1024,1024]{1,0:T(8,128)S(1)}, f32[1024,1024]{1,0:T(8,128)}, u32[]{:S(2)}) copy-start(f32[1024,1024]{1,0:T(8,128)} %get-tuple-element.177.refs_2_) | copy-start | bytes 12582916
  79.6 3.5 %copy-start.17 = (f32[1024,1024]{1,0:T(8,128)S(1)}, f32[1024,1024]{1,0:T(8,128)}, u32[]{:S(2)}) copy-start(f32[1024,1024]{1,0:T(8,128)} %get-tuple-element.178.refs_3_) | copy-start | bytes 12582916
  82.3 25.2 %collective-permute-start.15 = (bf16[2,2,4,64,512]{4,3,2,1,0:T(8,128)(2,1)S(1)}, bf16[2,2,4,64,512]{4,3,2,1,0:T(8,128)(2,1)S(1)}, u32[]{:S(2)}, u32[]{:S(2)}) collective-permute-start(bf16[2,2,4,64,512]{4,3,2,1,0:T(8,128)(2,1)S(1)} %bitcast.28), channel_id=1, source_target_pairs={{0,1},{1,0},{2,3},{3,2},{4,5},{5,4},{6,7},{7,6},{8,9},{9,8},{10,11... | collective-permute-start | bytes 3145736 | tf_op jit(solution)/shard_map/ppermute | solution.py:94
  90.0 8.1 %collective-permute-start.11 = (bf16[4,128,256]{2,1,0:T(8,128)(2,1)S(1)}, bf16[4,128,256]{2,1,0:T(8,128)(2,1)S(1)}, u32[]{:S(2)}, u32[]{:S(2)}) collective-permute-start(bf16[4,128,256]{2,1,0:T(8,128)(2,1)S(1)} %get-tuple-element.184.refs_0_), channel_id=1, source_target_pairs={{0,4},{2,6},{4,0},{6,2},{8,12},{10,14},{12,8},{14,10},{16,20},{18,... | collective-permute-start | bytes 786440 | tf_op jit(solution)/shard_map/ppermute | solution.py:94
  91.6 7.8 %collective-permute-start.12 = (bf16[4,128,256]{2,1,0:T(8,128)(2,1)S(1)}, bf16[4,128,256]{2,1,0:T(8,128)(2,1)S(1)}, u32[]{:S(2)}, u32[]{:S(2)}) collective-permute-start(bf16[4,128,256]{2,1,0:T(8,128)(2,1)S(1)} %get-tuple-element.185.refs_2_), channel_id=1, source_target_pairs={{0,2},{2,0},{4,6},{6,4},{8,10},{10,8},{12,14},{14,12},{16,18},{18,... | collective-permute-start | bytes 786440 | tf_op jit(solution)/shard_map/ppermute | solution.py:94
  96.6 10.9 %collective-permute-start.16 = (bf16[2,2,4,64,512]{4,3,2,1,0:T(8,128)(2,1)S(1)}, bf16[2,2,4,64,512]{4,3,2,1,0:T(8,128)(2,1)S(1)}, u32[]{:S(2)}, u32[]{:S(2)}) collective-permute-start(bf16[2,2,4,64,512]{4,3,2,1,0:T(8,128)(2,1)S(1)} %bitcast.30), channel_id=1, source_target_pairs={{0,1},{1,0},{2,3},{3,2},{4,5},{5,4},{6,7},{7,6},{8,9},{9,8},{10,11... | collective-permute-start | bytes 3145736 | tf_op jit(solution)/shard_map/ppermute | solution.py:94
  99.4 15.2 %collective-permute-start.13 = (bf16[2,4,128,256]{3,2,1,0:T(8,128)(2,1)S(1)}, bf16[2,4,128,256]{3,2,1,0:T(8,128)(2,1)S(1)}, u32[]{:S(2)}, u32[]{:S(2)}) collective-permute-start(bf16[2,4,128,256]{3,2,1,0:T(8,128)(2,1)S(1)} %get-tuple-element.189.refs_0_), channel_id=1, source_target_pairs={{0,2},{2,0},{4,6},{6,4},{8,10},{10,8},{12,14},{14,12},{16,18},{18,... | collective-permute-start | bytes 1572872 | tf_op jit(solution)/shard_map/ppermute | solution.py:94
  100.1 14.9 %collective-permute-start.14 = (bf16[2,4,128,256]{3,2,1,0:T(8,128)(2,1)S(1)}, bf16[2,4,128,256]{3,2,1,0:T(8,128)(2,1)S(1)}, u32[]{:S(2)}, u32[]{:S(2)}) collective-permute-start(bf16[2,4,128,256]{3,2,1,0:T(8,128)(2,1)S(1)} %get-tuple-element.190.refs_2_), channel_id=1, source_target_pairs={{0,4},{2,6},{4,0},{6,2},{8,12},{10,14},{12,8},{14,10},{16,20},{18,... | collective-permute-start | bytes 1572872 | tf_op jit(solution)/shard_map/ppermute | solution.py:94
  107.8 15.6 %collective-permute-start.19 = (bf16[2,4,64,512]{3,2,1,0:T(8,128)(2,1)S(1)}, bf16[2,4,64,512]{3,2,1,0:T(8,128)(2,1)S(1)}, u32[]{:S(2)}, u32[]{:S(2)}) collective-permute-start(bf16[2,4,64,512]{3,2,1,0:T(8,128)(2,1)S(1)} %get-tuple-element.210), channel_id=1, source_target_pairs={{0,2},{2,0},{4,6},{6,4},{8,10},{10,8},{12,14},{14,12},{16,18},{18,... | collective-permute-start | bytes 1572872 | tf_op jit(solution)/shard_map/ppermute | solution.py:94
  108.7 14.8 %collective-permute-start.20 = (bf16[2,4,64,512]{3,2,1,0:T(8,128)(2,1)S(1)}, bf16[2,4,64,512]{3,2,1,0:T(8,128)(2,1)S(1)}, u32[]{:S(2)}, u32[]{:S(2)}) collective-permute-start(bf16[2,4,64,512]{3,2,1,0:T(8,128)(2,1)S(1)} %get-tuple-element.212), channel_id=1, source_target_pairs={{0,4},{2,6},{4,0},{6,2},{8,12},{10,14},{12,8},{14,10},{16,20},{18,... | collective-permute-start | bytes 1572872 | tf_op jit(solution)/shard_map/ppermute | solution.py:94
  114.5 11.3 %collective-permute-start.18 = (bf16[2,2,4,64,512]{4,3,2,1,0:T(8,128)(2,1)S(1)}, bf16[2,2,4,64,512]{4,3,2,1,0:T(8,128)(2,1)S(1)}, u32[]{:S(2)}, u32[]{:S(2)}) collective-permute-start(bf16[2,2,4,64,512]{4,3,2,1,0:T(8,128)(2,1)S(1)} %bitcast.29), channel_id=1, source_target_pairs={{0,1},{1,0},{2,3},{3,2},{4,5},{5,4},{6,7},{7,6},{8,9},{9,8},{10,11... | collective-permute-start | bytes 3145736 | tf_op jit(solution)/shard_map/ppermute | solution.py:94
  115.1 13.1 %collective-permute-start.17 = (bf16[2,2,4,128,512]{4,3,2,1,0:T(8,128)(2,1)S(1)}, bf16[2,2,4,128,512]{4,3,2,1,0:T(8,128)(2,1)S(1)}, u32[]{:S(2)}, u32[]{:S(2)}) collective-permute-start(bf16[2,2,4,128,512]{4,3,2,1,0:T(8,128)(2,1)S(1)} %get-tuple-element.204), channel_id=1, source_target_pairs={{0,1},{1,0},{2,3},{3,2},{4,5},{5,4},{6,7},{7,6},{8,9},{9,8},{10,11... | collective-permute-start | bytes 6291464 | tf_op jit(solution)/shard_map/ppermute | solution.py:94
  123.7 9.2 %collective-permute-start.21 = (bf16[4,64,512]{2,1,0:T(8,128)(2,1)S(1)}, bf16[4,64,512]{2,1,0:T(8,128)(2,1)S(1)}, u32[]{:S(2)}, u32[]{:S(2)}) collective-permute-start(bf16[4,64,512]{2,1,0:T(8,128)(2,1)S(1)} %get-tuple-element.221), channel_id=1, source_target_pairs={{0,4},{2,6},{4,0},{6,2},{8,12},{10,14},{12,8},{14,10},{16,20},{18,... | collective-permute-start | bytes 786440 | tf_op jit(solution)/shard_map/ppermute | solution.py:94
  124.7 9.2 %collective-permute-start.22 = (bf16[4,64,512]{2,1,0:T(8,128)(2,1)S(1)}, bf16[4,64,512]{2,1,0:T(8,128)(2,1)S(1)}, u32[]{:S(2)}, u32[]{:S(2)}) collective-permute-start(bf16[4,64,512]{2,1,0:T(8,128)(2,1)S(1)} %get-tuple-element.223), channel_id=1, source_target_pairs={{0,2},{2,0},{4,6},{6,4},{8,10},{10,8},{12,14},{14,12},{16,18},{18,... | collective-permute-start | bytes 786440 | tf_op jit(solution)/shard_map/ppermute | solution.py:94
  126.0 20.7 %collective-permute-start.26 = (bf16[2,4,64,256]{3,2,1,0:T(8,128)(2,1)S(1)}, bf16[2,4,64,256]{3,2,1,0:T(8,128)(2,1)S(1)}, u32[]{:S(2)}, u32[]{:S(2)}) collective-permute-start(bf16[2,4,64,256]{3,2,1,0:T(8,128)(2,1)S(1)} %get-tuple-element.231), channel_id=1, source_target_pairs={{0,2},{2,0},{4,6},{6,4},{8,10},{10,8},{12,14},{14,12},{16,18},{18,... | collective-permute-start | bytes 786440 | tf_op jit(solution)/shard_map/ppermute | solution.py:94
  127.1 19.7 %collective-permute-start.27 = (bf16[2,4,64,256]{3,2,1,0:T(8,128)(2,1)S(1)}, bf16[2,4,64,256]{3,2,1,0:T(8,128)(2,1)S(1)}, u32[]{:S(2)}, u32[]{:S(2)}) collective-permute-start(bf16[2,4,64,256]{3,2,1,0:T(8,128)(2,1)S(1)} %get-tuple-element.233), channel_id=1, source_target_pairs={{0,4},{2,6},{4,0},{6,2},{8,12},{10,14},{12,8},{14,10},{16,20},{18,... | collective-permute-start | bytes 786440 | tf_op jit(solution)/shard_map/ppermute | solution.py:94
  134.1 15.3 %collective-permute-start.23 = (bf16[160,512]{1,0:T(8,128)(2,1)S(1)}, bf16[160,512]{1,0:T(8,128)(2,1)S(1)}, u32[]{:S(2)}, u32[]{:S(2)}) collective-permute-start(bf16[160,512]{1,0:T(8,128)(2,1)S(1)} %get-tuple-element.227), channel_id=1, source_target_pairs={{0,8},{2,10},{4,12},{6,14},{8,0},{10,2},{12,4},{14,6},{16,24},{18,... | collective-permute-start | bytes 491528 | tf_op jit(solution)/shard_map/ppermute | solution.py:94
  135.2 14.2 %collective-permute-start.24 = (bf16[160,512]{1,0:T(8,128)(2,1)S(1)}, bf16[160,512]{1,0:T(8,128)(2,1)S(1)}, u32[]{:S(2)}, u32[]{:S(2)}) collective-permute-start(bf16[160,512]{1,0:T(8,128)(2,1)S(1)} %get-tuple-element.228), channel_id=1, source_target_pairs={{0,16},{2,18},{4,20},{6,22},{8,24},{10,26},{12,28},{14,30},{16,0},... | collective-permute-start | bytes 491528 | tf_op jit(solution)/shard_map/ppermute | solution.py:94
  137.2 12.2 %collective-permute-start.25 = (bf16[160,512]{1,0:T(8,128)(2,1)S(1)}, bf16[160,512]{1,0:T(8,128)(2,1)S(1)}, u32[]{:S(2)}, u32[]{:S(2)}) collective-permute-start(bf16[160,512]{1,0:T(8,128)(2,1)S(1)} %get-tuple-element.229), channel_id=1, source_target_pairs={{0,24},{2,26},{4,28},{6,30},{8,16},{10,18},{12,20},{14,22},{16,8},... | collective-permute-start | bytes 491528 | tf_op jit(solution)/shard_map/ppermute | solution.py:94
  146.8 15.3 %collective-permute-start.31 = (bf16[4,64,256]{2,1,0:T(8,128)(2,1)S(1)}, bf16[4,64,256]{2,1,0:T(8,128)(2,1)S(1)}, u32[]{:S(2)}, u32[]{:S(2)}) collective-permute-start(bf16[4,64,256]{2,1,0:T(8,128)(2,1)S(1)} %get-tuple-element.240), channel_id=1, source_target_pairs={{0,4},{2,6},{4,0},{6,2},{8,12},{10,14},{12,8},{14,10},{16,20},{18,... | collective-permute-start | bytes 393224 | tf_op jit(solution)/shard_map/ppermute | solution.py:94
  148.0 14.2 %collective-permute-start.32 = (bf16[4,64,256]{2,1,0:T(8,128)(2,1)S(1)}, bf16[4,64,256]{2,1,0:T(8,128)(2,1)S(1)}, u32[]{:S(2)}, u32[]{:S(2)}) collective-permute-start(bf16[4,64,256]{2,1,0:T(8,128)(2,1)S(1)} %get-tuple-element.242), channel_id=1, source_target_pairs={{0,2},{2,0},{4,6},{6,4},{8,10},{10,8},{12,14},{14,12},{16,18},{18,... | collective-permute-start | bytes 393224 | tf_op jit(solution)/shard_map/ppermute | solution.py:94
  149.5 15.8 %collective-permute-start.28 = (bf16[128,512]{1,0:T(8,128)(2,1)S(1)}, bf16[128,512]{1,0:T(8,128)(2,1)S(1)}, u32[]{:S(2)}, u32[]{:S(2)}) collective-permute-start(bf16[128,512]{1,0:T(8,128)(2,1)S(1)} %get-tuple-element.237.refs_0_), channel_id=1, source_target_pairs={{0,8},{2,10},{4,12},{6,14},{8,0},{10,2},{12,4},{14,6},{16,24},{18,... | collective-permute-start | bytes 393224 | tf_op jit(solution)/shard_map/ppermute | solution.py:94
  150.7 16.0 %collective-permute-start.29 = (bf16[128,512]{1,0:T(8,128)(2,1)S(1)}, bf16[128,512]{1,0:T(8,128)(2,1)S(1)}, u32[]{:S(2)}, u32[]{:S(2)}) collective-permute-start(bf16[128,512]{1,0:T(8,128)(2,1)S(1)} %get-tuple-element.237.refs_0_), channel_id=1, source_target_pairs={{0,16},{2,18},{4,20},{6,22},{8,24},{10,26},{12,28},{14,30},{16,0},... | collective-permute-start | bytes 393224 | tf_op jit(solution)/shard_map/ppermute | solution.py:94
  152.6 14.1 %collective-permute-start.30 = (bf16[128,512]{1,0:T(8,128)(2,1)S(1)}, bf16[128,512]{1,0:T(8,128)(2,1)S(1)}, u32[]{:S(2)}, u32[]{:S(2)}) collective-permute-start(bf16[128,512]{1,0:T(8,128)(2,1)S(1)} %get-tuple-element.237.refs_0_), channel_id=1, source_target_pairs={{0,24},{2,26},{4,28},{6,30},{8,16},{10,18},{12,20},{14,22},{16,8},... | collective-permute-start | bytes 393224 | tf_op jit(solution)/shard_map/ppermute | solution.py:94
  162.2 11.8 %collective-permute-start.35 = (bf16[64,512]{1,0:T(8,128)(2,1)S(1)}, bf16[64,512]{1,0:T(8,128)(2,1)S(1)}, u32[]{:S(2)}, u32[]{:S(2)}) collective-permute-start(bf16[64,512]{1,0:T(8,128)(2,1)S(1)} %get-tuple-element.254), channel_id=1, source_target_pairs={{0,8},{2,10},{4,12},{6,14},{8,0},{10,2},{12,4},{14,6},{16,24},{18,... | collective-permute-start | bytes 196616 | tf_op jit(solution)/shard_map/ppermute | solution.py:94
  162.5 11.6 %collective-permute-start.36 = (bf16[64,512]{1,0:T(8,128)(2,1)S(1)}, bf16[64,512]{1,0:T(8,128)(2,1)S(1)}, u32[]{:S(2)}, u32[]{:S(2)}) collective-permute-start(bf16[64,512]{1,0:T(8,128)(2,1)S(1)} %get-tuple-element.255), channel_id=1, source_target_pairs={{0,16},{2,18},{4,20},{6,22},{8,24},{10,26},{12,28},{14,30},{16,0},... | collective-permute-start | bytes 196616 | tf_op jit(solution)/shard_map/ppermute | solution.py:94
  165.3 8.7 %collective-permute-start.37 = (bf16[64,512]{1,0:T(8,128)(2,1)S(1)}, bf16[64,512]{1,0:T(8,128)(2,1)S(1)}, u32[]{:S(2)}, u32[]{:S(2)}) collective-permute-start(bf16[64,512]{1,0:T(8,128)(2,1)S(1)} %get-tuple-element.256), channel_id=1, source_target_pairs={{0,24},{2,26},{4,28},{6,30},{8,16},{10,18},{12,20},{14,22},{16,8},... | collective-permute-start | bytes 196616 | tf_op jit(solution)/shard_map/ppermute | solution.py:94
  166.7 7.4 %collective-permute-start.34 = (bf16[4,80,512]{2,1,0:T(8,128)(2,1)S(1)}, bf16[4,80,512]{2,1,0:T(8,128)(2,1)S(1)}, u32[]{:S(2)}, u32[]{:S(2)}) collective-permute-start(bf16[4,80,512]{2,1,0:T(8,128)(2,1)S(1)} %get-tuple-element.252.refs_2_), channel_id=1, source_target_pairs={{0,2},{2,0},{4,6},{6,4},{8,10},{10,8},{12,14},{14,12},{16,18},{18,... | collective-permute-start | bytes 983048 | tf_op jit(solution)/shard_map/ppermute | solution.py:94
  167.4 6.7 %collective-permute-start.33 = (bf16[4,64,512]{2,1,0:T(8,128)(2,1)S(1)}, bf16[4,64,512]{2,1,0:T(8,128)(2,1)S(1)}, u32[]{:S(2)}, u32[]{:S(2)}) collective-permute-start(bf16[4,64,512]{2,1,0:T(8,128)(2,1)S(1)} %get-tuple-element.251.refs_0_), channel_id=1, source_target_pairs={{0,4},{2,6},{4,0},{6,2},{8,12},{10,14},{12,8},{14,10},{16,20},{18,... | collective-permute-start | bytes 786440 | tf_op jit(solution)/shard_map/ppermute | solution.py:94
  174.0 14.0 %collective-permute-start.45 = (f32[512,256]{1,0:T(8,128)S(1)}, f32[512,256]{1,0:T(8,128)S(1)}, u32[]{:S(2)}, u32[]{:S(2)}) collective-permute-start(f32[512,256]{1,0:T(8,128)S(1)} %get-tuple-element.265.refs_0_), channel_id=1, source_target_pairs={{0,1},{1,0},{2,3},{3,2},{4,5},{5,4},{6,7},{7,6},{8,9},{9,8},{10,11... | collective-permute-start | bytes 1572872 | tf_op jit(solution)/shard_map/ppermute | solution.py:94
  174.2 20.1 %collective-permute-start.39 = (bf16[2,4,80,512]{3,2,1,0:T(8,128)(2,1)S(1)}, bf16[2,4,80,512]{3,2,1,0:T(8,128)(2,1)S(1)}, u32[]{:S(2)}, u32[]{:S(2)}) collective-permute-start(bf16[2,4,80,512]{3,2,1,0:T(8,128)(2,1)S(1)} %get-tuple-element.260.refs_2_), channel_id=1, source_target_pairs={{0,4},{2,6},{4,0},{6,2},{8,12},{10,14},{12,8},{14,10},{16,20},{18,... | collective-permute-start | bytes 1966088 | tf_op jit(solution)/shard_map/ppermute | solution.py:94
  175.3 4.5 %collective-permute-start.40 = (bf16[64,512]{1,0:T(8,128)(2,1)S(1)}, bf16[64,512]{1,0:T(8,128)(2,1)S(1)}, u32[]{:S(2)}, u32[]{:S(2)}) collective-permute-start(bf16[64,512]{1,0:T(8,128)(2,1)S(1)} %get-tuple-element.261.refs_0_), channel_id=1, source_target_pairs={{0,8},{2,10},{4,12},{6,14},{8,0},{10,2},{12,4},{14,6},{16,24},{18,... | collective-permute-start | bytes 196616 | tf_op jit(solution)/shard_map/ppermute | solution.py:94
  175.3 18.9 %collective-permute-start.38 = (bf16[2,4,64,512]{3,2,1,0:T(8,128)(2,1)S(1)}, bf16[2,4,64,512]{3,2,1,0:T(8,128)(2,1)S(1)}, u32[]{:S(2)}, u32[]{:S(2)}) collective-permute-start(bf16[2,4,64,512]{3,2,1,0:T(8,128)(2,1)S(1)} %get-tuple-element.259.refs_0_), channel_id=1, source_target_pairs={{0,2},{2,0},{4,6},{6,4},{8,10},{10,8},{12,14},{14,12},{16,18},{18,... | collective-permute-start | bytes 1572872 | tf_op jit(solution)/shard_map/ppermute | solution.py:94
  176.8 7.9 %collective-permute-start.41 = (bf16[64,512]{1,0:T(8,128)(2,1)S(1)}, bf16[64,512]{1,0:T(8,128)(2,1)S(1)}, u32[]{:S(2)}, u32[]{:S(2)}) collective-permute-start(bf16[64,512]{1,0:T(8,128)(2,1)S(1)} %get-tuple-element.261.refs_0_), channel_id=1, source_target_pairs={{0,16},{2,18},{4,20},{6,22},{8,24},{10,26},{12,28},{14,30},{16,0},... | collective-permute-start | bytes 196616 | tf_op jit(solution)/shard_map/ppermute | solution.py:94
  179.8 6.2 %collective-permute-start.42 = (bf16[64,512]{1,0:T(8,128)(2,1)S(1)}, bf16[64,512]{1,0:T(8,128)(2,1)S(1)}, u32[]{:S(2)}, u32[]{:S(2)}) collective-permute-start(bf16[64,512]{1,0:T(8,128)(2,1)S(1)} %get-tuple-element.261.refs_0_), channel_id=1, source_target_pairs={{0,24},{2,26},{4,28},{6,30},{8,16},{10,18},{12,20},{14,22},{16,8},... | collective-permute-start | bytes 196616 | tf_op jit(solution)/shard_map/ppermute | solution.py:94
  186.0 8.2 %collective-permute-start.43 = (bf16[4,64,256]{2,1,0:T(8,128)(2,1)S(1)}, bf16[4,64,256]{2,1,0:T(8,128)(2,1)S(1)}, u32[]{:S(2)}, u32[]{:S(2)}) collective-permute-start(bf16[4,64,256]{2,1,0:T(8,128)(2,1)S(1)} %get-tuple-element.263.refs_0_), channel_id=1, source_target_pairs={{0,4},{2,6},{4,0},{6,2},{8,12},{10,14},{12,8},{14,10},{16,20},{18,... | collective-permute-start | bytes 393224 | tf_op jit(solution)/shard_map/ppermute | solution.py:94
  186.8 7.4 %collective-permute-start.44 = (bf16[4,64,256]{2,1,0:T(8,128)(2,1)S(1)}, bf16[4,64,256]{2,1,0:T(8,128)(2,1)S(1)}, u32[]{:S(2)}, u32[]{:S(2)}) collective-permute-start(bf16[4,64,256]{2,1,0:T(8,128)(2,1)S(1)} %get-tuple-element.264.refs_2_), channel_id=1, source_target_pairs={{0,2},{2,0},{4,6},{6,4},{8,10},{10,8},{12,14},{14,12},{16,18},{18,... | collective-permute-start | bytes 393224 | tf_op jit(solution)/shard_map/ppermute | solution.py:94
  194.4 2.7 %collective-permute-start.47 = (bf16[2,2,4,64,512]{4,3,2,1,0:T(8,128)(2,1)S(1)}, bf16[2,2,4,64,512]{4,3,2,1,0:T(8,128)(2,1)S(1)}, u32[]{:S(2)}, u32[]{:S(2)}) collective-permute-start(bf16[2,2,4,64,512]{4,3,2,1,0:T(8,128)(2,1)S(1)} %get-tuple-element.270), channel_id=1, source_target_pairs={{0,1},{1,0},{2,3},{3,2},{4,5},{5,4},{6,7},{7,6},{8,9},{9,8},{10,11... | collective-permute-start | bytes 3145736 | tf_op jit(solution)/shard_map/ppermute | solution.py:94
  194.5 9.1 %collective-permute-start.48 = (bf16[2,4,64,256]{3,2,1,0:T(8,128)(2,1)S(1)}, bf16[2,4,64,256]{3,2,1,0:T(8,128)(2,1)S(1)}, u32[]{:S(2)}, u32[]{:S(2)}) collective-permute-start(bf16[2,4,64,256]{3,2,1,0:T(8,128)(2,1)S(1)} %get-tuple-element.276.refs_0_), channel_id=1, source_target_pairs={{0,2},{2,0},{4,6},{6,4},{8,10},{10,8},{12,14},{14,12},{16,18},{18,... | collective-permute-start | bytes 786440 | tf_op jit(solution)/shard_map/ppermute | solution.py:94
  195.7 8.4 %collective-permute-start.49 = (bf16[2,4,64,256]{3,2,1,0:T(8,128)(2,1)S(1)}, bf16[2,4,64,256]{3,2,1,0:T(8,128)(2,1)S(1)}, u32[]{:S(2)}, u32[]{:S(2)}) collective-permute-start(bf16[2,4,64,256]{3,2,1,0:T(8,128)(2,1)S(1)} %get-tuple-element.277.refs_2_), channel_id=1, source_target_pairs={{0,4},{2,6},{4,0},{6,2},{8,12},{10,14},{12,8},{14,10},{16,20},{18,... | collective-permute-start | bytes 786440 | tf_op jit(solution)/shard_map/ppermute | solution.py:94
  197.1 3.2 %collective-permute-start.46 = (bf16[2,2,4,80,512]{4,3,2,1,0:T(8,128)(2,1)S(1)}, bf16[2,2,4,80,512]{4,3,2,1,0:T(8,128)(2,1)S(1)}, u32[]{:S(2)}, u32[]{:S(2)}) collective-permute-start(bf16[2,2,4,80,512]{4,3,2,1,0:T(8,128)(2,1)S(1)} %get-tuple-element.269), channel_id=1, source_target_pairs={{0,1},{1,0},{2,3},{3,2},{4,5},{5,4},{6,7},{7,6},{8,9},{9,8},{10,11... | collective-permute-start | bytes 3932168 | tf_op jit(solution)/shard_map/ppermute | solution.py:94
  204.1 2.7 %collective-permute-start.50 = (bf16[2,2,4,64,512]{4,3,2,1,0:T(8,128)(2,1)S(1)}, bf16[2,2,4,64,512]{4,3,2,1,0:T(8,128)(2,1)S(1)}, u32[]{:S(2)}, u32[]{:S(2)}) collective-permute-start(bf16[2,2,4,64,512]{4,3,2,1,0:T(8,128)(2,1)S(1)} %get-tuple-element.279), channel_id=1, source_target_pairs={{0,1},{1,0},{2,3},{3,2},{4,5},{5,4},{6,7},{7,6},{8,9},{9,8},{10,11... | collective-permute-start | bytes 3145736 | tf_op jit(solution)/shard_map/ppermute | solution.py:94
  (10 other events, 18.3 us)
